TPU v7x, 128 devices: a whole 4x4x4 slice. The times are simulated.
128 devices in a mesh: gx: 8 (over x, core), gy: 16 (over z, y).
Axes of the slice: x: 4, y: 4, z: 4, core: 2. Of those that a mesh axis runs over, the one named last changes fastest.
Arguments:
- positions: float32 [3, 2097152], P(None, ('gx', 'gy')), may hold values from 0.1 to 0.9
- velocity: float32 [3, 2097152], P(None, ('gx', 'gy')), may hold values from -2.5 to 2.5
- radius: float32 [2097152], P(('gx', 'gy')), may hold values from 0.3 to 0.5
- grain_mask: int32 [2097152], P(('gx', 'gy')), may hold values 0 or 1
- grain_cell: int32 [2097152], P(('gx', 'gy')), may hold values from 0 to 2047, as said below
- inner_pairs: int32 [5, 131072], P(None, ('gx', 'gy')), may hold values from -1 to 511, as said below
- cross_pairs: int32 [5, 131072], P(None, ('gx', 'gy')), may hold values from -1 to 511, as said below
- send_lists: int32 [65536], P(('gx', 'gy')), may hold values from 0 to 511
- fluid_velocity: float32 [3, 262144], P(None, ('gx', 'gy')), may hold values from -3 to 3
- pressure_grad: float32 [3, 262144], P(None, ('gx', 'gy')), may hold values from -4 to 4
Outputs:
- positions_out: float32 [3, 2097152], P(None, ('gx', 'gy'))
- velocity_out: float32 [3, 2097152], P(None, ('gx', 'gy'))
- fluid_out: float32 [3, 262144], P(None, ('gx', 'gy'))
- void_out: float32 [262144], P(('gx', 'gy'))
Inputs may be any that keep to these rules, and one draw needn't show every extreme that they name: `grain_cell`: any local cell number below 2048; it names a cell of the fluid blocks of the grain's own slab, within the range of its own column. `inner_pairs`: column p belongs to DEM block p // 1024; rows 0 and 1 are two different local cluster numbers of that block; rows 2 to 4 are an offset of -1, 0 or 1 each, never all zero. `cross_pairs`: column p belongs to DEM block p // 1024; row 0 is a local cluster number, row 1 a copy slot below 512; rows 2 to 4 are an offset of -1, 0 or 1 each, never all zero.
All inputs are finite; a program needn't handle non-finite values. No bound on the sum of `grain_mask` on one device may be relied on, other than what follows from the above.
Results may differ from a plain program's by a relative error of at most 0.00014.
Values sent between devices are 32-bit elements; how exact they have to be, the bound alone decides.
No kernel may reach another device: no remote copies, remote signals or barrier semaphores. Data moves between devices by JAX's collectives and lax.ppermute only.
A program may use at most 128 MiB of HBM per device.

v0:
```python
import math

import jax
import jax.numpy as jnp
from jax import lax
from jax.sharding import PartitionSpec as P

SLOTS = 32
SUBSTEPS = 2


spring = 4.0
time_step = 0.1
grain_density = 2.65
gravity = 1.0
cell_volume = 4.0
void_floor = 0.35
drag_factor = 0.5
table_entries = 2**21


def with_halo(array, sides, width):
    for axis, dim in sides:
        size, length = (lax.axis_size(axis), array.shape[dim])
        up = [(i, (i + 1) % size) for i in range(size - 1)]
        down = [(j, i) for i, j in up]
        last = lax.slice_in_dim(array, length - width, length, axis=dim)
        leading = lax.slice_in_dim(array, 0, width, axis=dim)
        before = lax.ppermute(last, axis, up)
        after = lax.ppermute(leading, axis, down)
        array = jnp.concatenate([before, array, after], axis=dim)
    return array


def grain_terms(radius, grain_mask):
    weights_mask = grain_mask.astype(jnp.float32)
    sphere = 4.0 * math.pi / 3.0 * radius * radius * radius
    return (weights_mask, grain_density * sphere, weights_mask * sphere)


def fluid_update(totals, fluid_velocity, pressure_grad):
    void_out = jnp.maximum(1.0 - totals[0] / cell_volume, void_floor)
    drag_rate = drag_factor * (1.1 - void_out) / (void_out * void_out)
    numerator = void_out * fluid_velocity + time_step * (
        void_out * pressure_grad + drag_rate * totals[1:] / cell_volume
    )
    fluid_out = numerator / (void_out + time_step * drag_rate * totals[0] / cell_volume)
    return (fluid_out, void_out, drag_rate)


def indicator(index, count):
    return (index[:, None] == jnp.arange(count, dtype=jnp.int32)[None, :]).astype(jnp.float32)


def block_length(length, count):
    return math.gcd(length, max(1, table_entries // count))


def select_columns(table, index):
    count = table.shape[-1]
    leading_shape = table.shape[:-1]
    flat = table.reshape(-1, count)
    length = index.shape[0]
    stride = block_length(length, count)

    def select_one_block(block_index):
        return jnp.einsum(
            "rn,bn->rb",
            flat,
            indicator(block_index, count),
            precision=lax.Precision.HIGHEST,
            preferred_element_type=jnp.float32,
        )

    picked = lax.map(select_one_block, index.reshape(length // stride, stride))
    return jnp.moveaxis(picked, 0, 1).reshape(leading_shape + (length,))


def add_columns(values, index, count):
    leading_shape = values.shape[:-1]
    length = index.shape[0]
    flat = values.reshape(-1, length)
    stride = block_length(length, count)
    pieces = jnp.moveaxis(flat.reshape(flat.shape[0], length // stride, stride), 1, 0)

    def add_one_block(total, items):
        piece, block_index = items
        return (
            total
            + jnp.einsum(
                "rb,bn->rn",
                piece,
                indicator(block_index, count),
                precision=lax.Precision.HIGHEST,
                preferred_element_type=jnp.float32,
            ),
            None,
        )

    start = jnp.zeros((flat.shape[0], count), jnp.float32)
    total, unused = lax.scan(
        add_one_block, start, (pieces, index.reshape(length // stride, stride))
    )
    return total.reshape(leading_shape + (count,))


def contact_pairs(leading, partner, offsets):
    separation = leading[:3, :, None, :] - partner[:3, None, :, :] - offsets[:, None, None, :]
    squared = jnp.sum(separation * separation, axis=0)
    reach_sum = leading[3][:, None, :] + partner[3][None, :, :]
    weight = (
        spring
        * jnp.maximum(reach_sum * reach_sum - squared, 0.0)
        * leading[4][:, None, :]
        * partner[4][None, :, :]
    )
    pushes = weight[None] * separation
    return (jnp.sum(pushes, axis=2), -jnp.sum(pushes, axis=1))


def cluster_forces(own_clusters, ghosts, inner_list, cross_list):
    cluster_count = own_clusters.shape[2]
    ghost_slots = ghosts.shape[2]
    leading = select_columns(own_clusters, inner_list[0])
    partner = select_columns(own_clusters, inner_list[1])
    on_leading, on_partner = contact_pairs(leading, partner, inner_list[2:5].astype(jnp.float32))
    forces = add_columns(on_leading, inner_list[0], cluster_count) + add_columns(
        on_partner, inner_list[1], cluster_count
    )
    leading = select_columns(own_clusters, cross_list[0])
    partner = select_columns(ghosts, cross_list[1])
    on_leading, on_partner = contact_pairs(leading, partner, cross_list[2:5].astype(jnp.float32))
    forces = forces + add_columns(on_leading, cross_list[0], cluster_count)
    reactions = add_columns(on_partner, cross_list[1], ghost_slots)
    return (forces, reactions)


def advance(positions, velocity, contact, grain_fluid, grain_drag, weights_mask, masses, volumes):
    upward = jnp.array([0.0, 0.0, 1.0], jnp.float32)[:, None]
    drag_pull = grain_drag * volumes * (grain_fluid - velocity)
    velocity = velocity + time_step * weights_mask * (
        (contact + drag_pull) / masses - gravity * upward
    )
    positions = positions + time_step * weights_mask * velocity
    return (positions, velocity)


def trade(pieces):
    vacant = jnp.zeros_like(pieces[:1])
    arranged = jnp.concatenate([pieces[:4], vacant, pieces[4:]], axis=0)
    arranged = arranged.reshape((3, 3, pieces.shape[1], -1))
    padded = with_halo(arranged, (("gx", 0), ("gy", 1)), 1)
    landed = padded[0::2, 0::2]
    landed = landed.reshape((9,) + pieces.shape[1:])
    return jnp.concatenate([landed[:4], landed[5:]], axis=0)


def shards(
    positions,
    velocity,
    radius,
    grain_mask,
    grain_cell,
    inner_pairs,
    cross_pairs,
    send_lists,
    fluid_velocity,
    pressure_grad,
):
    grains = positions.shape[1]
    clusters_here = grains // SLOTS
    cells_here = fluid_velocity.shape[1]
    parts_y = lax.axis_size("gy")
    per_range = cells_here // parts_y
    reach_cells = parts_y * per_range
    weights_mask, masses, volumes = grain_terms(radius, grain_mask)
    deposits = jnp.concatenate([volumes[None], volumes[None] * velocity], axis=0)
    compact = add_columns(deposits, grain_cell, reach_cells)
    column_here = lax.axis_index("gy")
    layout = jnp.zeros((4, parts_y, parts_y, per_range), jnp.float32)
    layout = lax.dynamic_update_slice_in_dim(
        layout, compact.reshape(4, parts_y, 1, per_range), column_here, 2
    )
    totals = lax.psum_scatter(
        layout.reshape(4, parts_y * cells_here), "gy", scatter_dimension=1, tiled=True
    )
    fluid_out, void_out, drag_rate = fluid_update(totals, fluid_velocity, pressure_grad)
    fields = jnp.concatenate([fluid_out, drag_rate[None]], axis=0)
    spread = lax.all_gather(fields, "gy", axis=1, tiled=True)
    reached = lax.dynamic_slice_in_dim(
        spread.reshape(4, parts_y, parts_y, per_range), column_here, 1, 2
    )
    reached = reached.reshape(4, reach_cells)
    at_grain = select_columns(reached, grain_cell)
    grain_fluid = at_grain[:3]
    grain_drag = at_grain[3]
    ghost_count = send_lists.shape[0] // 8
    for substep in range(SUBSTEPS):
        packed = jnp.concatenate([positions, radius[None], weights_mask[None]], axis=0)
        own_clusters = packed.reshape(5, clusters_here, SLOTS).transpose(0, 2, 1)
        outgoing = (
            select_columns(own_clusters, send_lists)
            .reshape(5, SLOTS, 8, ghost_count)
            .transpose(2, 0, 1, 3)
        )
        received = trade(outgoing)
        ghosts = received.transpose(1, 2, 0, 3).reshape(5, SLOTS, 8 * ghost_count)
        forces, reactions = cluster_forces(own_clusters, ghosts, inner_pairs, cross_pairs)
        returned = trade(reactions.reshape(3, SLOTS, 8, ghost_count).transpose(2, 0, 1, 3))
        returned = returned.transpose(1, 2, 0, 3).reshape(3, SLOTS, 8 * ghost_count)
        forces = forces + add_columns(returned, send_lists, clusters_here)
        contact = forces.transpose(0, 2, 1).reshape(3, grains)
        positions, velocity = advance(
            positions, velocity, contact, grain_fluid, grain_drag, weights_mask, masses, volumes
        )
    return (positions, velocity, fluid_out, void_out)


def solution(mesh):
    placed = (
        P(None, ("gx", "gy")),
        P(None, ("gx", "gy")),
        P(("gx", "gy")),
        P(("gx", "gy")),
        P(("gx", "gy")),
        P(None, ("gx", "gy")),
        P(None, ("gx", "gy")),
        P(("gx", "gy")),
        P(None, ("gx", "gy")),
        P(None, ("gx", "gy")),
    )
    return jax.shard_map(
        shards,
        mesh=mesh,
        in_specs=placed,
        out_specs=(
            P(None, ("gx", "gy")),
            P(None, ("gx", "gy")),
            P(None, ("gx", "gy")),
            P(("gx", "gy")),
        ),
        check_vma=False,
    )
```

profile of v0, /device:TPU:27, one launch (start us, length us, event | category | flops | bytes accessed | tf_op | source)
XLA Modules:
  0.0 381.5 jit_solution(8971013026744328559)
XLA Ops:
  21.0 44.8 %while.6 = (s32[]{:T(128)}, f32[4,2048]{1,0:T(4,128)S(1)}, f32[16,4,1024]{2,1,0:T(4,128)S(1)}, s32[16,1024]{1,0:T(8,128)S(1)}, s32[]{:T(128)}, /*index=5*/s32[]{:T(128)}) while((s32[]{:T(128)}, f32[4,2048]{1,0:T(4,128)S(1)}, f32[16,4,1024]{2,1,0:T(4,128)S(1)}, s32[16,1024]{1,0:T(8,128)S(1)}, s32[]{:T(128)}, ...), condition=%wide.region_7.8_spmd.clone, body=%wide.region_6.7_spmd.clone.sunk | while | flops 102776832 | bytes 94295 | solution.py:101
  66.1 8.7 %copy.146 = f32[4,16,16,128]{0,3,2,1:T(8,128)} copy(f32[4,16,16,128]{3,2,1,0:T(8,128)S(1)} %dynamic_update_slice.29) | data formatting | bytes 1048576
  83.6 4.1 %fusion.21 = (f32[3,32,1024]{2,1,0:T(8,128)}, f32[3,32,1024]{2,1,0:T(8,128)S(1)}) fusion(f32[32,32,1024]{2,1,0:T(8,128)S(1)} %multiply_multiply_fusion.3, f32[3,1024]{1,0:T(4,128)S(1)} %slice_convert_fusion.1, f32[3,32,1024]{2,1,0:T(8,128)S(1)} %bitcast.261, f32[3,32,1024]{2,1,0:T(8,128)S(1)} %bitcast.259), kind=kLoop, calls=%fused_computation.33 | loop fusion | flops 15532032 | bytes 5779456 | tf_op jit(solution)/shard_map/reduce_sum | solution.py:118
  96.4 7.3 %collective-permute-done.2 = f32[5,1,5,2048]{3,1,0,2:T(1,128)S(1)} collective-permute-done((f32[5,1,5,2048]{3,1,0,2:T(1,128)S(1)}, f32[5,1,5,2048]{3,1,0,2:T(1,128)S(1)}, u32[]{:S(2)}, u32[]{:S(2)}) %collective-permute-start.2) | collective-permute-done | bytes 204832 | tf_op jit(solution)/shard_map/ppermute | solution.py:29
  103.8 5.1 %collective-permute-done.3 = f32[5,1,5,2048]{3,1,0,2:T(1,128)S(1)} collective-permute-done((f32[5,1,5,2048]{3,1,0,2:T(1,128)S(1)}, f32[5,1,5,2048]{3,1,0,2:T(1,128)S(1)}, u32[]{:S(2)}, u32[]{:S(2)}) %collective-permute-start.3) | collective-permute-done | bytes 204832 | tf_op jit(solution)/shard_map/ppermute | solution.py:30
  122.0 4.8 %collective-permute-start.4 = (f32[1,3,3,2048]{3,2,1,0:T(4,128)S(1)}, f32[1,3,3,2048]{3,2,1,0:T(4,128)S(1)}, u32[]{:S(2)}, u32[]{:S(2)}) collective-permute-start(f32[1,3,3,2048]{3,2,1,0:T(4,128)S(1)} %copy.140), channel_id=1, source_target_pairs={{0,16},{16,32},{32,48},{48,64},{64,80},{80,96},{96,112},{1,17},{17... | collective-permute-start | bytes 221192 | tf_op jit(solution)/shard_map/ppermute | solution.py:29
  129.5 4.2 %collective-permute-done.5 = f32[1,3,3,2048]{3,2,1,0:T(4,128)S(1)} collective-permute-done((f32[1,3,3,2048]{3,2,1,0:T(4,128)S(1)}, f32[1,3,3,2048]{3,2,1,0:T(4,128)S(1)}, u32[]{:S(2)}, u32[]{:S(2)}) %collective-permute-start.5) | collective-permute-done | bytes 73760 | tf_op jit(solution)/shard_map/ppermute | solution.py:30
  151.1 43.5 %reduce-scatter.4.cloned.1.call-done = f32[2048,4]{1,0:T(8,128)} async-done(((f32[32768,4]{1,0:T(8,128)}), f32[2048,4]{1,0:T(8,128)}) %reduce-scatter.4.cloned.1.call-update) | async-done | bytes 32784
  198.2 16.6 %all_gather.3 = f32[4,32768]{1,0:T(4,128)S(1)} all-gather(f32[4,2048]{1,0:T(4,128)S(1)} %pad_maximum_fusion.18), channel_id=1, replica_groups=mesh['gx'=8,'gy'=16] {'gy'}, dimensions={1}, use_global_device_ids=true | all-gather | bytes 557056 | tf_op jit(solution)/shard_map/all_gather | solution.py:189
  215.0 74.3 %while.5 = (s32[]{:T(128)}, f32[16,4,1024]{2,1,0:T(4,128)S(1)}, s32[16,1024]{1,0:T(8,128)}, f32[4,2048]{1,0:T(4,128)S(1)}, s32[]{:T(128)}) while((s32[]{:T(128)}, f32[16,4,1024]{2,1,0:T(4,128)S(1)}, s32[16,1024]{1,0:T(8,128)}, f32[4,2048]{1,0:T(4,128)S(1)}, s32[]{:T(128)}) %tuple.128), condition=%wide.region_10.11_spmd, body=%wide.region_9.10_spmd.sunk | while | flops 102760448 | bytes 61509 | solution.py:75
  215.9 3.9 %fusion.169 = f32[16,4,1024]{2,1,0:T(4,128)S(1)} fusion(f32[16,4,1024]{2,1,0:T(4,128)S(1)} %get-tuple-element.469, s32[]{:T(128)} %get-tuple-element.468, f32[4,2048]{1,0:T(4,128)S(1)} %get-tuple-element.476, s32[1024]{0:T(1024)S(1)} %bitcast.289), kind=kOutput, calls=%fused_computation.4.clone.1 | convolution fusion | flops 102760448 | bytes 53252 | tf_op jit(solution)/shard_map/while/body/eval_jaxpr/rn,bn->rb/dot_general | solution.py:67
  220.5 3.9 %fusion.169 = f32[16,4,1024]{2,1,0:T(4,128)S(1)} fusion(f32[16,4,1024]{2,1,0:T(4,128)S(1)} %get-tuple-element.469, s32[]{:T(128)} %get-tuple-element.468, f32[4,2048]{1,0:T(4,128)S(1)} %get-tuple-element.476, s32[1024]{0:T(1024)S(1)} %bitcast.289), kind=kOutput, calls=%fused_computation.4.clone.1 | convolution fusion | flops 102760448 | bytes 53252 | tf_op jit(solution)/shard_map/while/body/eval_jaxpr/rn,bn->rb/dot_general | solution.py:67
  225.1 3.9 %fusion.169 = f32[16,4,1024]{2,1,0:T(4,128)S(1)} fusion(f32[16,4,1024]{2,1,0:T(4,128)S(1)} %get-tuple-element.469, s32[]{:T(128)} %get-tuple-element.468, f32[4,2048]{1,0:T(4,128)S(1)} %get-tuple-element.476, s32[1024]{0:T(1024)S(1)} %bitcast.289), kind=kOutput, calls=%fused_computation.4.clone.1 | convolution fusion | flops 102760448 | bytes 53252 | tf_op jit(solution)/shard_map/while/body/eval_jaxpr/rn,bn->rb/dot_general | solution.py:67
  229.8 3.9 %fusion.169 = f32[16,4,1024]{2,1,0:T(4,128)S(1)} fusion(f32[16,4,1024]{2,1,0:T(4,128)S(1)} %get-tuple-element.469, s32[]{:T(128)} %get-tuple-element.468, f32[4,2048]{1,0:T(4,128)S(1)} %get-tuple-element.476, s32[1024]{0:T(1024)S(1)} %bitcast.289), kind=kOutput, calls=%fused_computation.4.clone.1 | convolution fusion | flops 102760448 | bytes 53252 | tf_op jit(solution)/shard_map/while/body/eval_jaxpr/rn,bn->rb/dot_general | solution.py:67
  234.4 3.9 %fusion.169 = f32[16,4,1024]{2,1,0:T(4,128)S(1)} fusion(f32[16,4,1024]{2,1,0:T(4,128)S(1)} %get-tuple-element.469, s32[]{:T(128)} %get-tuple-element.468, f32[4,2048]{1,0:T(4,128)S(1)} %get-tuple-element.476, s32[1024]{0:T(1024)S(1)} %bitcast.289), kind=kOutput, calls=%fused_computation.4.clone.1 | convolution fusion | flops 102760448 | bytes 53252 | tf_op jit(solution)/shard_map/while/body/eval_jaxpr/rn,bn->rb/dot_general | solution.py:67
  239.0 3.9 %fusion.169 = f32[16,4,1024]{2,1,0:T(4,128)S(1)} fusion(f32[16,4,1024]{2,1,0:T(4,128)S(1)} %get-tuple-element.469, s32[]{:T(128)} %get-tuple-element.468, f32[4,2048]{1,0:T(4,128)S(1)} %get-tuple-element.476, s32[1024]{0:T(1024)S(1)} %bitcast.289), kind=kOutput, calls=%fused_computation.4.clone.1 | convolution fusion | flops 102760448 | bytes 53252 | tf_op jit(solution)/shard_map/while/body/eval_jaxpr/rn,bn->rb/dot_general | solution.py:67
  243.7 3.9 %fusion.169 = f32[16,4,1024]{2,1,0:T(4,128)S(1)} fusion(f32[16,4,1024]{2,1,0:T(4,128)S(1)} %get-tuple-element.469, s32[]{:T(128)} %get-tuple-element.468, f32[4,2048]{1,0:T(4,128)S(1)} %get-tuple-element.476, s32[1024]{0:T(1024)S(1)} %bitcast.289), kind=kOutput, calls=%fused_computation.4.clone.1 | convolution fusion | flops 102760448 | bytes 53252 | tf_op jit(solution)/shard_map/while/body/eval_jaxpr/rn,bn->rb/dot_general | solution.py:67
  248.3 3.9 %fusion.169 = f32[16,4,1024]{2,1,0:T(4,128)S(1)} fusion(f32[16,4,1024]{2,1,0:T(4,128)S(1)} %get-tuple-element.469, s32[]{:T(128)} %get-tuple-element.468, f32[4,2048]{1,0:T(4,128)S(1)} %get-tuple-element.476, s32[1024]{0:T(1024)S(1)} %bitcast.289), kind=kOutput, calls=%fused_computation.4.clone.1 | convolution fusion | flops 102760448 | bytes 53252 | tf_op jit(solution)/shard_map/while/body/eval_jaxpr/rn,bn->rb/dot_general | solution.py:67
  252.9 3.9 %fusion.169 = f32[16,4,1024]{2,1,0:T(4,128)S(1)} fusion(f32[16,4,1024]{2,1,0:T(4,128)S(1)} %get-tuple-element.469, s32[]{:T(128)} %get-tuple-element.468, f32[4,2048]{1,0:T(4,128)S(1)} %get-tuple-element.476, s32[1024]{0:T(1024)S(1)} %bitcast.289), kind=kOutput, calls=%fused_computation.4.clone.1 | convolution fusion | flops 102760448 | bytes 53252 | tf_op jit(solution)/shard_map/while/body/eval_jaxpr/rn,bn->rb/dot_general | solution.py:67
  257.5 3.9 %fusion.169 = f32[16,4,1024]{2,1,0:T(4,128)S(1)} fusion(f32[16,4,1024]{2,1,0:T(4,128)S(1)} %get-tuple-element.469, s32[]{:T(128)} %get-tuple-element.468, f32[4,2048]{1,0:T(4,128)S(1)} %get-tuple-element.476, s32[1024]{0:T(1024)S(1)} %bitcast.289), kind=kOutput, calls=%fused_computation.4.clone.1 | convolution fusion | flops 102760448 | bytes 53252 | tf_op jit(solution)/shard_map/while/body/eval_jaxpr/rn,bn->rb/dot_general | solution.py:67
  262.2 3.9 %fusion.169 = f32[16,4,1024]{2,1,0:T(4,128)S(1)} fusion(f32[16,4,1024]{2,1,0:T(4,128)S(1)} %get-tuple-element.469, s32[]{:T(128)} %get-tuple-element.468, f32[4,2048]{1,0:T(4,128)S(1)} %get-tuple-element.476, s32[1024]{0:T(1024)S(1)} %bitcast.289), kind=kOutput, calls=%fused_computation.4.clone.1 | convolution fusion | flops 102760448 | bytes 53252 | tf_op jit(solution)/shard_map/while/body/eval_jaxpr/rn,bn->rb/dot_general | solution.py:67
  266.8 3.9 %fusion.169 = f32[16,4,1024]{2,1,0:T(4,128)S(1)} fusion(f32[16,4,1024]{2,1,0:T(4,128)S(1)} %get-tuple-element.469, s32[]{:T(128)} %get-tuple-element.468, f32[4,2048]{1,0:T(4,128)S(1)} %get-tuple-element.476, s32[1024]{0:T(1024)S(1)} %bitcast.289), kind=kOutput, calls=%fused_computation.4.clone.1 | convolution fusion | flops 102760448 | bytes 53252 | tf_op jit(solution)/shard_map/while/body/eval_jaxpr/rn,bn->rb/dot_general | solution.py:67
  271.4 3.9 %fusion.169 = f32[16,4,1024]{2,1,0:T(4,128)S(1)} fusion(f32[16,4,1024]{2,1,0:T(4,128)S(1)} %get-tuple-element.469, s32[]{:T(128)} %get-tuple-element.468, f32[4,2048]{1,0:T(4,128)S(1)} %get-tuple-element.476, s32[1024]{0:T(1024)S(1)} %bitcast.289), kind=kOutput, calls=%fused_computation.4.clone.1 | convolution fusion | flops 102760448 | bytes 53252 | tf_op jit(solution)/shard_map/while/body/eval_jaxpr/rn,bn->rb/dot_general | solution.py:67
  276.1 3.9 %fusion.169 = f32[16,4,1024]{2,1,0:T(4,128)S(1)} fusion(f32[16,4,1024]{2,1,0:T(4,128)S(1)} %get-tuple-element.469, s32[]{:T(128)} %get-tuple-element.468, f32[4,2048]{1,0:T(4,128)S(1)} %get-tuple-element.476, s32[1024]{0:T(1024)S(1)} %bitcast.289), kind=kOutput, calls=%fused_computation.4.clone.1 | convolution fusion | flops 102760448 | bytes 53252 | tf_op jit(solution)/shard_map/while/body/eval_jaxpr/rn,bn->rb/dot_general | solution.py:67
  280.7 3.9 %fusion.169 = f32[16,4,1024]{2,1,0:T(4,128)S(1)} fusion(f32[16,4,1024]{2,1,0:T(4,128)S(1)} %get-tuple-element.469, s32[]{:T(128)} %get-tuple-element.468, f32[4,2048]{1,0:T(4,128)S(1)} %get-tuple-element.476, s32[1024]{0:T(1024)S(1)} %bitcast.289), kind=kOutput, calls=%fused_computation.4.clone.1 | convolution fusion | flops 102760448 | bytes 53252 | tf_op jit(solution)/shard_map/while/body/eval_jaxpr/rn,bn->rb/dot_general | solution.py:67
  285.3 3.9 %fusion.169 = f32[16,4,1024]{2,1,0:T(4,128)S(1)} fusion(f32[16,4,1024]{2,1,0:T(4,128)S(1)} %get-tuple-element.469, s32[]{:T(128)} %get-tuple-element.468, f32[4,2048]{1,0:T(4,128)S(1)} %get-tuple-element.476, s32[1024]{0:T(1024)S(1)} %bitcast.289), kind=kOutput, calls=%fused_computation.4.clone.1 | convolution fusion | flops 102760448 | bytes 53252 | tf_op jit(solution)/shard_map/while/body/eval_jaxpr/rn,bn->rb/dot_general | solution.py:67
  299.9 4.2 %fusion.15 = (f32[3,32,1024]{2,1,0:T(8,128)S(1)}, f32[3,32,1024]{2,1,0:T(8,128)}) fusion(f32[32,32,1024]{2,1,0:T(8,128)S(1)} %multiply_multiply_fusion.1, f32[3,32,1024]{2,1,0:T(8,128)S(1)} %bitcast.257, f32[3,32,1024]{2,1,0:T(8,128)S(1)} %bitcast.255, f32[3,1024]{1,0:T(4,128)S(1)} %slice_convert_fusion.1), kind=kLoop, calls=%fused_computation.23 | loop fusion | flops 15532032 | bytes 5779456 | tf_op jit(solution)/shard_map/reduce_sum | solution.py:118
  305.7 8.9 %collective-permute-start.8 = (f32[1,3,5,2048]{3,1,2,0:T(4,128)S(1)}, f32[1,3,5,2048]{3,1,2,0:T(4,128)S(1)}, u32[]{:S(2)}, u32[]{:S(2)}) collective-permute-start(f32[1,3,5,2048]{3,1,2,0:T(4,128)S(1)} %slice.346), channel_id=1, source_target_pairs={{0,16},{16,32},{32,48},{48,64},{64,80},{80,96},{96,112},{1,17},{17... | collective-permute-start | bytes 368648 | tf_op jit(solution)/shard_map/ppermute | solution.py:29
  329.7 6.0 %collective-permute-done.11 = f32[5,1,5,2048]{3,1,0,2:T(1,128)S(1)} collective-permute-done((f32[5,1,5,2048]{3,1,0,2:T(1,128)S(1)}, f32[5,1,5,2048]{3,1,0,2:T(1,128)S(1)}, u32[]{:S(2)}, u32[]{:S(2)}) %collective-permute-start.11) | collective-permute-done | bytes 204832 | tf_op jit(solution)/shard_map/ppermute | solution.py:30
  348.7 3.8 collective-permute-start.12
  355.1 3.8 %collective-permute-done.13 = f32[1,3,3,2048]{3,2,1,0:T(4,128)S(1)} collective-permute-done((f32[1,3,3,2048]{3,2,1,0:T(4,128)S(1)}, f32[1,3,3,2048]{3,2,1,0:T(4,128)S(1)}, u32[]{:S(2)}, u32[]{:S(2)}) %collective-permute-start.13) | collective-permute-done | bytes 73760 | tf_op jit(solution)/shard_map/ppermute | solution.py:30
  365.5 3.8 collective-permute-done.15
  (317 shorter events, 178.7 us)
Async XLA Ops:
  7.2 187.4 %reduce-scatter.4.cloned.1.call-start = ((), (), s32[]{:S(2)}) async-start(), calls=%async_computation.1 | async-start | bytes 17825792
  8.4 66.6 %copy-start.8 = (f32[1,512,32]{1,2,0:T(8,128)}, f32[1,512,32]{1,2,0:T(8,128)S(1)}, u32[]{:S(2)}) copy-start(f32[1,512,32]{1,2,0:T(8,128)S(1)} %copy.111) | copy-start | bytes 196612
  9.5 65.5 %copy-start.10 = (f32[1,512,32]{1,2,0:T(8,128)}, f32[1,512,32]{1,2,0:T(8,128)S(1)}, u32[]{:S(2)}) copy-start(f32[1,512,32]{1,2,0:T(8,128)S(1)} %copy.110) | copy-start | bytes 196612
  13.6 76.9 %collective-permute-start = (f32[1,3,5,2048]{3,1,2,0:T(4,128)}, f32[1,3,5,2048]{3,1,2,0:T(4,128)S(1)}, u32[]{:S(2)}, u32[]{:S(2)}) collective-permute-start(f32[1,3,5,2048]{3,1,2,0:T(4,128)} %slice.305), channel_id=1, source_target_pairs={{0,16},{16,32},{32,48},{48,64},{64,80},{80,96},{96,112},{1,17},{17... | collective-permute-start | bytes 368648 | tf_op jit(solution)/shard_map/ppermute | solution.py:29
  18.1 72.4 %collective-permute-start.1 = (f32[1,3,5,2048]{3,1,2,0:T(4,128)}, f32[1,3,5,2048]{3,1,2,0:T(4,128)S(1)}, u32[]{:S(2)}, u32[]{:S(2)}) collective-permute-start(f32[1,3,5,2048]{3,1,2,0:T(4,128)} %slice.309), channel_id=1, source_target_pairs={{16,0},{32,16},{48,32},{64,48},{80,64},{96,80},{112,96},{17,1},{33... | collective-permute-start | bytes 368648 | tf_op jit(solution)/shard_map/ppermute | solution.py:30
  90.9 12.9 %collective-permute-start.2 = (f32[5,1,5,2048]{3,1,0,2:T(1,128)S(1)}, f32[5,1,5,2048]{3,1,0,2:T(1,128)S(1)}, u32[]{:S(2)}, u32[]{:S(2)}) collective-permute-start(f32[5,1,5,2048]{3,1,0,2:T(1,128)S(1)} %get-tuple-element.321), channel_id=1, source_target_pairs={{0,1},{1,2},{2,3},{3,4},{4,5},{5,6},{6,7},{7,8},{8,9},{9,10},{10,1... | collective-permute-start | bytes 614408 | tf_op jit(solution)/shard_map/ppermute | solution.py:29
  94.1 14.8 %collective-permute-start.3 = (f32[5,1,5,2048]{3,1,0,2:T(1,128)S(1)}, f32[5,1,5,2048]{3,1,0,2:T(1,128)S(1)}, u32[]{:S(2)}, u32[]{:S(2)}) collective-permute-start(f32[5,1,5,2048]{3,1,0,2:T(1,128)S(1)} %get-tuple-element.322), channel_id=1, source_target_pairs={{1,0},{2,1},{3,2},{4,3},{5,4},{6,5},{7,6},{8,7},{9,8},{10,9},{11,1... | collective-permute-start | bytes 614408 | tf_op jit(solution)/shard_map/ppermute | solution.py:30
  122.0 7.4 %collective-permute-start.4 = (f32[1,3,3,2048]{3,2,1,0:T(4,128)S(1)}, f32[1,3,3,2048]{3,2,1,0:T(4,128)S(1)}, u32[]{:S(2)}, u32[]{:S(2)}) collective-permute-start(f32[1,3,3,2048]{3,2,1,0:T(4,128)S(1)} %copy.140), channel_id=1, source_target_pairs={{0,16},{16,32},{32,48},{48,64},{64,80},{80,96},{96,112},{1,17},{17... | collective-permute-start | bytes 221192 | tf_op jit(solution)/shard_map/ppermute | solution.py:29
  127.3 21.6 %copy-start.40 = (s32[512]{0:T(512)S(1)}, s32[512]{0:T(512)}, u32[]{:S(2)}) copy-start(s32[512]{0:T(512)} %param.23) | copy-start | bytes 6148
  127.3 6.5 %collective-permute-start.5 = (f32[1,3,3,2048]{3,2,1,0:T(4,128)S(1)}, f32[1,3,3,2048]{3,2,1,0:T(4,128)S(1)}, u32[]{:S(2)}, u32[]{:S(2)}) collective-permute-start(f32[1,3,3,2048]{3,2,1,0:T(4,128)S(1)} %copy.141), channel_id=1, source_target_pairs={{16,0},{32,16},{48,32},{64,48},{80,64},{96,80},{112,96},{17,1},{33... | collective-permute-start | bytes 221192 | tf_op jit(solution)/shard_map/ppermute | solution.py:30
  129.4 20.0 %copy-start = (f32[3,32,1024]{2,1,0:T(8,128)S(1)}, f32[3,32,1024]{2,1,0:T(8,128)}, u32[]{:S(2)}) copy-start(f32[3,32,1024]{2,1,0:T(8,128)} %get-tuple-element.265) | copy-start | bytes 1179652
  129.4 20.0 %copy-start.23 = (f32[3,32,512]{2,1,0:T(8,128)S(1)}, f32[3,32,512]{2,1,0:T(8,128)}, u32[]{:S(2)}) copy-start(f32[3,32,512]{2,1,0:T(8,128)} %fusion.36) | copy-start | bytes 589828
  134.0 9.7 %collective-permute-start.6 = (f32[5,1,3,2048]{3,1,0,2:T(1,128)S(1)}, f32[5,1,3,2048]{3,1,0,2:T(1,128)S(1)}, u32[]{:S(2)}, u32[]{:S(2)}) collective-permute-start(f32[5,1,3,2048]{3,1,0,2:T(1,128)S(1)} %get-tuple-element.369), channel_id=1, source_target_pairs={{0,1},{1,2},{2,3},{3,4},{4,5},{5,6},{6,7},{7,8},{8,9},{9,10},{10,1... | collective-permute-start | bytes 368648 | tf_op jit(solution)/shard_map/ppermute | solution.py:29
  135.9 11.2 %collective-permute-start.7 = (f32[5,1,3,2048]{3,1,0,2:T(1,128)S(1)}, f32[5,1,3,2048]{3,1,0,2:T(1,128)S(1)}, u32[]{:S(2)}, u32[]{:S(2)}) collective-permute-start(f32[5,1,3,2048]{3,1,0,2:T(1,128)S(1)} %get-tuple-element.370), channel_id=1, source_target_pairs={{1,0},{2,1},{3,2},{4,3},{5,4},{6,5},{7,6},{8,7},{9,8},{10,9},{11,1... | collective-permute-start | bytes 368648 | tf_op jit(solution)/shard_map/ppermute | solution.py:30
  148.7 49.4 %copy-start.27 = (f32[3,2048]{1,0:T(4,128)S(1)}, f32[3,2048]{1,0:T(4,128)}, u32[]{:S(2)}) copy-start(f32[3,2048]{1,0:T(4,128)} %param.25) | copy-start | bytes 73732
  148.7 49.4 %copy-start.28 = (f32[3,2048]{1,0:T(4,128)S(1)}, f32[3,2048]{1,0:T(4,128)}, u32[]{:S(2)}) copy-start(f32[3,2048]{1,0:T(4,128)} %param.24) | copy-start | bytes 73732
  214.9 74.5 %copy-start.2 = (f32[3,16384]{1,0:T(4,128)S(1)}, f32[3,16384]{1,0:T(4,128)}, u32[]{:S(2)}) copy-start(f32[3,16384]{1,0:T(4,128)} %param.17) | copy-start | bytes 589828
  215.0 74.5 %copy-start.3 = (f32[3,16384]{1,0:T(4,128)S(1)}, f32[3,16384]{1,0:T(4,128)}, u32[]{:S(2)}) copy-start(f32[3,16384]{1,0:T(4,128)} %param.16) | copy-start | bytes 589828
  215.0 74.5 %copy-start.12 = (f32[16384]{0:T(1024)S(1)}, f32[16384]{0:T(1024)}, u32[]{:S(2)}) copy-start(f32[16384]{0:T(1024)} %get-tuple-element.384) | copy-start | bytes 196612
  215.0 74.5 %copy-start.14 = (f32[16384]{0:T(1024)S(1)}, f32[16384]{0:T(1024)}, u32[]{:S(2)}) copy-start(f32[16384]{0:T(1024)} %get-tuple-element.385) | copy-start | bytes 196612
  215.0 74.5 %copy-start.42 = (f32[3]{0:T(128)S(1)}, f32[3]{0:T(128)}, u32[]{:S(2)}) copy-start(f32[3]{0:T(128)} %constant.191) | copy-start | bytes 40
  215.0 76.0 %copy-start.9 = (f32[1,512,32]{1,2,0:T(8,128)S(1)}, f32[1,512,32]{1,2,0:T(8,128)}, u32[]{:S(2)}) copy-start(f32[1,512,32]{1,2,0:T(8,128)} %copy-done.8) | copy-start | bytes 196612
  215.0 76.0 %copy-start.11 = (f32[1,512,32]{1,2,0:T(8,128)S(1)}, f32[1,512,32]{1,2,0:T(8,128)}, u32[]{:S(2)}) copy-start(f32[1,512,32]{1,2,0:T(8,128)} %copy-done.10) | copy-start | bytes 196612
  305.7 13.9 %collective-permute-start.8 = (f32[1,3,5,2048]{3,1,2,0:T(4,128)S(1)}, f32[1,3,5,2048]{3,1,2,0:T(4,128)S(1)}, u32[]{:S(2)}, u32[]{:S(2)}) collective-permute-start(f32[1,3,5,2048]{3,1,2,0:T(4,128)S(1)} %slice.346), channel_id=1, source_target_pairs={{0,16},{16,32},{32,48},{48,64},{64,80},{80,96},{96,112},{1,17},{17... | collective-permute-start | bytes 368648 | tf_op jit(solution)/shard_map/ppermute | solution.py:29
  314.7 6.6 %collective-permute-start.9 = (f32[1,3,5,2048]{3,1,2,0:T(4,128)S(1)}, f32[1,3,5,2048]{3,1,2,0:T(4,128)S(1)}, u32[]{:S(2)}, u32[]{:S(2)}) collective-permute-start(f32[1,3,5,2048]{3,1,2,0:T(4,128)S(1)} %slice.350), channel_id=1, source_target_pairs={{16,0},{32,16},{48,32},{64,48},{80,64},{96,80},{112,96},{17,1},{33... | collective-permute-start | bytes 368648 | tf_op jit(solution)/shard_map/ppermute | solution.py:30
  321.7 8.0 %collective-permute-start.10 = (f32[5,1,5,2048]{3,1,0,2:T(1,128)S(1)}, f32[5,1,5,2048]{3,1,0,2:T(1,128)S(1)}, u32[]{:S(2)}, u32[]{:S(2)}) collective-permute-start(f32[5,1,5,2048]{3,1,0,2:T(1,128)S(1)} %get-tuple-element.315), channel_id=1, source_target_pairs={{0,1},{1,2},{2,3},{3,4},{4,5},{5,6},{6,7},{7,8},{8,9},{9,10},{10,1... | collective-permute-start | bytes 614408 | tf_op jit(solution)/shard_map/ppermute | solution.py:29
  325.3 10.4 %collective-permute-start.11 = (f32[5,1,5,2048]{3,1,0,2:T(1,128)S(1)}, f32[5,1,5,2048]{3,1,0,2:T(1,128)S(1)}, u32[]{:S(2)}, u32[]{:S(2)}) collective-permute-start(f32[5,1,5,2048]{3,1,0,2:T(1,128)S(1)} %get-tuple-element.320), channel_id=1, source_target_pairs={{1,0},{2,1},{3,2},{4,3},{5,4},{6,5},{7,6},{8,7},{9,8},{10,9},{11,1... | collective-permute-start | bytes 614408 | tf_op jit(solution)/shard_map/ppermute | solution.py:30
  348.7 6.3 %collective-permute-start.12 = (f32[1,3,3,2048]{3,2,1,0:T(4,128)S(1)}, f32[1,3,3,2048]{3,2,1,0:T(4,128)S(1)}, u32[]{:S(2)}, u32[]{:S(2)}) collective-permute-start(f32[1,3,3,2048]{3,2,1,0:T(4,128)S(1)} %copy.142), channel_id=1, source_target_pairs={{0,16},{16,32},{32,48},{48,64},{64,80},{80,96},{96,112},{1,17},{17... | collective-permute-start | bytes 221192 | tf_op jit(solution)/shard_map/ppermute | solution.py:29
  353.0 18.0 %copy-start.41 = (s32[512]{0:T(512)S(1)}, s32[512]{0:T(512)}, u32[]{:S(2)}) copy-start(s32[512]{0:T(512)} %param.23) | copy-start | bytes 6148
  353.0 5.9 %collective-permute-start.13 = (f32[1,3,3,2048]{3,2,1,0:T(4,128)S(1)}, f32[1,3,3,2048]{3,2,1,0:T(4,128)S(1)}, u32[]{:S(2)}, u32[]{:S(2)}) collective-permute-start(f32[1,3,3,2048]{3,2,1,0:T(4,128)S(1)} %copy.143), channel_id=1, source_target_pairs={{16,0},{32,16},{48,32},{64,48},{80,64},{96,80},{112,96},{17,1},{33... | collective-permute-start | bytes 221192 | tf_op jit(solution)/shard_map/ppermute | solution.py:30
  359.2 6.2 %collective-permute-start.14 = (f32[5,1,3,2048]{3,1,0,2:T(1,128)S(1)}, f32[5,1,3,2048]{3,1,0,2:T(1,128)S(1)}, u32[]{:S(2)}, u32[]{:S(2)}) collective-permute-start(f32[5,1,3,2048]{3,1,0,2:T(1,128)S(1)} %get-tuple-element.367), channel_id=1, source_target_pairs={{0,1},{1,2},{2,3},{3,4},{4,5},{5,6},{6,7},{7,8},{8,9},{9,10},{10,1... | collective-permute-start | bytes 368648 | tf_op jit(solution)/shard_map/ppermute | solution.py:29
  361.2 8.1 %collective-permute-start.15 = (f32[5,1,3,2048]{3,1,0,2:T(1,128)S(1)}, f32[5,1,3,2048]{3,1,0,2:T(1,128)S(1)}, u32[]{:S(2)}, u32[]{:S(2)}) collective-permute-start(f32[5,1,3,2048]{3,1,0,2:T(1,128)S(1)} %get-tuple-element.368), channel_id=1, source_target_pairs={{1,0},{2,1},{3,2},{4,3},{5,4},{6,5},{7,6},{8,7},{9,8},{10,9},{11,1... | collective-permute-start | bytes 368648 | tf_op jit(solution)/shard_map/ppermute | solution.py:30
  (29 other events, 234.5 us)
Sparse Core Ops, SparseCore 0:
  75.0 119.5 reduce-scatter.3
where the time goes:
time: 388 us; the launch traced here: 381 us
  matrix products  132 us (34%)
  waiting for transfers between devices  83.9 us (22%)
  starting transfers between devices  51.2 us (13%)
  local copies, waits for them, and re-layouts  45.3 us (12%)
  other arithmetic  36.7 us (9%)
  blocking collectives  16.6 us (4%)
  between operations  15.8 us (4%)
    dot_general x26, matrix products, select_one_block(): jnp.einsum('rn,bn->rb', flat, indicator(block_index, count), precision=la...  74.6 us
    dot_general x26, matrix products, add_one_block(): jnp.einsum('rb,bn->rn', piece, indicator(block_index, count), precision=l...  56.9 us
    unnamed x2, waiting for transfers between devices  43.5 us
    ppermute x8, starting transfers between devices, with_halo(): before = lax.ppermute(last, axis, up)  31.8 us
    ppermute x8, waiting for transfers between devices, with_halo(): after = lax.ppermute(leading, axis, down)  28.3 us
    ppermute x8, starting transfers between devices, with_halo(): after = lax.ppermute(leading, axis, down)  19.4 us
    all_gather x1, blocking collectives, shards(): spread = lax.all_gather(fields, 'gy', axis=1, tiled=True)  16.6 us
    reduce_sum x4, other arithmetic, contact_pairs(): return (jnp.sum(pushes, axis=2), -jnp.sum(pushes, axis=1))  15 us
  transfers between devices with their start and end apart: 17, of which 11 were waited for; matrix products, arithmetic and copies ran while one was open for 25% of the time, Pallas kernels for 0%

commit v1 on v0

v1 whole, which is shorter than its diff:
```python
import math

import jax
import jax.numpy as jnp
from jax import lax
from jax.experimental import pallas as pl
from jax.experimental.pallas import tpu as pltpu
from jax.sharding import PartitionSpec as P

SLOTS = 32
LANES = 128
CLUSTERS = 512
GHOSTS = 64
PAIRS = 1024
CHUNKS = 128
GROUP = 4
NEIGHBOURS = ((-1, -1), (-1, 0), (-1, 1), (0, -1), (0, 1), (1, -1), (1, 0), (1, 1))
GHOST_ORDER = (7, 2, 3, 4, 5, 0, 1, 6)
FAR = 2.0**30

spring = 4.0
time_step = 0.1
grain_density = 2.65
gravity = 1.0
cell_volume = 4.0
void_floor = 0.35
drag_factor = 0.5

f32 = jnp.float32
bf16 = jnp.bfloat16
PARAMS = pltpu.CompilerParams(vmem_limit_bytes=24 * 1024 * 1024)


def split(values, parts):
    pieces = []
    for _ in range(parts - 1):
        piece = values.astype(bf16)
        pieces.append(piece)
        values = values - piece.astype(f32)
    pieces.append(values.astype(bf16))
    return pieces


def one_hot(index_row, count):
    rows = lax.broadcasted_iota(jnp.int32, (count, index_row.shape[1]), 0)
    return jnp.where(rows == index_row, 1.0, 0.0).astype(bf16)


def dot(left, right):
    return jnp.dot(left, right, preferred_element_type=f32)


def dot_lanes(left, right):
    return lax.dot_general(left, right, (((1,), (1,)), ((), ())), preferred_element_type=f32)


def cluster_column(index):
    return (index & (GROUP - 1)) * LANES + (index >> 2)


def ghost_column(slot):
    block = slot >> 6
    column = jnp.zeros_like(slot)
    for position, offset in enumerate(GHOST_ORDER):
        column = jnp.where(block == offset, position * GHOSTS, column)
    return column + (slot & (GHOSTS - 1))


def lower_half(shape):
    return lax.broadcasted_iota(jnp.int32, shape, 1) < GHOSTS


def to_table(square):
    turned = square.T
    return jnp.concatenate([turned[k * SLOTS : (k + 1) * SLOTS] for k in range(GROUP)], axis=1)


def from_table(table):
    stacked = jnp.concatenate([table[:, k * LANES : (k + 1) * LANES] for k in range(GROUP)], axis=0)
    return stacked.T


def load_components(ref, stage):
    for i in range(CHUNKS):
        stage[pl.ds(i, 3, stride=CHUNKS), :] = ref[:, i * LANES : (i + 1) * LANES]
    return [to_table(stage[c * CHUNKS : (c + 1) * CHUNKS, :]) for c in range(3)]


def store_components(ref, stage, table):
    for c in range(3):
        stage[c * CHUNKS : (c + 1) * CHUNKS, :] = from_table(table[c * SLOTS : (c + 1) * SLOTS])
    for i in range(CHUNKS):
        ref[:, i * LANES : (i + 1) * LANES] = stage[pl.ds(i, 3, stride=CHUNKS), :]


def gather(table_parts, hot, rows):
    picked = dot(table_parts, hot)
    total = picked[:rows]
    for k in range(1, table_parts.shape[0] // rows):
        total = total + picked[k * rows : (k + 1) * rows]
    return total


def send_pieces(table, rows, send_ref, first_ref, second_ref):
    parts = jnp.concatenate(split(table[:rows], 3), axis=0)
    half = CLUSTERS // 2
    for k, out in enumerate((first_ref, second_ref)):
        hot = one_hot(cluster_column(send_ref[:, k * half : (k + 1) * half]), CLUSTERS)
        out[...] = gather(parts, hot, rows)


def prepare(positions, radius, mask, send, table_out, state_out, first, second, stage):
    parts = load_components(positions, stage)
    reach = to_table(radius[...])
    weights = to_table(mask[...].astype(f32))
    real = weights > 0.5
    table = jnp.concatenate([jnp.where(real, part, FAR) for part in parts] + [reach], axis=0)
    table_out[...] = table
    for c in range(3):
        state_out[c * SLOTS : (c + 1) * SLOTS] = parts[c]
    state_out[3 * SLOTS :] = weights
    send_pieces(table, 4 * SLOTS, send, first, second)


def contacts(leading, partner, on_leading, on_partner):
    on_partner[...] = jnp.zeros_like(on_partner)
    step = 4

    def row(component, slot):
        return pl.ds(pl.multiple_of((component * SLOTS + slot) * 8, 8), 8)

    def some_slots(block, carry):
        base = block * step
        ours = [[leading[row(c, base + i), :] for c in range(4)] for i in range(step)]
        sums = [[jnp.zeros((8, LANES), f32) for _ in range(3)] for _ in range(step)]
        for q in range(SLOTS):
            theirs = [partner[row(c, q), :] for c in range(4)]
            back = [on_partner[row(c, q), :] for c in range(3)]
            for i in range(step):
                apart = [ours[i][c] - theirs[c] for c in range(3)]
                squared = apart[0] * apart[0] + apart[1] * apart[1] + apart[2] * apart[2]
                reach = ours[i][3] + theirs[3]
                weight = jnp.maximum(reach * reach - squared, 0.0)
                for c in range(3):
                    push = weight * apart[c]
                    sums[i][c] = sums[i][c] + push
                    back[c] = back[c] + push
            for c in range(3):
                on_partner[row(c, q), :] = back[c]
        for i in range(step):
            for c in range(3):
                on_leading[row(c, base + i), :] = sums[i][c]
        return carry

    lax.fori_loop(0, SLOTS // step, some_slots, 0)


def pair_sums(pairs, leading_parts, partner_parts, partner_column, scratch):
    hot_a, hot_b, leading, partner, on_leading, on_partner = scratch
    width = 2 * LANES
    for block in range(PAIRS // width):
        span = slice(block * width, (block + 1) * width)
        for row, column, parts, hot, landed in (
            (0, cluster_column, leading_parts, hot_a, leading),
            (1, partner_column, partner_parts, hot_b, partner),
        ):
            chosen = one_hot(column(pairs[row : row + 1, span]), CLUSTERS)
            hot[:, span] = chosen
            picked = gather(parts, chosen, 4 * SLOTS)
            if row == 0:
                offsets = pairs[2:5, span].astype(f32)
                picked = jnp.concatenate(
                    [picked[c * SLOTS : (c + 1) * SLOTS] - offsets[c : c + 1] for c in range(3)]
                    + [picked[3 * SLOTS :]],
                    axis=0,
                )
            for k in range(2):
                landed[pl.ds(2 * block + k, 4 * SLOTS, stride=8), :] = picked[
                    :, k * LANES : (k + 1) * LANES
                ]
    contacts(leading, partner, on_leading, on_partner)
    totals = []
    for sums, hot in ((on_leading, hot_a), (on_partner, hot_b)):
        pieces = jnp.concatenate(
            [sums[pl.ds(k, 3 * SLOTS, stride=8), :] for k in range(PAIRS // LANES)], axis=1
        )
        added = dot_lanes(jnp.concatenate(split(pieces, 2), axis=0), hot[...])
        totals.append(added[: 3 * SLOTS] + added[3 * SLOTS :])
    return totals


def inner_kernel(table, pairs, force, *scratch):
    parts = jnp.concatenate(split(table[...], 3), axis=0)
    on_leading, on_partner = pair_sums(pairs, parts, parts, cluster_column, scratch)
    force[...] = on_leading - on_partner


def present_tile(low, high):
    here_x, here_y = lax.axis_index("gx"), lax.axis_index("gy")
    flags = []
    for slot in (low, high):
        a, b = NEIGHBOURS[slot]
        x, y = here_x + a, here_y + b
        inside = (x >= 0) & (x < lax.axis_size("gx")) & (y >= 0) & (y < lax.axis_size("gy"))
        flags.append(jnp.where(inside, 1, 0))
    return jnp.where(lower_half((1, LANES)), flags[0], flags[1]) > 0


def cross_kernel(
    table, pairs, reach, below, above, from_next, from_last, force, up, down, keep, reach_out, *scratch
):
    rows = below.shape[0]
    low = lower_half((rows, LANES))
    tiles = [
        below[:, :LANES],
        jnp.where(low, above[:, LANES:], below[:, LANES:]),
        above[:, :LANES],
        jnp.where(low, from_last[:, LANES:], from_next[:, :LANES]),
    ]
    for k in range(4):
        there = present_tile(GHOST_ORDER[2 * k], GHOST_ORDER[2 * k + 1])
        placed = jnp.where(there, tiles[k][: 3 * SLOTS], FAR)
        size = reach[:, k * LANES : (k + 1) * LANES] if rows == 3 * SLOTS else tiles[k][3 * SLOTS :]
        reach_out[:, k * LANES : (k + 1) * LANES] = size
        tiles[k] = jnp.concatenate([placed, size], axis=0)
    ghosts = jnp.concatenate(tiles, axis=1)
    own_parts = jnp.concatenate(split(table[...], 3), axis=0)
    ghost_parts = jnp.concatenate(split(ghosts, 3), axis=0)
    on_leading, on_partner = pair_sums(pairs, own_parts, ghost_parts, ghost_column, scratch)
    force[...] = on_leading
    up[...] = on_partner[:, : 2 * LANES]
    down[...] = on_partner[:, LANES : 3 * LANES]
    keep[...] = on_partner[:, 3 * LANES :]


def deposit_kernel(velocity, radius, mask, cell, velocity_out, cell_out, totals, stage):
    parts = load_components(velocity, stage)
    reach = to_table(radius[...])
    weights = to_table(mask[...].astype(f32))
    cells = to_table(cell[...].astype(f32)).astype(jnp.int32)
    volumes = weights * ((4.0 * math.pi / 3.0) * reach * reach * reach)
    for c in range(3):
        velocity_out[c * SLOTS : (c + 1) * SLOTS] = parts[c]
    cell_out[...] = cells
    amounts = [volumes] + [volumes * part for part in parts]
    total = jnp.zeros((2 * 4 * 16, LANES), f32)
    for slot in range(SLOTS):
        cell_row = cells[slot : slot + 1]
        hot = one_hot(cell_row & (LANES - 1), LANES)
        group = lax.broadcasted_iota(jnp.int32, (16, CLUSTERS), 0) == (cell_row >> 7)
        spread = jnp.concatenate(
            [jnp.where(group, amount[slot : slot + 1], 0.0) for amount in amounts], axis=0
        )
        total = total + dot_lanes(jnp.concatenate(split(spread, 2), axis=0), hot)
    totals[...] = total[:64] + total[64:]


def fluid_kernel(totals, fluid, cell, fields_out, at_grain):
    volume = totals[:16]
    void_out = jnp.maximum(1.0 - volume / cell_volume, void_floor)
    drag_rate = drag_factor * (1.1 - void_out) / (void_out * void_out)
    below = void_out + time_step * drag_rate * volume / cell_volume
    fields = []
    for c in range(3):
        push = void_out * fluid[c + 3] + drag_rate * totals[(c + 1) * 16 : (c + 2) * 16] / cell_volume
        fields.append((void_out * fluid[c] + time_step * push) / below)
        fields_out[c] = fields[c]
    fields_out[3] = void_out
    fields.append(drag_rate)
    parts = jnp.concatenate(split(jnp.concatenate(fields, axis=0), 2), axis=1)
    for slot in range(SLOTS):
        cell_row = cell[slot : slot + 1, :]
        hot = one_hot(cell_row & (LANES - 1), LANES)
        seen = dot(parts, jnp.concatenate([hot, hot], axis=0))
        group = lax.broadcasted_iota(jnp.int32, (16, CLUSTERS), 0) == (cell_row >> 7)
        for c in range(4):
            chosen = jnp.where(group, seen[c * 16 : (c + 1) * 16], 0.0)
            row = c * SLOTS + slot
            at_grain[row : row + 1, :] = jnp.sum(chosen, axis=0, keepdims=True)


def advance(state, velocity, reach, at_grain, inner, cross, above, below, from_last, from_next, send):
    low = lower_half((3 * SLOTS, LANES))
    tiles = [
        from_last[:, :LANES],
        jnp.where(low, from_last[:, LANES:], below[:, LANES:]),
        jnp.where(low, above[:, :LANES], from_next[:, :LANES]),
        from_next[:, LANES:],
    ]
    tiles = [jnp.where(present_tile(2 * k, 2 * k + 1), tiles[k], 0.0) for k in range(4)]
    returned = jnp.concatenate(tiles, axis=1)
    hot = one_hot(cluster_column(send[...]), CLUSTERS)
    added = dot_lanes(jnp.concatenate(split(returned, 2), axis=0), hot)
    contact = spring * (inner[...] + cross[...] - (added[: 3 * SLOTS] + added[3 * SLOTS :]))
    weights = state[3 * SLOTS :, :]
    sphere = (4.0 * math.pi / 3.0) * reach * reach * reach
    masses = grain_density * sphere
    volumes = weights * sphere
    drag = at_grain[3 * SLOTS :, :] * volumes
    places, speeds = [], []
    for c in range(3):
        rows = slice(c * SLOTS, (c + 1) * SLOTS)
        speed = velocity[rows, :]
        pull = (contact[rows] + drag * (at_grain[rows, :] - speed)) / masses
        if c == 2:
            pull = pull - gravity
        speed = speed + time_step * weights * pull
        speeds.append(speed)
        places.append(state[rows, :] + time_step * weights * speed)
    return places, speeds, weights


def middle_kernel(
    table, state, velocity, at_grain, inner, cross, above, below, from_last, from_next, send,
    table_out, state_out, velocity_out, first, second,
):
    reach = table[3 * SLOTS :, :]
    places, speeds, weights = advance(
        state, velocity, reach, at_grain, inner, cross, above, below, from_last, from_next, send
    )
    real = weights > 0.5
    moved = jnp.concatenate([jnp.where(real, place, FAR) for place in places] + [reach], axis=0)
    table_out[...] = moved
    for c in range(3):
        state_out[c * SLOTS : (c + 1) * SLOTS] = places[c]
        velocity_out[c * SLOTS : (c + 1) * SLOTS] = speeds[c]
    state_out[3 * SLOTS :] = weights
    send_pieces(moved, 3 * SLOTS, send, first, second)


def last_kernel(
    table, state, velocity, at_grain, inner, cross, above, below, from_last, from_next, send,
    positions_out, velocity_out, stage,
):
    places, speeds, _ = advance(
        state, velocity, table[3 * SLOTS :, :], at_grain, inner, cross, above, below, from_last,
        from_next, send,
    )
    store_components(positions_out, stage, jnp.concatenate(places, axis=0))
    store_components(velocity_out, stage, jnp.concatenate(speeds, axis=0))


def shift(array, step_x, step_y):
    size_x, size_y = lax.axis_size("gx"), lax.axis_size("gy")
    moves = []
    for x in range(size_x):
        for y in range(size_y):
            target = (x + step_x) % size_x * size_y + (y + step_y) % size_y
            moves.append((x * size_y + y, target))
    return lax.ppermute(array, ("gx", "gy"), moves)


def halves(low_from, high_from):
    return jnp.where(lower_half(low_from.shape), low_from, high_from)


def spread_ghosts(first, second):
    from_next = shift(first, -1, 0)
    from_last = shift(second, 1, 0)
    minus = jnp.concatenate(
        [halves(from_next[:, :LANES], from_last[:, :LANES]), first[:, LANES:]], axis=1
    )
    plus = jnp.concatenate(
        [halves(from_next[:, LANES:], from_last[:, LANES:]), second[:, :LANES]], axis=1
    )
    return shift(minus, 0, -1), shift(plus, 0, 1), from_next, from_last


def return_forces(up, down, keep):
    below = shift(up, 0, 1)
    above = shift(down, 0, -1)
    first = jnp.concatenate([halves(below[:, :LANES], keep), above[:, LANES:]], axis=1)
    second = jnp.concatenate([below[:, :LANES], halves(keep, above[:, LANES:])], axis=1)
    return above, below, shift(first, 1, 0), shift(second, -1, 0)


def table_shape(rows, columns=CLUSTERS):
    return jax.ShapeDtypeStruct((rows, columns), f32)


STAGE = [pltpu.VMEM((3 * CHUNKS, LANES), f32)]
PAIR_SCRATCH = [
    pltpu.VMEM((CLUSTERS, PAIRS), bf16),
    pltpu.VMEM((CLUSTERS, PAIRS), bf16),
    pltpu.VMEM((4 * SLOTS * 8, LANES), f32),
    pltpu.VMEM((4 * SLOTS * 8, LANES), f32),
    pltpu.VMEM((3 * SLOTS * 8, LANES), f32),
    pltpu.VMEM((3 * SLOTS * 8, LANES), f32),
]


def call(kernel, out_shape, operands, scratch=(), cost=0):
    return pl.pallas_call(
        kernel,
        out_shape=out_shape,
        scratch_shapes=list(scratch),
        compiler_params=PARAMS,
        cost_estimate=pl.CostEstimate(flops=cost, bytes_accessed=cost // 200, transcendentals=0),
        name=kernel.__name__,
    )(*operands)


def shards(
    positions,
    velocity,
    radius,
    grain_mask,
    grain_cell,
    inner_pairs,
    cross_pairs,
    send_lists,
    fluid_velocity,
    pressure_grad,
):
    send = send_lists.reshape(1, -1)
    radius = radius.reshape(CHUNKS, LANES)
    mask = grain_mask.reshape(CHUNKS, LANES)
    cell = grain_cell.reshape(CHUNKS, LANES)
    column_here = lax.axis_index("gy")
    fluid = lax.all_gather(jnp.concatenate([fluid_velocity, pressure_grad], axis=0), "gy", axis=0)
    fluid = lax.dynamic_slice_in_dim(fluid, column_here * LANES, LANES, 2).transpose(1, 0, 2)

    full, wide = table_shape(4 * SLOTS), table_shape(4 * SLOTS, 2 * LANES)
    narrow = table_shape(3 * SLOTS, 2 * LANES)
    three = table_shape(3 * SLOTS)
    table, state, first, second = call(
        prepare, (full, full, wide, wide), (positions, radius, mask, send), STAGE, 10**9
    )
    moving, cells, totals = call(
        deposit_kernel,
        (three, jax.ShapeDtypeStruct((SLOTS, CLUSTERS), jnp.int32), table_shape(64, LANES)),
        (velocity, radius, mask, cell),
        STAGE,
        2 * 10**9,
    )
    fields, at_grain = call(
        fluid_kernel,
        (jax.ShapeDtypeStruct((4, 16, LANES), f32), full),
        (totals, fluid, cells),
        (),
        2 * 10**9,
    )
    spread = lax.all_gather(fields, "gy", axis=0)
    owned = lax.dynamic_index_in_dim(spread, column_here, 2, keepdims=False)
    owned = owned.transpose(1, 0, 2).reshape(4, -1)

    reach = table_shape(SLOTS)
    ghost_reach = jnp.zeros((SLOTS, CLUSTERS), f32)
    for substep in range(2):
        below, above, from_next, from_last = spread_ghosts(first, second)
        inner = call(inner_kernel, three, (table, inner_pairs), PAIR_SCRATCH, 4 * 10**9)
        cross, up, down, keep, new_reach = call(
            cross_kernel,
            (three, narrow, narrow, table_shape(3 * SLOTS, LANES), reach),
            (table, cross_pairs, ghost_reach, below, above, from_next, from_last),
            PAIR_SCRATCH,
            4 * 10**9,
        )
        above, below, from_last, from_next = return_forces(up, down, keep)
        operands = (
            table, state, moving, at_grain, inner, cross, above, below, from_last, from_next, send
        )
        if substep == 0:
            ghost_reach = new_reach
            table, state, moving, first, second = call(
                middle_kernel, (full, full, three, narrow, narrow), operands, (), 10**9
            )
        else:
            shape = jax.ShapeDtypeStruct(positions.shape, f32)
            positions, velocity = call(last_kernel, (shape, shape), operands, STAGE, 10**9)
    return positions, velocity, owned[:3], owned[3]


def solution(mesh):
    placed = (
        P(None, ("gx", "gy")),
        P(None, ("gx", "gy")),
        P(("gx", "gy")),
        P(("gx", "gy")),
        P(("gx", "gy")),
        P(None, ("gx", "gy")),
        P(None, ("gx", "gy")),
        P(("gx", "gy")),
        P(None, ("gx", "gy")),
        P(None, ("gx", "gy")),
    )
    return jax.shard_map(
        shards,
        mesh=mesh,
        in_specs=placed,
        out_specs=(
            P(None, ("gx", "gy")),
            P(None, ("gx", "gy")),
            P(None, ("gx", "gy")),
            P(("gx", "gy")),
        ),
        check_vma=False,
    )
```

time: 388 us -> 126 us (0.32)
  the two profiles are of different devices: /device:TPU:27 before, /device:TPU:1 now
where the time goes in v1:
time: 126 us; the launch traced here: 125 us
  blocking collectives  37.5 us (30%)
  starting transfers between devices  36.4 us (29%)
  Pallas kernels  28 us (22%)
  waiting for transfers between devices  16.9 us (13%)
  local copies, waits for them, and re-layouts  5.45 us (4%)
    ppermute x16, starting transfers between devices, shift(): return lax.ppermute(array, ('gx', 'gy'), moves)  36.4 us
    pallas_call x9, Pallas kernels, call(): pl.pallas_call(kernel, out_shape=out_shape, scratch_shapes=list(scratch),...  28 us
    all_gather x1, blocking collectives, shards(): lax.all_gather(jnp.concatenate([fluid_velocity, pressure_grad], axis=0),...  21.3 us
    ppermute x16, waiting for transfers between devices, shift(): return lax.ppermute(array, ('gx', 'gy'), moves)  16.9 us
    all_gather x1, blocking collectives, shards(): spread = lax.all_gather(fields, 'gy', axis=0)  16.2 us
    unnamed x27, local copies, waits for them, and re-layouts  4.77 us
  transfers between devices with their start and end apart: 16, of which 6 were waited for; matrix products, arithmetic and copies ran while one was open for 1% of the time, Pallas kernels for 12%

profile of v1, /device:TPU:1, one launch (start us, length us, event | category | flops | bytes accessed | tf_op | source)
XLA Modules:
  0.0 125.3 jit_solution(2283475571623943569)
XLA Ops:
  0.6 0.7 copy-done.9
  1.3 0.9 copy-done
  2.3 0.8 copy-done.2
  3.1 0.8 copy-done.4
  4.5 1.4 %collective-permute-start = (f32[128,256]{1,0:T(8,128)S(1)}, f32[128,256]{1,0:T(8,128)S(1)}, u32[]{:S(2)}, u32[]{:S(2)}) collective-permute-start(f32[128,256]{1,0:T(8,128)S(1)} %get-tuple-element.35), channel_id=1, source_target_pairs={{0,112},{1,113},{2,114},{3,115},{4,116},{5,117},{6,118},{7,119},{8... | collective-permute-start | bytes 393224 | tf_op jit(solution)/shard_map/ppermute | solution.py:350
  6.0 1.2 collective-permute-start.1
  7.2 21.3 %all-gather.2 = f32[16,6,2048]{2,1,0:T(8,128)S(1)} all-gather(f32[1,6,2048]{2,1,0:T(8,128)S(1)} %maximum_bitcast_fusion), channel_id=2, replica_groups=mesh['gx'=8,'gy'=16] {'gy'}, dimensions={0}, use_global_device_ids=true | all-gather | bytes 835584 | tf_op jit(solution)/shard_map/all_gather | solution.py:420
  28.5 5.1 %inner_kernel.2.inner = f32[96,512]{1,0:T(8,128)S(1)} custom-call(f32[128,512]{1,0:T(8,128)S(1)} %get-tuple-element.29.table, s32[5,1024]{1,0:T(8,128)S(1)} %copy-done.8), custom_call_target="tpu_custom_call" | custom-call | flops 4000000000 | bytes 20000000 | tf_op jit(solution)/shard_map/inner_kernel/pallas_call | solution.py:393
  33.8 2.5 %collective-permute-start.2 = (f32[128,256]{1,0:T(8,128)S(1)}, f32[128,256]{1,0:T(8,128)S(1)}, u32[]{:S(2)}, u32[]{:S(2)}) collective-permute-start(f32[128,256]{1,0:T(8,128)S(1)} %pad_maximum_fusion), channel_id=1, source_target_pairs={{0,15},{1,0},{2,1},{3,2},{4,3},{5,4},{6,5},{7,6},{8,7},{9,8},{10,9... | collective-permute-start | bytes 393224 | tf_op jit(solution)/shard_map/ppermute | solution.py:350
  36.4 0.7 copy-done.3
  37.1 2.0 %deposit_kernel.1 = (f32[96,512]{1,0:T(8,128)S(1)}, s32[32,512]{1,0:T(8,128)S(1)}, f32[64,128]{1,0:T(8,128)S(1)}) custom-call(f32[3,16384]{1,0:T(4,128)S(1)} %copy-done.1, f32[128,128]{1,0:T(8,128)S(1)} %bitcast.24, s32[128,128]{1,0:T(8,128)S(1)} %bitcast.26, s32[128,128]{1,0:T(8,128)S(1)} %bitcast.27), custom_call_target="tpu_custom_call" | custom-call | flops 2000000000 | bytes 10000000 | tf_op jit(solution)/shard_map/deposit_kernel/pallas_call | solution.py:393
  39.1 4.3 %collective-permute-done.3.above = f32[128,256]{1,0:T(8,128)S(1)} collective-permute-done((f32[128,256]{1,0:T(8,128)S(1)}, f32[128,256]{1,0:T(8,128)S(1)}, u32[]{:S(2)}, u32[]{:S(2)}) %collective-permute-start.3) | collective-permute-done | bytes 131104 | tf_op jit(solution)/shard_map/ppermute | solution.py:350
  43.5 5.0 %cross_kernel.2 = (f32[96,512]{1,0:T(8,128)S(1)}, f32[96,256]{1,0:T(8,128)S(1)}, f32[96,256]{1,0:T(8,128)S(1)}, f32[96,128]{1,0:T(8,128)S(1)}, f32[32,512]{1,0:T(8,128)S(1)}) custom-call(f32[128,512]{1,0:T(8,128)S(1)} %get-tuple-element.29.table, s32[5,1024]{1,0:T(8,128)S(1)} %copy-done.7, f32[32,512]{1,0:T(8,128)S(1)} %broadcast_in_dim.3.reach, ...), custom_call_target="tpu_custom_call" | custom-call | flops 4000000000 | bytes 20000000 | tf_op jit(solution)/shard_map/cross_kernel/pallas_call | solution.py:393
  49.0 1.1 collective-permute-start.5
  50.1 2.6 %fluid_kernel.1 = (f32[4,16,128]{2,1,0:T(8,128)S(1)}, f32[128,512]{1,0:T(8,128)S(1)}) custom-call(f32[64,128]{1,0:T(8,128)S(1)} %get-tuple-element.32.totals, f32[6,16,128]{2,1,0:T(8,128)S(1)} %bitcast.22, s32[32,512]{1,0:T(8,128)S(1)} %get-tuple-element.33.cell), custom_call_target="tpu_custom_call" | custom-call | flops 2000000000 | bytes 10000000 | tf_op jit(solution)/shard_map/fluid_kernel/pallas_call | solution.py:393
  52.7 3.1 %collective-permute-done.5.below = f32[96,256]{1,0:T(8,128)S(1)} collective-permute-done((f32[96,256]{1,0:T(8,128)S(1)}, f32[96,256]{1,0:T(8,128)S(1)}, u32[]{:S(2)}, u32[]{:S(2)}) %collective-permute-start.5) | collective-permute-done | bytes 98336 | tf_op jit(solution)/shard_map/ppermute | solution.py:350
  55.8 8.4 %collective-permute-start.7 = (f32[96,256]{1,0:T(8,128)S(1)}, f32[96,256]{1,0:T(8,128)S(1)}, u32[]{:S(2)}, u32[]{:S(2)}) collective-permute-start(f32[96,256]{1,0:T(8,128)S(1)} %pad_maximum_fusion.3), channel_id=1, source_target_pairs={{0,112},{1,113},{2,114},{3,115},{4,116},{5,117},{6,118},{7,119},{8... | collective-permute-start | bytes 294920 | tf_op jit(solution)/shard_map/ppermute | solution.py:350
  64.2 16.2 %all-gather.1 = f32[64,16,128]{2,1,0:T(8,128)S(1)} all-gather(f32[4,16,128]{2,1,0:T(8,128)S(1)} %get-tuple-element.53), channel_id=3, replica_groups=mesh['gx'=8,'gy'=16] {'gy'}, dimensions={0}, use_global_device_ids=true | all-gather | bytes 557056 | tf_op jit(solution)/shard_map/all_gather | solution.py:443
  80.4 0.7 middle_kernel.1
  81.1 5.4 %collective-permute-start.8 = (f32[96,256]{1,0:T(8,128)S(1)}, f32[96,256]{1,0:T(8,128)S(1)}, u32[]{:S(2)}, u32[]{:S(2)}) collective-permute-start(f32[96,256]{1,0:T(8,128)S(1)} %get-tuple-element.45), channel_id=1, source_target_pairs={{0,112},{1,113},{2,114},{3,115},{4,116},{5,117},{6,118},{7,119},{8... | collective-permute-start | bytes 294920 | tf_op jit(solution)/shard_map/ppermute | solution.py:350
  86.6 2.0 %collective-permute-done.8.from_next = f32[96,256]{1,0:T(8,128)S(1)} collective-permute-done((f32[96,256]{1,0:T(8,128)S(1)}, f32[96,256]{1,0:T(8,128)S(1)}, u32[]{:S(2)}, u32[]{:S(2)}) %collective-permute-start.8) | collective-permute-done | bytes 98336 | tf_op jit(solution)/shard_map/ppermute | solution.py:350
  88.7 1.9 %collective-permute-start.11 = (f32[96,256]{1,0:T(8,128)S(1)}, f32[96,256]{1,0:T(8,128)S(1)}, u32[]{:S(2)}, u32[]{:S(2)}) collective-permute-start(f32[96,256]{1,0:T(8,128)S(1)} %pad_maximum_fusion.5), channel_id=1, source_target_pairs={{0,1},{1,2},{2,3},{3,4},{4,5},{5,6},{6,7},{7,8},{8,9},{9,10},{10,1... | collective-permute-start | bytes 294920 | tf_op jit(solution)/shard_map/ppermute | solution.py:350
  90.6 3.1 %collective-permute-start.10 = (f32[96,256]{1,0:T(8,128)S(1)}, f32[96,256]{1,0:T(8,128)S(1)}, u32[]{:S(2)}, u32[]{:S(2)}) collective-permute-start(f32[96,256]{1,0:T(8,128)S(1)} %pad_maximum_fusion.4), channel_id=1, source_target_pairs={{0,15},{1,0},{2,1},{3,2},{4,3},{5,4},{6,5},{7,6},{8,7},{9,8},{10,9... | collective-permute-start | bytes 294920 | tf_op jit(solution)/shard_map/ppermute | solution.py:350
  93.6 1.9 %collective-permute-done.11.above = f32[96,256]{1,0:T(8,128)S(1)} collective-permute-done((f32[96,256]{1,0:T(8,128)S(1)}, f32[96,256]{1,0:T(8,128)S(1)}, u32[]{:S(2)}, u32[]{:S(2)}) %collective-permute-start.11) | collective-permute-done | bytes 98336 | tf_op jit(solution)/shard_map/ppermute | solution.py:350
  95.5 5.4 %cross_kernel.3 = (f32[96,512]{1,0:T(8,128)S(1)}, f32[96,256]{1,0:T(8,128)S(1)}, f32[96,256]{1,0:T(8,128)S(1)}, f32[96,128]{1,0:T(8,128)S(1)}, f32[32,512]{1,0:T(8,128)}) custom-call(f32[128,512]{1,0:T(8,128)S(1)} %get-tuple-element.41.table, s32[5,1024]{1,0:T(8,128)S(1)} %copy-done.7, f32[32,512]{1,0:T(8,128)S(1)} %get-tuple-element.44.reach, ...), custom_call_target="tpu_custom_call" | custom-call | flops 4000000000 | bytes 20000000 | tf_op jit(solution)/shard_map/cross_kernel/pallas_call | solution.py:393
  100.9 4.9 %collective-permute-start.12 = (f32[96,256]{1,0:T(8,128)S(1)}, f32[96,256]{1,0:T(8,128)S(1)}, u32[]{:S(2)}, u32[]{:S(2)}) collective-permute-start(f32[96,256]{1,0:T(8,128)S(1)} %get-tuple-element.48), channel_id=1, source_target_pairs={{0,15},{1,0},{2,1},{3,2},{4,3},{5,4},{6,5},{7,6},{8,7},{9,8},{10,9... | collective-permute-start | bytes 294920 | tf_op jit(solution)/shard_map/ppermute | solution.py:350
  105.8 0.6 slice_bitcast_fusion.1
  106.4 0.6 copy.24
  107.4 5.1 %collective-permute-done.13.below = f32[96,256]{1,0:T(8,128)S(1)} collective-permute-done((f32[96,256]{1,0:T(8,128)S(1)}, f32[96,256]{1,0:T(8,128)S(1)}, u32[]{:S(2)}, u32[]{:S(2)}) %collective-permute-start.13) | collective-permute-done | bytes 98336 | tf_op jit(solution)/shard_map/ppermute | solution.py:350
  112.6 6.1 %collective-permute-start.15 = (f32[96,256]{1,0:T(8,128)S(1)}, f32[96,256]{1,0:T(8,128)S(1)}, u32[]{:S(2)}, u32[]{:S(2)}) collective-permute-start(f32[96,256]{1,0:T(8,128)S(1)} %pad_maximum_fusion.7), channel_id=1, source_target_pairs={{0,112},{1,113},{2,114},{3,115},{4,116},{5,117},{6,118},{7,119},{8... | collective-permute-start | bytes 294920 | tf_op jit(solution)/shard_map/ppermute | solution.py:350
  118.7 5.1 %inner_kernel.3.inner = f32[96,512]{1,0:T(8,128)S(1)} custom-call(f32[128,512]{1,0:T(8,128)S(1)} %get-tuple-element.41.table, s32[5,1024]{1,0:T(8,128)S(1)} %copy-done.8), custom_call_target="tpu_custom_call" | custom-call | flops 4000000000 | bytes 20000000 | tf_op jit(solution)/shard_map/inner_kernel/pallas_call | solution.py:393
  123.8 1.5 %last_kernel.1 = (f32[3,16384]{1,0:T(4,128)}, f32[3,16384]{1,0:T(4,128)}) custom-call(f32[128,512]{1,0:T(8,128)S(1)} %get-tuple-element.41.table, f32[128,512]{1,0:T(8,128)S(1)} %get-tuple-element.42.state, f32[96,512]{1,0:T(8,128)S(1)} %get-tuple-element.43.velocity, f32[128,512]{1,0:T(8,128)S(1)} %get-tuple-element.34.at_grain, ...), custom_call_target="tpu_custom_call" | custom-call | flops 1000000000 | bytes 5000000 | tf_op jit(solution)/shard_map/last_kernel/pallas_call | solution.py:393
  (61 shorter events, 1.9 us)
Async XLA Ops:
  0.6 0.7 copy-start.9
  1.3 0.9 copy-start
  2.3 0.8 copy-start.2
  3.1 0.8 copy-start.4
  3.9 3.2 %copy-start.10 = (f32[3,2048]{1,0:T(4,128)S(1)}, f32[3,2048]{1,0:T(4,128)}, u32[]{:S(2)}) copy-start(f32[3,2048]{1,0:T(4,128)} %param.19) | copy-start | bytes 73732
  3.9 3.2 %copy-start.11 = (f32[3,2048]{1,0:T(4,128)S(1)}, f32[3,2048]{1,0:T(4,128)}, u32[]{:S(2)}) copy-start(f32[3,2048]{1,0:T(4,128)} %param.18) | copy-start | bytes 73732
  4.5 29.2 %collective-permute-start = (f32[128,256]{1,0:T(8,128)S(1)}, f32[128,256]{1,0:T(8,128)S(1)}, u32[]{:S(2)}, u32[]{:S(2)}) collective-permute-start(f32[128,256]{1,0:T(8,128)S(1)} %get-tuple-element.35), channel_id=1, source_target_pairs={{0,112},{1,113},{2,114},{3,115},{4,116},{5,117},{6,118},{7,119},{8... | collective-permute-start | bytes 393224 | tf_op jit(solution)/shard_map/ppermute | solution.py:350
  6.0 27.7 %collective-permute-start.1 = (f32[128,256]{1,0:T(8,128)S(1)}, f32[128,256]{1,0:T(8,128)S(1)}, u32[]{:S(2)}, u32[]{:S(2)}) collective-permute-start(f32[128,256]{1,0:T(8,128)S(1)} %get-tuple-element.36), channel_id=1, source_target_pairs={{0,16},{1,17},{2,18},{3,19},{4,20},{5,21},{6,22},{7,23},{8,24},{9,... | collective-permute-start | bytes 393224 | tf_op jit(solution)/shard_map/ppermute | solution.py:350
  7.2 21.3 %copy-start.8 = (s32[5,1024]{1,0:T(8,128)S(1)}, s32[5,1024]{1,0:T(8,128)}, u32[]{:S(2)}) copy-start(s32[5,1024]{1,0:T(8,128)} %pairs.6) | copy-start | bytes 61444
  33.7 2.6 %copy-start.1 = (f32[3,16384]{1,0:T(4,128)S(1)}, f32[3,16384]{1,0:T(4,128)}, u32[]{:S(2)}) copy-start(f32[3,16384]{1,0:T(4,128)} %velocity.1) | copy-start | bytes 589828
  33.8 5.3 %collective-permute-start.2 = (f32[128,256]{1,0:T(8,128)S(1)}, f32[128,256]{1,0:T(8,128)S(1)}, u32[]{:S(2)}, u32[]{:S(2)}) collective-permute-start(f32[128,256]{1,0:T(8,128)S(1)} %pad_maximum_fusion), channel_id=1, source_target_pairs={{0,15},{1,0},{2,1},{3,2},{4,3},{5,4},{6,5},{7,6},{8,7},{9,8},{10,9... | collective-permute-start | bytes 393224 | tf_op jit(solution)/shard_map/ppermute | solution.py:350
  36.2 0.8 copy-start.3
  36.2 0.9 copy-start.5
  36.2 0.9 copy-start.6
  36.3 7.2 %collective-permute-start.3 = (f32[128,256]{1,0:T(8,128)S(1)}, f32[128,256]{1,0:T(8,128)S(1)}, u32[]{:S(2)}, u32[]{:S(2)}) collective-permute-start(f32[128,256]{1,0:T(8,128)S(1)} %pad_maximum_fusion.1), channel_id=1, source_target_pairs={{0,1},{1,2},{2,3},{3,4},{4,5},{5,6},{6,7},{7,8},{8,9},{9,10},{10,1... | collective-permute-start | bytes 393224 | tf_op jit(solution)/shard_map/ppermute | solution.py:350
  39.1 4.4 %copy-start.7 = (s32[5,1024]{1,0:T(8,128)S(1)}, s32[5,1024]{1,0:T(8,128)}, u32[]{:S(2)}) copy-start(s32[5,1024]{1,0:T(8,128)} %pairs.7) | copy-start | bytes 61444
  48.5 4.2 %collective-permute-start.4 = (f32[96,256]{1,0:T(8,128)S(1)}, f32[96,256]{1,0:T(8,128)S(1)}, u32[]{:S(2)}, u32[]{:S(2)}) collective-permute-start(f32[96,256]{1,0:T(8,128)S(1)} %get-tuple-element.38), channel_id=1, source_target_pairs={{0,15},{1,0},{2,1},{3,2},{4,3},{5,4},{6,5},{7,6},{8,7},{9,8},{10,9... | collective-permute-start | bytes 294920 | tf_op jit(solution)/shard_map/ppermute | solution.py:350
  49.0 6.8 %collective-permute-start.5 = (f32[96,256]{1,0:T(8,128)S(1)}, f32[96,256]{1,0:T(8,128)S(1)}, u32[]{:S(2)}, u32[]{:S(2)}) collective-permute-start(f32[96,256]{1,0:T(8,128)S(1)} %get-tuple-element.39), channel_id=1, source_target_pairs={{0,1},{1,2},{2,3},{3,4},{4,5},{5,6},{6,7},{7,8},{8,9},{9,10},{10,1... | collective-permute-start | bytes 294920 | tf_op jit(solution)/shard_map/ppermute | solution.py:350
  55.8 24.6 %collective-permute-start.7 = (f32[96,256]{1,0:T(8,128)S(1)}, f32[96,256]{1,0:T(8,128)S(1)}, u32[]{:S(2)}, u32[]{:S(2)}) collective-permute-start(f32[96,256]{1,0:T(8,128)S(1)} %pad_maximum_fusion.3), channel_id=1, source_target_pairs={{0,112},{1,113},{2,114},{3,115},{4,116},{5,117},{6,118},{7,119},{8... | collective-permute-start | bytes 294920 | tf_op jit(solution)/shard_map/ppermute | solution.py:350
  64.2 16.2 %collective-permute-start.6 = (f32[96,256]{1,0:T(8,128)S(1)}, f32[96,256]{1,0:T(8,128)S(1)}, u32[]{:S(2)}, u32[]{:S(2)}) collective-permute-start(f32[96,256]{1,0:T(8,128)S(1)} %pad_maximum_fusion.2), channel_id=1, source_target_pairs={{0,16},{1,17},{2,18},{3,19},{4,20},{5,21},{6,22},{7,23},{8,24},{9,... | collective-permute-start | bytes 294920 | tf_op jit(solution)/shard_map/ppermute | solution.py:350
  81.1 7.5 %collective-permute-start.8 = (f32[96,256]{1,0:T(8,128)S(1)}, f32[96,256]{1,0:T(8,128)S(1)}, u32[]{:S(2)}, u32[]{:S(2)}) collective-permute-start(f32[96,256]{1,0:T(8,128)S(1)} %get-tuple-element.45), channel_id=1, source_target_pairs={{0,112},{1,113},{2,114},{3,115},{4,116},{5,117},{6,118},{7,119},{8... | collective-permute-start | bytes 294920 | tf_op jit(solution)/shard_map/ppermute | solution.py:350
  86.6 2.1 %collective-permute-start.9 = (f32[96,256]{1,0:T(8,128)S(1)}, f32[96,256]{1,0:T(8,128)S(1)}, u32[]{:S(2)}, u32[]{:S(2)}) collective-permute-start(f32[96,256]{1,0:T(8,128)S(1)} %get-tuple-element.46), channel_id=1, source_target_pairs={{0,16},{1,17},{2,18},{3,19},{4,20},{5,21},{6,22},{7,23},{8,24},{9,... | collective-permute-start | bytes 294920 | tf_op jit(solution)/shard_map/ppermute | solution.py:350
  88.7 6.9 %collective-permute-start.11 = (f32[96,256]{1,0:T(8,128)S(1)}, f32[96,256]{1,0:T(8,128)S(1)}, u32[]{:S(2)}, u32[]{:S(2)}) collective-permute-start(f32[96,256]{1,0:T(8,128)S(1)} %pad_maximum_fusion.5), channel_id=1, source_target_pairs={{0,1},{1,2},{2,3},{3,4},{4,5},{5,6},{6,7},{7,8},{8,9},{9,10},{10,1... | collective-permute-start | bytes 294920 | tf_op jit(solution)/shard_map/ppermute | solution.py:350
  90.6 5.0 %collective-permute-start.10 = (f32[96,256]{1,0:T(8,128)S(1)}, f32[96,256]{1,0:T(8,128)S(1)}, u32[]{:S(2)}, u32[]{:S(2)}) collective-permute-start(f32[96,256]{1,0:T(8,128)S(1)} %pad_maximum_fusion.4), channel_id=1, source_target_pairs={{0,15},{1,0},{2,1},{3,2},{4,3},{5,4},{6,5},{7,6},{8,7},{9,8},{10,9... | collective-permute-start | bytes 294920 | tf_op jit(solution)/shard_map/ppermute | solution.py:350
  100.9 6.5 %collective-permute-start.12 = (f32[96,256]{1,0:T(8,128)S(1)}, f32[96,256]{1,0:T(8,128)S(1)}, u32[]{:S(2)}, u32[]{:S(2)}) collective-permute-start(f32[96,256]{1,0:T(8,128)S(1)} %get-tuple-element.48), channel_id=1, source_target_pairs={{0,15},{1,0},{2,1},{3,2},{4,3},{5,4},{6,5},{7,6},{8,7},{9,8},{10,9... | collective-permute-start | bytes 294920 | tf_op jit(solution)/shard_map/ppermute | solution.py:350
  105.8 6.8 %collective-permute-start.13 = (f32[96,256]{1,0:T(8,128)S(1)}, f32[96,256]{1,0:T(8,128)S(1)}, u32[]{:S(2)}, u32[]{:S(2)}) collective-permute-start(f32[96,256]{1,0:T(8,128)S(1)} %get-tuple-element.49), channel_id=1, source_target_pairs={{0,1},{1,2},{2,3},{3,4},{4,5},{5,6},{6,7},{7,8},{8,9},{9,10},{10,1... | collective-permute-start | bytes 294920 | tf_op jit(solution)/shard_map/ppermute | solution.py:350
  112.6 11.2 %collective-permute-start.15 = (f32[96,256]{1,0:T(8,128)S(1)}, f32[96,256]{1,0:T(8,128)S(1)}, u32[]{:S(2)}, u32[]{:S(2)}) collective-permute-start(f32[96,256]{1,0:T(8,128)S(1)} %pad_maximum_fusion.7), channel_id=1, source_target_pairs={{0,112},{1,113},{2,114},{3,115},{4,116},{5,117},{6,118},{7,119},{8... | collective-permute-start | bytes 294920 | tf_op jit(solution)/shard_map/ppermute | solution.py:350
  118.7 5.1 %collective-permute-start.14 = (f32[96,256]{1,0:T(8,128)S(1)}, f32[96,256]{1,0:T(8,128)S(1)}, u32[]{:S(2)}, u32[]{:S(2)}) collective-permute-start(f32[96,256]{1,0:T(8,128)S(1)} %pad_maximum_fusion.6), channel_id=1, source_target_pairs={{0,16},{1,17},{2,18},{3,19},{4,20},{5,21},{6,22},{7,23},{8,24},{9,... | collective-permute-start | bytes 294920 | tf_op jit(solution)/shard_map/ppermute | solution.py:350

commit v2 on v1

--- a/solution.py
+++ b/solution.py
@@ -109,7 +109,13 @@
         out[...] = gather(parts, hot, rows)
 
 
-def prepare(positions, radius, mask, send, table_out, state_out, first, second, stage):
+def prepare(
+    positions_far, radius_far, mask_far, send_far, table_out, state_out, first, second,
+    positions, radius, mask, send, stage, arrived,
+):
+    fetch(
+        ((positions_far, positions), (radius_far, radius), (mask_far, mask), (send_far, send)), arrived
+    )
     parts = load_components(positions, stage)
     reach = to_table(radius[...])
     weights = to_table(mask[...].astype(f32))
@@ -122,8 +128,7 @@
     send_pieces(table, 4 * SLOTS, send, first, second)
 
 
-def contacts(leading, partner, on_leading, on_partner):
-    on_partner[...] = jnp.zeros_like(on_partner)
+def contacts(leading, partner, on_leading, on_partner, begin, end):
     step = 4
 
     def row(component, slot):
@@ -152,47 +157,86 @@
                 on_leading[row(c, base + i), :] = sums[i][c]
         return carry
 
-    lax.fori_loop(0, SLOTS // step, some_slots, 0)
-
-
-def pair_sums(pairs, leading_parts, partner_parts, partner_column, scratch):
-    hot_a, hot_b, leading, partner, on_leading, on_partner = scratch
+    lax.fori_loop(begin // step, end // step, some_slots, 0)
+
+
+def fill_hot(pairs, row, column, hot):
     width = 2 * LANES
     for block in range(PAIRS // width):
         span = slice(block * width, (block + 1) * width)
-        for row, column, parts, hot, landed in (
-            (0, cluster_column, leading_parts, hot_a, leading),
-            (1, partner_column, partner_parts, hot_b, partner),
-        ):
-            chosen = one_hot(column(pairs[row : row + 1, span]), CLUSTERS)
-            hot[:, span] = chosen
-            picked = gather(parts, chosen, 4 * SLOTS)
-            if row == 0:
-                offsets = pairs[2:5, span].astype(f32)
-                picked = jnp.concatenate(
-                    [picked[c * SLOTS : (c + 1) * SLOTS] - offsets[c : c + 1] for c in range(3)]
-                    + [picked[3 * SLOTS :]],
-                    axis=0,
-                )
-            for k in range(2):
-                landed[pl.ds(2 * block + k, 4 * SLOTS, stride=8), :] = picked[
-                    :, k * LANES : (k + 1) * LANES
-                ]
-    contacts(leading, partner, on_leading, on_partner)
-    totals = []
-    for sums, hot in ((on_leading, hot_a), (on_partner, hot_b)):
-        pieces = jnp.concatenate(
-            [sums[pl.ds(k, 3 * SLOTS, stride=8), :] for k in range(PAIRS // LANES)], axis=1
-        )
-        added = dot_lanes(jnp.concatenate(split(pieces, 2), axis=0), hot[...])
-        totals.append(added[: 3 * SLOTS] + added[3 * SLOTS :])
-    return totals
-
-
-def inner_kernel(table, pairs, force, *scratch):
-    parts = jnp.concatenate(split(table[...], 3), axis=0)
-    on_leading, on_partner = pair_sums(pairs, parts, parts, cluster_column, scratch)
-    force[...] = on_leading - on_partner
+        hot[:, span] = one_hot(column(pairs[row : row + 1, span]), CLUSTERS)
+
+
+def fill_slots(parts, hot, pairs, landed):
+    width = 2 * LANES
+    for block in range(PAIRS // width):
+        span = slice(block * width, (block + 1) * width)
+        picked = gather(parts, hot[:, span], 4 * SLOTS)
+        if pairs is not None:
+            offsets = pairs[2:5, span].astype(f32)
+            picked = jnp.concatenate(
+                [picked[c * SLOTS : (c + 1) * SLOTS] - offsets[c : c + 1] for c in range(3)]
+                + [picked[3 * SLOTS :]],
+                axis=0,
+            )
+        for k in range(2):
+            landed[pl.ds(2 * block + k, 4 * SLOTS, stride=8), :] = picked[
+                :, k * LANES : (k + 1) * LANES
+            ]
+
+
+def scatter(sums, hot):
+    pieces = jnp.concatenate(
+        [sums[pl.ds(k, 3 * SLOTS, stride=8), :] for k in range(PAIRS // LANES)], axis=1
+    )
+    added = dot_lanes(jnp.concatenate(split(pieces, 2), axis=0), hot[...])
+    return added[: 3 * SLOTS] + added[3 * SLOTS :]
+
+
+def table_parts(table):
+    return jnp.concatenate(split(table[...], 3), axis=0)
+
+
+INNER_SPLIT = 16
+
+
+def inner_start(table, pairs, hot_a, hot_b, leading, partner, on_leading, on_partner):
+    fill_hot(pairs, 0, cluster_column, hot_a)
+    fill_hot(pairs, 1, cluster_column, hot_b)
+    inner_again(table, pairs, hot_a, hot_b, leading, partner, on_leading, on_partner)
+
+
+def inner_again(table, pairs, hot_a, hot_b, leading, partner, on_leading, on_partner):
+    parts = table_parts(table)
+    fill_slots(parts, hot_a, pairs, leading)
+    fill_slots(parts, hot_b, None, partner)
+    on_partner[...] = jnp.zeros_like(on_partner)
+    contacts(leading, partner, on_leading, on_partner, 0, INNER_SPLIT)
+
+
+def inner_end(
+    hot_a, hot_b, leading, partner, on_leading_first, on_partner_first, force, on_leading, on_partner
+):
+    for c in range(3):
+        done = slice(c * SLOTS * 8, (c * SLOTS + INNER_SPLIT) * 8)
+        on_leading[done, :] = on_leading_first[done, :]
+    on_partner[...] = on_partner_first[...]
+    contacts(leading, partner, on_leading, on_partner, INNER_SPLIT, SLOTS)
+    force[...] = scatter(on_leading, hot_a) - scatter(on_partner, hot_b)
+
+
+def cross_start(table, pairs, hot_a, hot_b, leading):
+    fill_hot(pairs, 0, cluster_column, hot_a)
+    fill_hot(pairs, 1, ghost_column, hot_b)
+    cross_again(table, pairs, hot_a, leading)
+
+
+def cross_again(table, pairs, hot_a, leading):
+    fill_slots(table_parts(table), hot_a, pairs, leading)
+
+
+def cross_end(on_leading, hot_a, force):
+    force[...] = scatter(on_leading, hot_a)
 
 
 def present_tile(low, high):
@@ -207,7 +251,8 @@
 
 
 def cross_kernel(
-    table, pairs, reach, below, above, from_next, from_last, force, up, down, keep, reach_out, *scratch
+    leading, hot_b, reach, below, above, from_next, from_last,
+    on_leading, up, down, keep, reach_out, partner, on_partner,
 ):
     rows = below.shape[0]
     low = lower_half((rows, LANES))
@@ -224,16 +269,64 @@
         reach_out[:, k * LANES : (k + 1) * LANES] = size
         tiles[k] = jnp.concatenate([placed, size], axis=0)
     ghosts = jnp.concatenate(tiles, axis=1)
-    own_parts = jnp.concatenate(split(table[...], 3), axis=0)
-    ghost_parts = jnp.concatenate(split(ghosts, 3), axis=0)
-    on_leading, on_partner = pair_sums(pairs, own_parts, ghost_parts, ghost_column, scratch)
-    force[...] = on_leading
-    up[...] = on_partner[:, : 2 * LANES]
-    down[...] = on_partner[:, LANES : 3 * LANES]
-    keep[...] = on_partner[:, 3 * LANES :]
-
-
-def deposit_kernel(velocity, radius, mask, cell, velocity_out, cell_out, totals, stage):
+    fill_slots(jnp.concatenate(split(ghosts, 3), axis=0), hot_b, None, partner)
+    on_partner[...] = jnp.zeros_like(on_partner)
+    contacts(leading, partner, on_leading, on_partner, 0, SLOTS)
+    back = scatter(on_partner, hot_b)
+    up[...] = back[:, : 2 * LANES]
+    down[...] = back[:, LANES : 3 * LANES]
+    keep[...] = back[:, 3 * LANES :]
+
+
+def fetch(pairs, arrived):
+    copies = [
+        pltpu.make_async_copy(far, near, arrived.at[k]) for k, (far, near) in enumerate(pairs)
+    ]
+    for copy in copies:
+        copy.start()
+    for copy in copies:
+        copy.wait()
+
+
+def part_parcels(parcels, bit, stay, away):
+    mine = (lax.axis_index("gy") & bit) > 0
+    for k, low in enumerate([d for d in range(16) if not d & bit]):
+        stay[k] = jnp.where(mine, parcels[low | bit], parcels[low])
+        away[k] = jnp.where(mine, parcels[low], parcels[low | bit])
+
+
+def join_parcels(stay, got, bit):
+    mine = (lax.axis_index("gy") & bit) > 0
+    parcels = [None] * 16
+    for k, low in enumerate([d for d in range(16) if not d & bit]):
+        parcels[low] = jnp.where(mine, got[k], stay[k])
+        parcels[low | bit] = jnp.where(mine, stay[k], got[k])
+    return parcels
+
+
+def relay(bit):
+    def relay_parcels(stay, got, stay_out, away_out):
+        part_parcels(join_parcels(stay, got, bit), 2 * bit, stay_out, away_out)
+
+    return relay_parcels
+
+
+def deposit_kernel(
+    velocity_far, radius_far, mask_far, cell_far, fluid_far, pressure_far,
+    velocity_out, cell_out, totals_out, stay, away,
+    velocity, radius, mask, cell, fluid, pressure, stage, arrived,
+):
+    fetch(
+        (
+            (velocity_far, velocity),
+            (radius_far, radius),
+            (mask_far, mask),
+            (cell_far, cell),
+            (fluid_far, fluid),
+            (pressure_far, pressure),
+        ),
+        arrived,
+    )
     parts = load_components(velocity, stage)
     reach = to_table(radius[...])
     weights = to_table(mask[...].astype(f32))
@@ -252,20 +345,34 @@
             [jnp.where(group, amount[slot : slot + 1], 0.0) for amount in amounts], axis=0
         )
         total = total + dot_lanes(jnp.concatenate(split(spread, 2), axis=0), hot)
-    totals[...] = total[:64] + total[64:]
-
-
-def fluid_kernel(totals, fluid, cell, fields_out, at_grain):
+    total = total[:64] + total[64:]
+    totals_out[...] = total
+    parcels = []
+    for owner in range(16):
+        span = slice(owner * LANES, (owner + 1) * LANES)
+        parcels.append(
+            jnp.concatenate(
+                [total[c * 16 + owner : c * 16 + owner + 1] for c in range(4)]
+                + [fluid[:, span] + time_step * pressure[:, span], jnp.zeros((1, LANES), f32)],
+                axis=0,
+            )
+        )
+    part_parcels(parcels, 1, stay, away)
+
+
+def fluid_kernel(totals, stay, got, cell, at_grain, parcels_out):
+    parcels = join_parcels(stay, got, 8)
+    for source in range(16):
+        parcels_out[source] = parcels[source]
     volume = totals[:16]
-    void_out = jnp.maximum(1.0 - volume / cell_volume, void_floor)
-    drag_rate = drag_factor * (1.1 - void_out) / (void_out * void_out)
-    below = void_out + time_step * drag_rate * volume / cell_volume
+    void_here = jnp.maximum(1.0 - volume / cell_volume, void_floor)
+    drag_rate = drag_factor * (1.1 - void_here) / (void_here * void_here)
+    below = void_here + time_step * drag_rate * volume / cell_volume
     fields = []
     for c in range(3):
-        push = void_out * fluid[c + 3] + drag_rate * totals[(c + 1) * 16 : (c + 2) * 16] / cell_volume
-        fields.append((void_out * fluid[c] + time_step * push) / below)
-        fields_out[c] = fields[c]
-    fields_out[3] = void_out
+        momentum = drag_rate * totals[(c + 1) * 16 : (c + 2) * 16] / cell_volume
+        driven = jnp.concatenate([parcels[k][4 + c : 5 + c] for k in range(16)], axis=0)
+        fields.append((void_here * driven + time_step * momentum) / below)
     fields.append(drag_rate)
     parts = jnp.concatenate(split(jnp.concatenate(fields, axis=0), 2), axis=1)
     for slot in range(SLOTS):
@@ -277,6 +384,18 @@
             chosen = jnp.where(group, seen[c * 16 : (c + 1) * 16], 0.0)
             row = c * SLOTS + slot
             at_grain[row : row + 1, :] = jnp.sum(chosen, axis=0, keepdims=True)
+
+
+def owned_kernel(parcels, fluid, pressure, fluid_out, void_out):
+    for source in range(16):
+        span = slice(source * LANES, (source + 1) * LANES)
+        volume = parcels[source, 0:1, :]
+        void_here = jnp.maximum(1.0 - volume / cell_volume, void_floor)
+        drag_rate = drag_factor * (1.1 - void_here) / (void_here * void_here)
+        below = void_here + time_step * drag_rate * volume / cell_volume
+        push = void_here * pressure[:, span] + drag_rate * parcels[source, 1:4, :] / cell_volume
+        fluid_out[:, span] = (void_here * fluid[:, span] + time_step * push) / below
+        void_out[source : source + 1, :] = void_here
 
 
 def advance(state, velocity, reach, at_grain, inner, cross, above, below, from_last, from_next, send):
@@ -350,54 +469,65 @@
     return lax.ppermute(array, ("gx", "gy"), moves)
 
 
+def swap(array, bit):
+    size_x, size_y = lax.axis_size("gx"), lax.axis_size("gy")
+    moves = [(x * size_y + y, x * size_y + (y ^ bit)) for x in range(size_x) for y in range(size_y)]
+    return lax.ppermute(array, ("gx", "gy"), moves)
+
+
 def halves(low_from, high_from):
     return jnp.where(lower_half(low_from.shape), low_from, high_from)
 
 
-def spread_ghosts(first, second):
-    from_next = shift(first, -1, 0)
-    from_last = shift(second, 1, 0)
+def pass_ghosts(first, second, from_next, from_last):
     minus = jnp.concatenate(
         [halves(from_next[:, :LANES], from_last[:, :LANES]), first[:, LANES:]], axis=1
     )
     plus = jnp.concatenate(
         [halves(from_next[:, LANES:], from_last[:, LANES:]), second[:, :LANES]], axis=1
     )
-    return shift(minus, 0, -1), shift(plus, 0, 1), from_next, from_last
-
-
-def return_forces(up, down, keep):
-    below = shift(up, 0, 1)
-    above = shift(down, 0, -1)
+    return minus, plus
+
+
+def pass_forces(above, below, keep):
     first = jnp.concatenate([halves(below[:, :LANES], keep), above[:, LANES:]], axis=1)
     second = jnp.concatenate([below[:, :LANES], halves(keep, above[:, LANES:])], axis=1)
-    return above, below, shift(first, 1, 0), shift(second, -1, 0)
+    return first, second
 
 
 def table_shape(rows, columns=CLUSTERS):
     return jax.ShapeDtypeStruct((rows, columns), f32)
 
 
-STAGE = [pltpu.VMEM((3 * CHUNKS, LANES), f32)]
-PAIR_SCRATCH = [
-    pltpu.VMEM((CLUSTERS, PAIRS), bf16),
-    pltpu.VMEM((CLUSTERS, PAIRS), bf16),
-    pltpu.VMEM((4 * SLOTS * 8, LANES), f32),
-    pltpu.VMEM((4 * SLOTS * 8, LANES), f32),
-    pltpu.VMEM((3 * SLOTS * 8, LANES), f32),
-    pltpu.VMEM((3 * SLOTS * 8, LANES), f32),
-]
-
-
-def call(kernel, out_shape, operands, scratch=(), cost=0):
+STAGE = pltpu.VMEM((3 * CHUNKS, LANES), f32)
+HOT = jax.ShapeDtypeStruct((CLUSTERS, PAIRS), bf16)
+SLOT_ROWS = table_shape(4 * SLOTS * 8, LANES)
+FORCE_ROWS = table_shape(3 * SLOTS * 8, LANES)
+FORCE_SCRATCH = pltpu.VMEM((3 * SLOTS * 8, LANES), f32)
+PARCELS = jax.ShapeDtypeStruct((8, 8, LANES), f32)
+
+
+def call(kernel, out_shape, operands, scratch=(), cost=1.0, far=False, after=()):
+    count = len(operands)
+
+    def body(*refs):
+        kernel(*refs[:count], *refs[count + len(after) :])
+
+    space = pltpu.HBM if far else pltpu.VMEM
+    if far:
+        operands = tuple(pltpu.with_memory_space_constraint(array, pltpu.HBM) for array in operands)
     return pl.pallas_call(
-        kernel,
+        body,
         out_shape=out_shape,
+        in_specs=[pl.BlockSpec(memory_space=space)] * count
+        + [pl.BlockSpec(memory_space=pl.ANY)] * len(after),
         scratch_shapes=list(scratch),
         compiler_params=PARAMS,
-        cost_estimate=pl.CostEstimate(flops=cost, bytes_accessed=cost // 200, transcendentals=0),
+        cost_estimate=pl.CostEstimate(
+            flops=int(cost * 10**9), bytes_accessed=int(cost * 10**6), transcendentals=0
+        ),
         name=kernel.__name__,
-    )(*operands)
+    )(*operands, *after)
 
 
 def shards(
@@ -416,59 +546,120 @@
     radius = radius.reshape(CHUNKS, LANES)
     mask = grain_mask.reshape(CHUNKS, LANES)
     cell = grain_cell.reshape(CHUNKS, LANES)
-    column_here = lax.axis_index("gy")
-    fluid = lax.all_gather(jnp.concatenate([fluid_velocity, pressure_grad], axis=0), "gy", axis=0)
-    fluid = lax.dynamic_slice_in_dim(fluid, column_here * LANES, LANES, 2).transpose(1, 0, 2)
 
     full, wide = table_shape(4 * SLOTS), table_shape(4 * SLOTS, 2 * LANES)
-    narrow = table_shape(3 * SLOTS, 2 * LANES)
-    three = table_shape(3 * SLOTS)
+    narrow, single = table_shape(3 * SLOTS, 2 * LANES), table_shape(3 * SLOTS, LANES)
+    three, reach = table_shape(3 * SLOTS), table_shape(SLOTS)
+
+    def near(array):
+        return pltpu.VMEM(array.shape, array.dtype)
+
+    operands = (positions, radius, mask, send)
     table, state, first, second = call(
-        prepare, (full, full, wide, wide), (positions, radius, mask, send), STAGE, 10**9
-    )
-    moving, cells, totals = call(
+        prepare,
+        (full, full, wide, wide),
+        operands,
+        [near(array) for array in operands] + [STAGE, pltpu.SemaphoreType.DMA((4,))],
+        far=True,
+    )
+    operands = (velocity, radius, mask, cell, fluid_velocity, pressure_grad)
+    moving, cells, totals, stay, away = call(
         deposit_kernel,
-        (three, jax.ShapeDtypeStruct((SLOTS, CLUSTERS), jnp.int32), table_shape(64, LANES)),
-        (velocity, radius, mask, cell),
-        STAGE,
-        2 * 10**9,
-    )
-    fields, at_grain = call(
-        fluid_kernel,
-        (jax.ShapeDtypeStruct((4, 16, LANES), f32), full),
-        (totals, fluid, cells),
-        (),
-        2 * 10**9,
-    )
-    spread = lax.all_gather(fields, "gy", axis=0)
-    owned = lax.dynamic_index_in_dim(spread, column_here, 2, keepdims=False)
-    owned = owned.transpose(1, 0, 2).reshape(4, -1)
-
-    reach = table_shape(SLOTS)
+        (
+            three,
+            jax.ShapeDtypeStruct((SLOTS, CLUSTERS), jnp.int32),
+            table_shape(64, LANES),
+            PARCELS,
+            PARCELS,
+        ),
+        operands,
+        [near(array) for array in operands] + [STAGE, pltpu.SemaphoreType.DMA((6,))],
+        3,
+        far=True,
+        after=(table,),
+    )
+    got = swap(away, 1)
+
     ghost_reach = jnp.zeros((SLOTS, CLUSTERS), f32)
     for substep in range(2):
-        below, above, from_next, from_last = spread_ghosts(first, second)
-        inner = call(inner_kernel, three, (table, inner_pairs), PAIR_SCRATCH, 4 * 10**9)
-        cross, up, down, keep, new_reach = call(
+        from_next, from_last = shift(first, -1, 0), shift(second, 1, 0)
+        minus, plus = pass_ghosts(first, second, from_next, from_last)
+        below, above = shift(minus, 0, -1), shift(plus, 0, 1)
+        if substep == 0:
+            hot_a, hot_b, *rows = call(
+                inner_start,
+                (HOT, HOT, SLOT_ROWS, SLOT_ROWS, FORCE_ROWS, FORCE_ROWS),
+                (table, inner_pairs),
+                cost=3,
+                after=(minus, plus),
+            )
+            stay, away = call(relay(1), (PARCELS, PARCELS), (stay, got), after=(rows[0],))
+            got = swap(away, 2)
+            hot_c, hot_d, leading = call(
+                cross_start, (HOT, HOT, SLOT_ROWS), (table, cross_pairs), after=(away,)
+            )
+        else:
+            rows = call(
+                inner_again,
+                (SLOT_ROWS, SLOT_ROWS, FORCE_ROWS, FORCE_ROWS),
+                (table, inner_pairs, hot_a, hot_b),
+                cost=3,
+            )
+            leading = call(
+                cross_again, SLOT_ROWS, (table, cross_pairs, hot_c), after=(minus, plus, rows[0])
+            )
+        on_leading, up, down, keep, ghost_reach = call(
             cross_kernel,
-            (three, narrow, narrow, table_shape(3 * SLOTS, LANES), reach),
-            (table, cross_pairs, ghost_reach, below, above, from_next, from_last),
-            PAIR_SCRATCH,
-            4 * 10**9,
+            (FORCE_ROWS, narrow, narrow, single, reach),
+            (leading, hot_d, ghost_reach, below, above, from_next, from_last),
+            [pltpu.VMEM(SLOT_ROWS.shape, f32), FORCE_SCRATCH],
+            4,
         )
-        above, below, from_last, from_next = return_forces(up, down, keep)
+        below, above = shift(up, 0, 1), shift(down, 0, -1)
+        if substep == 0:
+            stay, away = call(relay(2), (PARCELS, PARCELS), (stay, got), after=(keep,))
+            got = swap(away, 4)
+        inner = call(
+            inner_end,
+            three,
+            (hot_a, hot_b, *rows),
+            [FORCE_SCRATCH, FORCE_SCRATCH],
+            3,
+            after=(keep, away),
+        )
+        cross = call(cross_end, three, (on_leading, hot_c), after=(away,))
+        if substep == 0:
+            stay, away = call(relay(4), (PARCELS, PARCELS), (stay, got), after=(inner, cross))
+            got = swap(away, 8)
+        first, second = pass_forces(above, below, keep)
+        from_last, from_next = shift(first, 1, 0), shift(second, -1, 0)
+        if substep == 0:
+            at_grain, parcels = call(
+                fluid_kernel,
+                (full, jax.ShapeDtypeStruct((16, 8, LANES), f32)),
+                (totals, stay, got, cells),
+                (),
+                3,
+                after=(first, second),
+            )
+        else:
+            fluid_out, void_out = call(
+                owned_kernel,
+                (jax.ShapeDtypeStruct(fluid_velocity.shape, f32), table_shape(16, LANES)),
+                (parcels, fluid_velocity, pressure_grad),
+                after=(first, second),
+            )
         operands = (
             table, state, moving, at_grain, inner, cross, above, below, from_last, from_next, send
         )
         if substep == 0:
-            ghost_reach = new_reach
             table, state, moving, first, second = call(
-                middle_kernel, (full, full, three, narrow, narrow), operands, (), 10**9
+                middle_kernel, (full, full, three, narrow, narrow), operands
             )
         else:
             shape = jax.ShapeDtypeStruct(positions.shape, f32)
-            positions, velocity = call(last_kernel, (shape, shape), operands, STAGE, 10**9)
-    return positions, velocity, owned[:3], owned[3]
+            positions, velocity = call(last_kernel, (shape, shape), operands, [STAGE])
+    return positions, velocity, fluid_out, void_out.reshape(-1)
 
 
 def solution(mesh):

time: 126 us -> 86.4 us (0.69)
  the two profiles are of different devices: /device:TPU:1 before, /device:TPU:7 now
where the time goes in v2:
time: 86.4 us; the launch traced here: 86 us
  starting transfers between devices  31.3 us (36%)
  Pallas kernels  30.7 us (36%)
  waiting for transfers between devices  20.6 us (24%)
  local copies, waits for them, and re-layouts  2.26 us (3%)
  between operations  0.99 us (1%)
    pallas_call x19, Pallas kernels, call(): pl.pallas_call(body, out_shape=out_shape, in_specs=[pl.BlockSpec(memory_s...  30.7 us
    ppermute x16, starting transfers between devices, shift(): return lax.ppermute(array, ('gx', 'gy'), moves)  29.5 us
    ppermute x16, waiting for transfers between devices, shift(): return lax.ppermute(array, ('gx', 'gy'), moves)  18.8 us
    unnamed x10, local copies, waits for them, and re-layouts  2.23 us
    ppermute x4, starting transfers between devices, swap(): return lax.ppermute(array, ('gx', 'gy'), moves)  1.82 us
    ppermute x4, waiting for transfers between devices, swap(): return lax.ppermute(array, ('gx', 'gy'), moves)  1.78 us
  transfers between devices with their start and end apart: 20, of which 9 were waited for; matrix products, arithmetic and copies ran while one was open for 0% of the time, Pallas kernels for 26%

profile of v2, /device:TPU:7, one launch (start us, length us, event | category | flops | bytes accessed | tf_op | source)
XLA Modules:
  0.0 86.0 jit_solution(10234059101590554634)
XLA Ops:
  0.6 1.6 %prepare.1 = (f32[128,512]{1,0:T(8,128)S(1)}, f32[128,512]{1,0:T(8,128)S(1)}, f32[128,256]{1,0:T(8,128)S(1)}, f32[128,256]{1,0:T(8,128)S(1)}) custom-call(f32[3,16384]{1,0:T(4,128)} %refs_0_.2, f32[128,128]{1,0:T(8,128)} %bitcast.8, s32[128,128]{1,0:T(8,128)} %bitcast.10, s32[1,512]{1,0:T(1,128)} %bitcast.5), custom_call_target="tpu_custom_call" | custom-call | flops 1000000000 | bytes 1000000 | tf_op jit(solution)/shard_map/prepare/pallas_call | solution.py:519
  2.2 0.7 collective-permute-start.1
  2.9 2.3 %collective-permute-start.2 = (f32[128,256]{1,0:T(8,128)S(1)}, f32[128,256]{1,0:T(8,128)S(1)}, u32[]{:S(2)}, u32[]{:S(2)}) collective-permute-start(f32[128,256]{1,0:T(8,128)S(1)} %get-tuple-element.59), channel_id=1, source_target_pairs={{0,16},{1,17},{2,18},{3,19},{4,20},{5,21},{6,22},{7,23},{8,24},{9,... | collective-permute-start | bytes 393224 | tf_op jit(solution)/shard_map/ppermute | solution.py:469
  5.2 3.0 %deposit_kernel.1 = (f32[96,512]{1,0:T(8,128)S(1)}, s32[32,512]{1,0:T(8,128)S(1)}, f32[64,128]{1,0:T(8,128)S(1)}, f32[8,8,128]{2,1,0:T(8,128)S(1)}, f32[8,8,128]{2,1,0:T(8,128)S(1)}) custom-call(f32[3,16384]{1,0:T(4,128)} %refs_0_.3, f32[128,128]{1,0:T(8,128)} %bitcast.9, s32[128,128]{1,0:T(8,128)} %bitcast.11, s32[128,128]{1,0:T(8,128)} %bitcast.12, ...), custom_call_target="tpu_custom_call" | custom-call | flops 3000000000 | bytes 3000000 | tf_op jit(solution)/shard_map/deposit_kernel/pallas_call | solution.py:519
  8.2 1.4 %collective-permute-start = (f32[8,8,128]{2,1,0:T(8,128)S(1)}, f32[8,8,128]{2,1,0:T(8,128)S(1)}, u32[]{:S(2)}, u32[]{:S(2)}) collective-permute-start(f32[8,8,128]{2,1,0:T(8,128)S(1)} %get-tuple-element.57), channel_id=1, source_target_pairs={{0,1},{1,0},{2,3},{3,2},{4,5},{5,4},{6,7},{7,6},{8,9},{9,8},{10,11... | collective-permute-start | bytes 98312 | tf_op jit(solution)/shard_map/ppermute | solution.py:475
  9.7 5.4 %collective-permute-start.4 = (f32[128,256]{1,0:T(8,128)S(1)}, f32[128,256]{1,0:T(8,128)S(1)}, u32[]{:S(2)}, u32[]{:S(2)}) collective-permute-start(f32[128,256]{1,0:T(8,128)S(1)} %pad_maximum_fusion.refs_2_), channel_id=1, source_target_pairs={{0,15},{1,0},{2,1},{3,2},{4,3},{5,4},{6,5},{7,6},{8,7},{9,8},{10,9... | collective-permute-start | bytes 393224 | tf_op jit(solution)/shard_map/ppermute | solution.py:469
  15.9 2.5 %inner_start.1 = (bf16[512,1024]{1,0:T(8,128)(2,1)S(1)}, bf16[512,1024]{1,0:T(8,128)(2,1)S(1)}, f32[1024,128]{1,0:T(8,128)S(1)}, f32[1024,128]{1,0:T(8,128)S(1)}...) custom-call(f32[128,512]{1,0:T(8,128)S(1)} %get-tuple-element.52.refs_6_.refs_0_, s32[5,1024]{1,0:T(8,128)S(1)} %copy-done, ...), custom_call_target="tpu_custom_call" | custom-call | flops 3000000000 | bytes 3000000 | tf_op jit(solution)/shard_map/inner_start/pallas_call | solution.py:519
  19.2 0.8 cross_start.1
  20.0 3.9 %collective-permute-done.5.refs_4_ = f32[128,256]{1,0:T(8,128)S(1)} collective-permute-done((f32[128,256]{1,0:T(8,128)S(1)}, f32[128,256]{1,0:T(8,128)S(1)}, u32[]{:S(2)}, u32[]{:S(2)}) %collective-permute-start.5) | collective-permute-done | bytes 131104 | tf_op jit(solution)/shard_map/ppermute | solution.py:469
  23.9 4.0 %cross_kernel.2 = (f32[768,128]{1,0:T(8,128)S(1)}, f32[96,256]{1,0:T(8,128)S(1)}, f32[96,256]{1,0:T(8,128)S(1)}, f32[96,128]{1,0:T(8,128)S(1)}, f32[32,512]{1,0:T(8,128)S(1)}) custom-call(f32[1024,128]{1,0:T(8,128)S(1)} %get-tuple-element.63.refs_0_, bf16[512,1024]{1,0:T(8,128)(2,1)S(1)} %get-tuple-element.64.refs_1_, ...), custom_call_target="tpu_custom_call" | custom-call | flops 4000000000 | bytes 4000000 | tf_op jit(solution)/shard_map/cross_kernel/pallas_call | solution.py:519
  28.2 4.8 %collective-permute-start.9 = (f32[96,256]{1,0:T(8,128)S(1)}, f32[96,256]{1,0:T(8,128)S(1)}, u32[]{:S(2)}, u32[]{:S(2)}) collective-permute-start(f32[96,256]{1,0:T(8,128)S(1)} %get-tuple-element.79), channel_id=1, source_target_pairs={{0,15},{1,0},{2,1},{3,2},{4,3},{5,4},{6,5},{7,6},{8,7},{9,8},{10,9... | collective-permute-start | bytes 294920 | tf_op jit(solution)/shard_map/ppermute | solution.py:469
  33.0 2.3 %inner_end.2.refs_2_.refs_4_ = f32[96,512]{1,0:T(8,128)S(1)} custom-call(bf16[512,1024]{1,0:T(8,128)(2,1)S(1)} %get-tuple-element.68.refs_0_.refs_2_, bf16[512,1024]{1,0:T(8,128)(2,1)S(1)} %get-tuple-element.69.refs_1_.refs_3_, f32[1024,128]{1,0:T(8,128)S(1)} %get-tuple-element.60.refs_2_, f32[1024,128]{1,0:T(8,128)S(1)} %get-tuple-element.70.refs_3_, ...), custom_call_target="tpu_custom_call" | custom-call | flops 3000000000 | bytes 3000000 | tf_op jit(solution)/shard_map/inner_end/pallas_call | solution.py:519
  36.2 2.4 %collective-permute-start.10 = (f32[96,256]{1,0:T(8,128)S(1)}, f32[96,256]{1,0:T(8,128)S(1)}, u32[]{:S(2)}, u32[]{:S(2)}) collective-permute-start(f32[96,256]{1,0:T(8,128)S(1)} %pad_maximum_fusion.2.refs_4_), channel_id=1, source_target_pairs={{0,16},{1,17},{2,18},{3,19},{4,20},{5,21},{6,22},{7,23},{8,24},{9,... | collective-permute-start | bytes 294920 | tf_op jit(solution)/shard_map/ppermute | solution.py:469
  38.6 1.8 %collective-permute-done.7.refs_2_ = f32[8,8,128]{2,1,0:T(8,128)S(1)} collective-permute-done((f32[8,8,128]{2,1,0:T(8,128)S(1)}, f32[8,8,128]{2,1,0:T(8,128)S(1)}, u32[]{:S(2)}, u32[]{:S(2)}) %collective-permute-start.7) | collective-permute-done | bytes 32800 | tf_op jit(solution)/shard_map/ppermute | solution.py:475
  40.4 2.6 %fluid_kernel.1 = (f32[128,512]{1,0:T(8,128)S(1)}, f32[16,8,128]{2,1,0:T(8,128)S(1)}) custom-call(f32[64,128]{1,0:T(8,128)S(1)} %get-tuple-element.55.refs_0_, f32[8,8,128]{2,1,0:T(8,128)S(1)} %get-tuple-element.75.refs_1_, f32[8,8,128]{2,1,0:T(8,128)S(1)} %collective-permute-done.7.refs_2_, s32[32,512]{1,0:T(8,128)S(1)} %get-tuple-element.77.refs_3_, ...), custom_call_target="tpu_custom_call" | custom-call | flops 3000000000 | bytes 3000000 | tf_op jit(solution)/shard_map/fluid_kernel/pallas_call | solution.py:519
  43.0 0.8 collective-permute-done.11.refs_9_
  43.8 0.7 copy-done.4
  44.5 0.7 middle_kernel.1
  45.2 1.2 %collective-permute-start.12 = (f32[96,256]{1,0:T(8,128)S(1)}, f32[96,256]{1,0:T(8,128)S(1)}, u32[]{:S(2)}, u32[]{:S(2)}) collective-permute-start(f32[96,256]{1,0:T(8,128)S(1)} %get-tuple-element.88), channel_id=1, source_target_pairs={{0,112},{1,113},{2,114},{3,115},{4,116},{5,117},{6,118},{7,119},{8... | collective-permute-start | bytes 294920 | tf_op jit(solution)/shard_map/ppermute | solution.py:469
  46.4 1.8 %collective-permute-start.13 = (f32[96,256]{1,0:T(8,128)S(1)}, f32[96,256]{1,0:T(8,128)S(1)}, u32[]{:S(2)}, u32[]{:S(2)}) collective-permute-start(f32[96,256]{1,0:T(8,128)S(1)} %get-tuple-element.89), channel_id=1, source_target_pairs={{0,16},{1,17},{2,18},{3,19},{4,20},{5,21},{6,22},{7,23},{8,24},{9,... | collective-permute-start | bytes 294920 | tf_op jit(solution)/shard_map/ppermute | solution.py:469
  48.2 2.3 %collective-permute-done.12.refs_5_ = f32[96,256]{1,0:T(8,128)S(1)} collective-permute-done((f32[96,256]{1,0:T(8,128)S(1)}, f32[96,256]{1,0:T(8,128)S(1)}, u32[]{:S(2)}, u32[]{:S(2)}) %collective-permute-start.12) | collective-permute-done | bytes 98336 | tf_op jit(solution)/shard_map/ppermute | solution.py:469
  50.5 4.6 %collective-permute-start.14 = (f32[96,256]{1,0:T(8,128)S(1)}, f32[96,256]{1,0:T(8,128)S(1)}, u32[]{:S(2)}, u32[]{:S(2)}) collective-permute-start(f32[96,256]{1,0:T(8,128)S(1)} %pad_maximum_fusion.4.refs_3_), channel_id=1, source_target_pairs={{0,15},{1,0},{2,1},{3,2},{4,3},{5,4},{6,5},{7,6},{8,7},{9,8},{10,9... | collective-permute-start | bytes 294920 | tf_op jit(solution)/shard_map/ppermute | solution.py:469
  55.2 2.5 %inner_again.1 = (f32[1024,128]{1,0:T(8,128)S(1)}, f32[1024,128]{1,0:T(8,128)S(1)}, f32[768,128]{1,0:T(8,128)S(1)}, f32[768,128]{1,0:T(8,128)S(1)}) custom-call(f32[128,512]{1,0:T(8,128)S(1)} %get-tuple-element.81.refs_0_, s32[5,1024]{1,0:T(8,128)S(1)} %copy-done, bf16[512,1024]{1,0:T(8,128)(2,1)S(1)} %get-tuple-element.68.refs_0_.refs_2_, ...), custom_call_target="tpu_custom_call" | custom-call | flops 3000000000 | bytes 3000000 | tf_op jit(solution)/shard_map/inner_again/pallas_call | solution.py:519
  58.2 3.7 %collective-permute-done.15.refs_4_ = f32[96,256]{1,0:T(8,128)S(1)} collective-permute-done((f32[96,256]{1,0:T(8,128)S(1)}, f32[96,256]{1,0:T(8,128)S(1)}, u32[]{:S(2)}, u32[]{:S(2)}) %collective-permute-start.15) | collective-permute-done | bytes 98336 | tf_op jit(solution)/shard_map/ppermute | solution.py:469
  61.9 4.5 %cross_kernel.3 = (f32[768,128]{1,0:T(8,128)S(1)}, f32[96,256]{1,0:T(8,128)S(1)}, f32[96,256]{1,0:T(8,128)S(1)}, f32[96,128]{1,0:T(8,128)S(1)}, f32[32,512]{1,0:T(8,128)}) custom-call(f32[1024,128]{1,0:T(8,128)S(1)} %cross_again.1.refs_0_, bf16[512,1024]{1,0:T(8,128)(2,1)S(1)} %get-tuple-element.64.refs_1_, f32[32,512]{1,0:T(8,128)S(1)} %get-tuple-element.90.refs_2_, ...), custom_call_target="tpu_custom_call" | custom-call | flops 4000000000 | bytes 4000000 | tf_op jit(solution)/shard_map/cross_kernel/pallas_call | solution.py:519
  66.4 1.1 %collective-permute-start.16 = (f32[96,256]{1,0:T(8,128)S(1)}, f32[96,256]{1,0:T(8,128)S(1)}, u32[]{:S(2)}, u32[]{:S(2)}) collective-permute-start(f32[96,256]{1,0:T(8,128)S(1)} %get-tuple-element.93), channel_id=1, source_target_pairs={{0,15},{1,0},{2,1},{3,2},{4,3},{5,4},{6,5},{7,6},{8,7},{9,8},{10,9... | collective-permute-start | bytes 294920 | tf_op jit(solution)/shard_map/ppermute | solution.py:469
  67.9 2.3 %inner_end.3.refs_4_ = f32[96,512]{1,0:T(8,128)S(1)} custom-call(bf16[512,1024]{1,0:T(8,128)(2,1)S(1)} %get-tuple-element.68.refs_0_.refs_2_, bf16[512,1024]{1,0:T(8,128)(2,1)S(1)} %get-tuple-element.69.refs_1_.refs_3_, f32[1024,128]{1,0:T(8,128)S(1)} %get-tuple-element.84.refs_5_.refs_2_, f32[1024,128]{1,0:T(8,128)S(1)} %get-tuple-element.85.refs_3_, ...), custom_call_target="tpu_custom_call" | custom-call | flops 3000000000 | bytes 3000000 | tf_op jit(solution)/shard_map/inner_end/pallas_call | solution.py:519
  70.8 3.7 %collective-permute-done.17.refs_7_ = f32[96,256]{1,0:T(8,128)S(1)} collective-permute-done((f32[96,256]{1,0:T(8,128)S(1)}, f32[96,256]{1,0:T(8,128)S(1)}, u32[]{:S(2)}, u32[]{:S(2)}) %collective-permute-start.17) | collective-permute-done | bytes 98336 | tf_op jit(solution)/shard_map/ppermute | solution.py:469
  74.6 4.7 %collective-permute-start.18 = (f32[96,256]{1,0:T(8,128)S(1)}, f32[96,256]{1,0:T(8,128)S(1)}, u32[]{:S(2)}, u32[]{:S(2)}) collective-permute-start(f32[96,256]{1,0:T(8,128)S(1)} %pad_maximum_fusion.6.refs_3_), channel_id=1, source_target_pairs={{0,16},{1,17},{2,18},{3,19},{4,20},{5,21},{6,22},{7,23},{8,24},{9,... | collective-permute-start | bytes 294920 | tf_op jit(solution)/shard_map/ppermute | solution.py:469
  80.1 0.7 owned_kernel.1
  80.9 3.6 %collective-permute-done.19.refs_9_ = f32[96,256]{1,0:T(8,128)S(1)} collective-permute-done((f32[96,256]{1,0:T(8,128)S(1)}, f32[96,256]{1,0:T(8,128)S(1)}, u32[]{:S(2)}, u32[]{:S(2)}) %collective-permute-start.19) | collective-permute-done | bytes 98336 | tf_op jit(solution)/shard_map/ppermute | solution.py:469
  84.5 1.5 %last_kernel.1 = (f32[3,16384]{1,0:T(4,128)}, f32[3,16384]{1,0:T(4,128)}) custom-call(f32[128,512]{1,0:T(8,128)S(1)} %get-tuple-element.81.refs_0_, f32[128,512]{1,0:T(8,128)S(1)} %get-tuple-element.82.refs_1_, f32[96,512]{1,0:T(8,128)S(1)} %get-tuple-element.83.refs_2_, f32[128,512]{1,0:T(8,128)S(1)} %get-tuple-element.80.refs_3_, ...), custom_call_target="tpu_custom_call" | custom-call | flops 1000000000 | bytes 1000000 | tf_op jit(solution)/shard_map/last_kernel/pallas_call | solution.py:519
  (55 shorter events, 5.2 us)
Async XLA Ops:
  2.2 7.4 %collective-permute-start.1 = (f32[128,256]{1,0:T(8,128)S(1)}, f32[128,256]{1,0:T(8,128)S(1)}, u32[]{:S(2)}, u32[]{:S(2)}) collective-permute-start(f32[128,256]{1,0:T(8,128)S(1)} %get-tuple-element.58), channel_id=1, source_target_pairs={{0,112},{1,113},{2,114},{3,115},{4,116},{5,117},{6,118},{7,119},{8... | collective-permute-start | bytes 393224 | tf_op jit(solution)/shard_map/ppermute | solution.py:469
  2.9 6.7 %collective-permute-start.2 = (f32[128,256]{1,0:T(8,128)S(1)}, f32[128,256]{1,0:T(8,128)S(1)}, u32[]{:S(2)}, u32[]{:S(2)}) collective-permute-start(f32[128,256]{1,0:T(8,128)S(1)} %get-tuple-element.59), channel_id=1, source_target_pairs={{0,16},{1,17},{2,18},{3,19},{4,20},{5,21},{6,22},{7,23},{8,24},{9,... | collective-permute-start | bytes 393224 | tf_op jit(solution)/shard_map/ppermute | solution.py:469
  8.2 10.2 %collective-permute-start = (f32[8,8,128]{2,1,0:T(8,128)S(1)}, f32[8,8,128]{2,1,0:T(8,128)S(1)}, u32[]{:S(2)}, u32[]{:S(2)}) collective-permute-start(f32[8,8,128]{2,1,0:T(8,128)S(1)} %get-tuple-element.57), channel_id=1, source_target_pairs={{0,1},{1,0},{2,3},{3,2},{4,5},{5,4},{6,7},{7,6},{8,9},{9,8},{10,11... | collective-permute-start | bytes 98312 | tf_op jit(solution)/shard_map/ppermute | solution.py:475
  9.7 10.3 %collective-permute-start.4 = (f32[128,256]{1,0:T(8,128)S(1)}, f32[128,256]{1,0:T(8,128)S(1)}, u32[]{:S(2)}, u32[]{:S(2)}) collective-permute-start(f32[128,256]{1,0:T(8,128)S(1)} %pad_maximum_fusion.refs_2_), channel_id=1, source_target_pairs={{0,15},{1,0},{2,1},{3,2},{4,3},{5,4},{6,5},{7,6},{8,7},{9,8},{10,9... | collective-permute-start | bytes 393224 | tf_op jit(solution)/shard_map/ppermute | solution.py:469
  15.1 0.8 copy-start
  15.1 8.8 %collective-permute-start.5 = (f32[128,256]{1,0:T(8,128)S(1)}, f32[128,256]{1,0:T(8,128)S(1)}, u32[]{:S(2)}, u32[]{:S(2)}) collective-permute-start(f32[128,256]{1,0:T(8,128)S(1)} %pad_maximum_fusion.1.refs_3_), channel_id=1, source_target_pairs={{0,1},{1,2},{2,3},{3,4},{4,5},{5,6},{6,7},{7,8},{8,9},{9,10},{10,1... | collective-permute-start | bytes 393224 | tf_op jit(solution)/shard_map/ppermute | solution.py:469
  18.4 0.8 copy-start.1
  18.4 9.5 %collective-permute-start.3 = (f32[8,8,128]{2,1,0:T(8,128)S(1)}, f32[8,8,128]{2,1,0:T(8,128)S(1)}, u32[]{:S(2)}, u32[]{:S(2)}) collective-permute-start(f32[8,8,128]{2,1,0:T(8,128)S(1)} %get-tuple-element.62.refs_2_), channel_id=1, source_target_pairs={{0,2},{1,3},{2,0},{3,1},{4,6},{5,7},{6,4},{7,5},{8,10},{9,11},{10,... | collective-permute-start | bytes 98312 | tf_op jit(solution)/shard_map/ppermute | solution.py:475
  28.0 7.8 %collective-permute-start.6 = (f32[8,8,128]{2,1,0:T(8,128)S(1)}, f32[8,8,128]{2,1,0:T(8,128)S(1)}, u32[]{:S(2)}, u32[]{:S(2)}) collective-permute-start(f32[8,8,128]{2,1,0:T(8,128)S(1)} %get-tuple-element.67.refs_7_.refs_2_), channel_id=1, source_target_pairs={{0,4},{1,5},{2,6},{3,7},{4,0},{5,1},{6,2},{7,3},{8,12},{9,13},{10,... | collective-permute-start | bytes 98312 | tf_op jit(solution)/shard_map/ppermute | solution.py:475
  28.1 8.0 %collective-permute-start.8 = (f32[96,256]{1,0:T(8,128)S(1)}, f32[96,256]{1,0:T(8,128)S(1)}, u32[]{:S(2)}, u32[]{:S(2)}) collective-permute-start(f32[96,256]{1,0:T(8,128)S(1)} %get-tuple-element.78), channel_id=1, source_target_pairs={{0,1},{1,2},{2,3},{3,4},{4,5},{5,6},{6,7},{7,8},{8,9},{9,10},{10,1... | collective-permute-start | bytes 294920 | tf_op jit(solution)/shard_map/ppermute | solution.py:469
  28.2 7.9 %collective-permute-start.9 = (f32[96,256]{1,0:T(8,128)S(1)}, f32[96,256]{1,0:T(8,128)S(1)}, u32[]{:S(2)}, u32[]{:S(2)}) collective-permute-start(f32[96,256]{1,0:T(8,128)S(1)} %get-tuple-element.79), channel_id=1, source_target_pairs={{0,15},{1,0},{2,1},{3,2},{4,3},{5,4},{6,5},{7,6},{8,7},{9,8},{10,9... | collective-permute-start | bytes 294920 | tf_op jit(solution)/shard_map/ppermute | solution.py:469
  35.8 4.5 %collective-permute-start.7 = (f32[8,8,128]{2,1,0:T(8,128)S(1)}, f32[8,8,128]{2,1,0:T(8,128)S(1)}, u32[]{:S(2)}, u32[]{:S(2)}) collective-permute-start(f32[8,8,128]{2,1,0:T(8,128)S(1)} %get-tuple-element.76.refs_7_.refs_2_), channel_id=1, source_target_pairs={{0,8},{1,9},{2,10},{3,11},{4,12},{5,13},{6,14},{7,15},{8,0},{9,1},... | collective-permute-start | bytes 98312 | tf_op jit(solution)/shard_map/ppermute | solution.py:475
  36.2 6.8 %collective-permute-start.10 = (f32[96,256]{1,0:T(8,128)S(1)}, f32[96,256]{1,0:T(8,128)S(1)}, u32[]{:S(2)}, u32[]{:S(2)}) collective-permute-start(f32[96,256]{1,0:T(8,128)S(1)} %pad_maximum_fusion.2.refs_4_), channel_id=1, source_target_pairs={{0,16},{1,17},{2,18},{3,19},{4,20},{5,21},{6,22},{7,23},{8,24},{9,... | collective-permute-start | bytes 294920 | tf_op jit(solution)/shard_map/ppermute | solution.py:469
  38.6 5.3 %collective-permute-start.11 = (f32[96,256]{1,0:T(8,128)S(1)}, f32[96,256]{1,0:T(8,128)S(1)}, u32[]{:S(2)}, u32[]{:S(2)}) collective-permute-start(f32[96,256]{1,0:T(8,128)S(1)} %pad_maximum_fusion.3.refs_5_), channel_id=1, source_target_pairs={{0,112},{1,113},{2,114},{3,115},{4,116},{5,117},{6,118},{7,119},{8... | collective-permute-start | bytes 294920 | tf_op jit(solution)/shard_map/ppermute | solution.py:469
  43.8 0.7 copy-start.4
  45.2 5.3 %collective-permute-start.12 = (f32[96,256]{1,0:T(8,128)S(1)}, f32[96,256]{1,0:T(8,128)S(1)}, u32[]{:S(2)}, u32[]{:S(2)}) collective-permute-start(f32[96,256]{1,0:T(8,128)S(1)} %get-tuple-element.88), channel_id=1, source_target_pairs={{0,112},{1,113},{2,114},{3,115},{4,116},{5,117},{6,118},{7,119},{8... | collective-permute-start | bytes 294920 | tf_op jit(solution)/shard_map/ppermute | solution.py:469
  46.4 4.1 %collective-permute-start.13 = (f32[96,256]{1,0:T(8,128)S(1)}, f32[96,256]{1,0:T(8,128)S(1)}, u32[]{:S(2)}, u32[]{:S(2)}) collective-permute-start(f32[96,256]{1,0:T(8,128)S(1)} %get-tuple-element.89), channel_id=1, source_target_pairs={{0,16},{1,17},{2,18},{3,19},{4,20},{5,21},{6,22},{7,23},{8,24},{9,... | collective-permute-start | bytes 294920 | tf_op jit(solution)/shard_map/ppermute | solution.py:469
  50.5 7.7 %collective-permute-start.14 = (f32[96,256]{1,0:T(8,128)S(1)}, f32[96,256]{1,0:T(8,128)S(1)}, u32[]{:S(2)}, u32[]{:S(2)}) collective-permute-start(f32[96,256]{1,0:T(8,128)S(1)} %pad_maximum_fusion.4.refs_3_), channel_id=1, source_target_pairs={{0,15},{1,0},{2,1},{3,2},{4,3},{5,4},{6,5},{7,6},{8,7},{9,8},{10,9... | collective-permute-start | bytes 294920 | tf_op jit(solution)/shard_map/ppermute | solution.py:469
  55.1 6.9 %collective-permute-start.15 = (f32[96,256]{1,0:T(8,128)S(1)}, f32[96,256]{1,0:T(8,128)S(1)}, u32[]{:S(2)}, u32[]{:S(2)}) collective-permute-start(f32[96,256]{1,0:T(8,128)S(1)} %pad_maximum_fusion.5.refs_4_), channel_id=1, source_target_pairs={{0,1},{1,2},{2,3},{3,4},{4,5},{5,6},{6,7},{7,8},{8,9},{9,10},{10,1... | collective-permute-start | bytes 294920 | tf_op jit(solution)/shard_map/ppermute | solution.py:469
  66.4 4.4 %collective-permute-start.16 = (f32[96,256]{1,0:T(8,128)S(1)}, f32[96,256]{1,0:T(8,128)S(1)}, u32[]{:S(2)}, u32[]{:S(2)}) collective-permute-start(f32[96,256]{1,0:T(8,128)S(1)} %get-tuple-element.93), channel_id=1, source_target_pairs={{0,15},{1,0},{2,1},{3,2},{4,3},{5,4},{6,5},{7,6},{8,7},{9,8},{10,9... | collective-permute-start | bytes 294920 | tf_op jit(solution)/shard_map/ppermute | solution.py:469
  67.5 7.0 %collective-permute-start.17 = (f32[96,256]{1,0:T(8,128)S(1)}, f32[96,256]{1,0:T(8,128)S(1)}, u32[]{:S(2)}, u32[]{:S(2)}) collective-permute-start(f32[96,256]{1,0:T(8,128)S(1)} %get-tuple-element.94), channel_id=1, source_target_pairs={{0,1},{1,2},{2,3},{3,4},{4,5},{5,6},{6,7},{7,8},{8,9},{9,10},{10,1... | collective-permute-start | bytes 294920 | tf_op jit(solution)/shard_map/ppermute | solution.py:469
  74.6 6.3 %collective-permute-start.18 = (f32[96,256]{1,0:T(8,128)S(1)}, f32[96,256]{1,0:T(8,128)S(1)}, u32[]{:S(2)}, u32[]{:S(2)}) collective-permute-start(f32[96,256]{1,0:T(8,128)S(1)} %pad_maximum_fusion.6.refs_3_), channel_id=1, source_target_pairs={{0,16},{1,17},{2,18},{3,19},{4,20},{5,21},{6,22},{7,23},{8,24},{9,... | collective-permute-start | bytes 294920 | tf_op jit(solution)/shard_map/ppermute | solution.py:469
  79.3 5.3 %collective-permute-start.19 = (f32[96,256]{1,0:T(8,128)S(1)}, f32[96,256]{1,0:T(8,128)S(1)}, u32[]{:S(2)}, u32[]{:S(2)}) collective-permute-start(f32[96,256]{1,0:T(8,128)S(1)} %pad_maximum_fusion.7.refs_4_), channel_id=1, source_target_pairs={{0,112},{1,113},{2,114},{3,115},{4,116},{5,117},{6,118},{7,119},{8... | collective-permute-start | bytes 294920 | tf_op jit(solution)/shard_map/ppermute | solution.py:469
  79.3 0.8 copy-start.2
  79.3 0.8 copy-start.3

commit v3 on v2

--- a/solution.py
+++ b/solution.py
@@ -70,6 +70,14 @@
     return lax.broadcasted_iota(jnp.int32, shape, 1) < GHOSTS
 
 
+def by_parity(axis, even_first, even_second):
+    even = lax.axis_index(axis) % 2 == 0
+    return (
+        jnp.where(even, even_first, even_second),
+        jnp.where(even, even_second, even_first),
+    )
+
+
 def to_table(square):
     turned = square.T
     return jnp.concatenate([turned[k * SLOTS : (k + 1) * SLOTS] for k in range(GROUP)], axis=1)
@@ -101,16 +109,14 @@
     return total
 
 
-def send_pieces(table, rows, send_ref, first_ref, second_ref):
-    parts = jnp.concatenate(split(table[:rows], 3), axis=0)
+def send_pieces(table, rows, hot, lead, trail):
+    pieces = gather(jnp.concatenate(split(table[:rows], 3), axis=0), hot[...], rows)
     half = CLUSTERS // 2
-    for k, out in enumerate((first_ref, second_ref)):
-        hot = one_hot(cluster_column(send_ref[:, k * half : (k + 1) * half]), CLUSTERS)
-        out[...] = gather(parts, hot, rows)
+    lead[...], trail[...] = by_parity("gy", pieces[:, half:], pieces[:, :half])
 
 
 def prepare(
-    positions_far, radius_far, mask_far, send_far, table_out, state_out, first, second,
+    positions_far, radius_far, mask_far, send_far, table_out, state_out, hot, lead, trail,
     positions, radius, mask, send, stage, arrived,
 ):
     fetch(
@@ -125,7 +131,8 @@
     for c in range(3):
         state_out[c * SLOTS : (c + 1) * SLOTS] = parts[c]
     state_out[3 * SLOTS :] = weights
-    send_pieces(table, 4 * SLOTS, send, first, second)
+    hot[...] = one_hot(cluster_column(send[...]), CLUSTERS)
+    send_pieces(table, 4 * SLOTS, hot, lead, trail)
 
 
 def contacts(leading, partner, on_leading, on_partner, begin, end):
@@ -212,17 +219,17 @@
     fill_slots(parts, hot_b, None, partner)
     on_partner[...] = jnp.zeros_like(on_partner)
     contacts(leading, partner, on_leading, on_partner, 0, INNER_SPLIT)
-
-
-def inner_end(
-    hot_a, hot_b, leading, partner, on_leading_first, on_partner_first, force, on_leading, on_partner
-):
+    for c in range(3):
+        later = slice((c * SLOTS + INNER_SPLIT) * 8, (c + 1) * SLOTS * 8)
+        on_leading[later, :] = jnp.zeros(((SLOTS - INNER_SPLIT) * 8, LANES), f32)
+
+
+def inner_rest(leading, partner, on_leading_first, on_partner_first, on_leading, on_partner):
     for c in range(3):
         done = slice(c * SLOTS * 8, (c * SLOTS + INNER_SPLIT) * 8)
         on_leading[done, :] = on_leading_first[done, :]
     on_partner[...] = on_partner_first[...]
     contacts(leading, partner, on_leading, on_partner, INNER_SPLIT, SLOTS)
-    force[...] = scatter(on_leading, hot_a) - scatter(on_partner, hot_b)
 
 
 def cross_start(table, pairs, hot_a, hot_b, leading):
@@ -235,8 +242,10 @@
     fill_slots(table_parts(table), hot_a, pairs, leading)
 
 
-def cross_end(on_leading, hot_a, force):
-    force[...] = scatter(on_leading, hot_a)
+def scatter_kernel(on_leading, on_partner, on_crossing, hot_a, hot_b, hot_c, force):
+    force[...] = (
+        scatter(on_leading, hot_a) - scatter(on_partner, hot_b) + scatter(on_crossing, hot_c)
+    )
 
 
 def present_tile(low, high):
@@ -250,32 +259,74 @@
     return jnp.where(lower_half((1, LANES)), flags[0], flags[1]) > 0
 
 
-def cross_kernel(
-    leading, hot_b, reach, below, above, from_next, from_last,
-    on_leading, up, down, keep, reach_out, partner, on_partner,
-):
-    rows = below.shape[0]
-    low = lower_half((rows, LANES))
-    tiles = [
-        below[:, :LANES],
-        jnp.where(low, above[:, LANES:], below[:, LANES:]),
-        above[:, :LANES],
-        jnp.where(low, from_last[:, LANES:], from_next[:, :LANES]),
-    ]
-    for k in range(4):
-        there = present_tile(GHOST_ORDER[2 * k], GHOST_ORDER[2 * k + 1])
-        placed = jnp.where(there, tiles[k][: 3 * SLOTS], FAR)
-        size = reach[:, k * LANES : (k + 1) * LANES] if rows == 3 * SLOTS else tiles[k][3 * SLOTS :]
-        reach_out[:, k * LANES : (k + 1) * LANES] = size
-        tiles[k] = jnp.concatenate([placed, size], axis=0)
-    ghosts = jnp.concatenate(tiles, axis=1)
+def pass_ghosts(lead, trail, got_lead, got_trail, lead_out, trail_out, side):
+    low = lower_half((lead.shape[0], LANES))
+    own_second, own_first = by_parity("gy", lead[...], trail[...])
+    from_last, from_next = by_parity("gy", got_lead[...], got_trail[...])
+    minus = [jnp.where(low, from_next[:, :LANES], from_last[:, :LANES]), own_first[:, LANES:]]
+    plus = [jnp.where(low, from_next[:, LANES:], from_last[:, LANES:]), own_second[:, :LANES]]
+    for k in range(2):
+        span = slice(k * LANES, (k + 1) * LANES)
+        lead_out[:, span], trail_out[:, span] = by_parity("gx", plus[k], minus[k])
+    side[...] = jnp.where(low, from_last[:, LANES:], from_next[:, :LANES])
+
+
+def cross_contacts(ghosts, leading, hot_b, on_leading, lead, trail, side_out, partner, on_partner):
     fill_slots(jnp.concatenate(split(ghosts, 3), axis=0), hot_b, None, partner)
     on_partner[...] = jnp.zeros_like(on_partner)
     contacts(leading, partner, on_leading, on_partner, 0, SLOTS)
     back = scatter(on_partner, hot_b)
-    up[...] = back[:, : 2 * LANES]
-    down[...] = back[:, LANES : 3 * LANES]
-    keep[...] = back[:, 3 * LANES :]
+    lead[...], trail[...] = by_parity("gx", back[:, : 2 * LANES], back[:, LANES : 3 * LANES])
+    side_out[...] = back[:, 3 * LANES :]
+
+
+def ghost_places(got_lead, got_trail, side):
+    from_last, from_next = by_parity("gx", got_lead[...], got_trail[...])
+    low = lower_half(side.shape)
+    tiles = [
+        from_next[:, :LANES],
+        jnp.where(low, from_last[:, LANES:], from_next[:, LANES:]),
+        from_last[:, :LANES],
+        side[...],
+    ]
+    placed = [
+        jnp.where(
+            present_tile(GHOST_ORDER[2 * k], GHOST_ORDER[2 * k + 1]), tiles[k][: 3 * SLOTS], FAR
+        )
+        for k in range(4)
+    ]
+    return tiles, jnp.concatenate(placed, axis=1)
+
+
+def cross_kernel(
+    leading, hot_b, got_lead, got_trail, side,
+    on_leading, lead, trail, side_out, reach_out, partner, on_partner,
+):
+    tiles, placed = ghost_places(got_lead, got_trail, side)
+    reach = jnp.concatenate([tile[3 * SLOTS :] for tile in tiles], axis=1)
+    reach_out[...] = reach
+    ghosts = jnp.concatenate([placed, reach], axis=0)
+    cross_contacts(ghosts, leading, hot_b, on_leading, lead, trail, side_out, partner, on_partner)
+
+
+def cross_kernel_again(
+    leading, hot_b, got_lead, got_trail, side, reach,
+    on_leading, lead, trail, side_out, partner, on_partner,
+):
+    _, placed = ghost_places(got_lead, got_trail, side)
+    ghosts = jnp.concatenate([placed, reach[...]], axis=0)
+    cross_contacts(ghosts, leading, hot_b, on_leading, lead, trail, side_out, partner, on_partner)
+
+
+def pass_forces(got_lead, got_trail, side, lead_out, trail_out, middle):
+    low = lower_half((3 * SLOTS, LANES))
+    from_last, from_next = by_parity("gx", got_lead[...], got_trail[...])
+    up = [jnp.where(low, from_last[:, :LANES], side[...]), from_next[:, LANES:]]
+    down = [from_last[:, :LANES], jnp.where(low, side[...], from_next[:, LANES:])]
+    for k in range(2):
+        span = slice(k * LANES, (k + 1) * LANES)
+        lead_out[:, span], trail_out[:, span] = by_parity("gy", up[k], down[k])
+    middle[...] = jnp.where(low, from_next[:, :LANES], from_last[:, LANES:])
 
 
 def fetch(pairs, arrived):
@@ -312,9 +363,9 @@
 
 
 def deposit_kernel(
-    velocity_far, radius_far, mask_far, cell_far, fluid_far, pressure_far,
-    velocity_out, cell_out, totals_out, stay, away,
-    velocity, radius, mask, cell, fluid, pressure, stage, arrived,
+    velocity_far, radius_far, mask_far, cell_far, fluid_far, pressure_far, inner_far, cross_far,
+    velocity_out, cell_out, totals_out, stay, away, fluid, pressure, inner, cross,
+    velocity, radius, mask, cell, stage, arrived,
 ):
     fetch(
         (
@@ -324,6 +375,8 @@
             (cell_far, cell),
             (fluid_far, fluid),
             (pressure_far, pressure),
+            (inner_far, inner),
+            (cross_far, cross),
         ),
         arrived,
     )
@@ -398,19 +451,19 @@
         void_out[source : source + 1, :] = void_here
 
 
-def advance(state, velocity, reach, at_grain, inner, cross, above, below, from_last, from_next, send):
+def advance(state, velocity, reach, at_grain, force, middle, got_lead, got_trail, hot):
     low = lower_half((3 * SLOTS, LANES))
+    from_last, from_next = by_parity("gy", got_lead[...], got_trail[...])
     tiles = [
         from_last[:, :LANES],
-        jnp.where(low, from_last[:, LANES:], below[:, LANES:]),
-        jnp.where(low, above[:, :LANES], from_next[:, :LANES]),
+        jnp.where(low, from_last[:, LANES:], middle[...]),
+        jnp.where(low, middle[...], from_next[:, :LANES]),
         from_next[:, LANES:],
     ]
     tiles = [jnp.where(present_tile(2 * k, 2 * k + 1), tiles[k], 0.0) for k in range(4)]
     returned = jnp.concatenate(tiles, axis=1)
-    hot = one_hot(cluster_column(send[...]), CLUSTERS)
-    added = dot_lanes(jnp.concatenate(split(returned, 2), axis=0), hot)
-    contact = spring * (inner[...] + cross[...] - (added[: 3 * SLOTS] + added[3 * SLOTS :]))
+    added = dot_lanes(jnp.concatenate(split(returned, 2), axis=0), hot[...])
+    contact = spring * (force[...] - (added[: 3 * SLOTS] + added[3 * SLOTS :]))
     weights = state[3 * SLOTS :, :]
     sphere = (4.0 * math.pi / 3.0) * reach * reach * reach
     masses = grain_density * sphere
@@ -430,12 +483,12 @@
 
 
 def middle_kernel(
-    table, state, velocity, at_grain, inner, cross, above, below, from_last, from_next, send,
-    table_out, state_out, velocity_out, first, second,
+    table, state, velocity, at_grain, force, middle, got_lead, got_trail, hot,
+    table_out, state_out, velocity_out, lead, trail,
 ):
     reach = table[3 * SLOTS :, :]
     places, speeds, weights = advance(
-        state, velocity, reach, at_grain, inner, cross, above, below, from_last, from_next, send
+        state, velocity, reach, at_grain, force, middle, got_lead, got_trail, hot
     )
     real = weights > 0.5
     moved = jnp.concatenate([jnp.where(real, place, FAR) for place in places] + [reach], axis=0)
@@ -444,28 +497,32 @@
         state_out[c * SLOTS : (c + 1) * SLOTS] = places[c]
         velocity_out[c * SLOTS : (c + 1) * SLOTS] = speeds[c]
     state_out[3 * SLOTS :] = weights
-    send_pieces(moved, 3 * SLOTS, send, first, second)
+    send_pieces(moved, 3 * SLOTS, hot, lead, trail)
 
 
 def last_kernel(
-    table, state, velocity, at_grain, inner, cross, above, below, from_last, from_next, send,
+    table, state, velocity, at_grain, force, middle, got_lead, got_trail, hot,
     positions_out, velocity_out, stage,
 ):
     places, speeds, _ = advance(
-        state, velocity, table[3 * SLOTS :, :], at_grain, inner, cross, above, below, from_last,
-        from_next, send,
+        state, velocity, table[3 * SLOTS :, :], at_grain, force, middle, got_lead, got_trail, hot
     )
     store_components(positions_out, stage, jnp.concatenate(places, axis=0))
     store_components(velocity_out, stage, jnp.concatenate(speeds, axis=0))
 
 
-def shift(array, step_x, step_y):
+def snake(array, axis, sign):
     size_x, size_y = lax.axis_size("gx"), lax.axis_size("gy")
     moves = []
     for x in range(size_x):
         for y in range(size_y):
-            target = (x + step_x) % size_x * size_y + (y + step_y) % size_y
-            moves.append((x * size_y + y, target))
+            if axis == "gx":
+                target = (x + (sign if y % 2 == 0 else -sign), y)
+                target = target if 0 <= target[0] < size_x else (x, y ^ 1)
+            else:
+                target = (x, y + (sign if x % 2 == 0 else -sign))
+                target = target if 0 <= target[1] < size_y else (x ^ 1, y)
+            moves.append((x * size_y + y, target[0] * size_y + target[1]))
     return lax.ppermute(array, ("gx", "gy"), moves)
 
 
@@ -473,26 +530,6 @@
     size_x, size_y = lax.axis_size("gx"), lax.axis_size("gy")
     moves = [(x * size_y + y, x * size_y + (y ^ bit)) for x in range(size_x) for y in range(size_y)]
     return lax.ppermute(array, ("gx", "gy"), moves)
-
-
-def halves(low_from, high_from):
-    return jnp.where(lower_half(low_from.shape), low_from, high_from)
-
-
-def pass_ghosts(first, second, from_next, from_last):
-    minus = jnp.concatenate(
-        [halves(from_next[:, :LANES], from_last[:, :LANES]), first[:, LANES:]], axis=1
-    )
-    plus = jnp.concatenate(
-        [halves(from_next[:, LANES:], from_last[:, LANES:]), second[:, :LANES]], axis=1
-    )
-    return minus, plus
-
-
-def pass_forces(above, below, keep):
-    first = jnp.concatenate([halves(below[:, :LANES], keep), above[:, LANES:]], axis=1)
-    second = jnp.concatenate([below[:, :LANES], halves(keep, above[:, LANES:])], axis=1)
-    return first, second
 
 
 def table_shape(rows, columns=CLUSTERS):
@@ -549,21 +586,24 @@
 
     full, wide = table_shape(4 * SLOTS), table_shape(4 * SLOTS, 2 * LANES)
     narrow, single = table_shape(3 * SLOTS, 2 * LANES), table_shape(3 * SLOTS, LANES)
-    three, reach = table_shape(3 * SLOTS), table_shape(SLOTS)
+    three, full_tile = table_shape(3 * SLOTS), table_shape(4 * SLOTS, LANES)
 
     def near(array):
         return pltpu.VMEM(array.shape, array.dtype)
 
+    def like(array):
+        return jax.ShapeDtypeStruct(array.shape, array.dtype)
+
     operands = (positions, radius, mask, send)
-    table, state, first, second = call(
+    table, state, hot, lead, trail = call(
         prepare,
-        (full, full, wide, wide),
+        (full, full, jax.ShapeDtypeStruct((CLUSTERS, CLUSTERS), bf16), wide, wide),
         operands,
         [near(array) for array in operands] + [STAGE, pltpu.SemaphoreType.DMA((4,))],
         far=True,
     )
-    operands = (velocity, radius, mask, cell, fluid_velocity, pressure_grad)
-    moving, cells, totals, stay, away = call(
+    operands = (velocity, radius, mask, cell, fluid_velocity, pressure_grad, inner_pairs, cross_pairs)
+    moving, cells, totals, stay, away, fluid, pressure, inner_pairs, cross_pairs = call(
         deposit_kernel,
         (
             three,
@@ -571,94 +611,107 @@
             table_shape(64, LANES),
             PARCELS,
             PARCELS,
+            *[like(array) for array in operands[4:]],
         ),
         operands,
-        [near(array) for array in operands] + [STAGE, pltpu.SemaphoreType.DMA((6,))],
+        [near(array) for array in operands[:4]] + [STAGE, pltpu.SemaphoreType.DMA((8,))],
         3,
         far=True,
         after=(table,),
     )
     got = swap(away, 1)
 
-    ghost_reach = jnp.zeros((SLOTS, CLUSTERS), f32)
+    cross_scratch = [pltpu.VMEM(SLOT_ROWS.shape, f32), FORCE_SCRATCH]
     for substep in range(2):
-        from_next, from_last = shift(first, -1, 0), shift(second, 1, 0)
-        minus, plus = pass_ghosts(first, second, from_next, from_last)
-        below, above = shift(minus, 0, -1), shift(plus, 0, 1)
-        if substep == 0:
+        first = substep == 0
+        got_lead, got_trail = snake(lead, "gx", 1), snake(trail, "gx", -1)
+        if not first:
+            rows = call(
+                inner_again,
+                (SLOT_ROWS, SLOT_ROWS, FORCE_ROWS, FORCE_ROWS),
+                (table, inner_pairs, hot_a, hot_b),
+                cost=3,
+            )
+        lead, trail, side = call(
+            pass_ghosts,
+            (wide, wide, full_tile) if first else (narrow, narrow, single),
+            (lead, trail, got_lead, got_trail),
+            after=(away,) if first else (rows[3],),
+        )
+        got_lead, got_trail = snake(lead, "gy", 1), snake(trail, "gy", -1)
+        if first:
+            stay, away = call(relay(1), (PARCELS, PARCELS), (stay, got), after=(lead, trail))
+            got = swap(away, 2)
             hot_a, hot_b, *rows = call(
                 inner_start,
                 (HOT, HOT, SLOT_ROWS, SLOT_ROWS, FORCE_ROWS, FORCE_ROWS),
                 (table, inner_pairs),
                 cost=3,
-                after=(minus, plus),
-            )
-            stay, away = call(relay(1), (PARCELS, PARCELS), (stay, got), after=(rows[0],))
-            got = swap(away, 2)
+                after=(away,),
+            )
             hot_c, hot_d, leading = call(
-                cross_start, (HOT, HOT, SLOT_ROWS), (table, cross_pairs), after=(away,)
+                cross_start, (HOT, HOT, SLOT_ROWS), (table, cross_pairs), after=(rows[3],)
+            )
+            stay, away = call(relay(2), (PARCELS, PARCELS), (stay, got), after=(leading,))
+            got = swap(away, 4)
+            on_crossing, lead, trail, side, reach = call(
+                cross_kernel,
+                (FORCE_ROWS, narrow, narrow, single, table_shape(SLOTS)),
+                (leading, hot_d, got_lead, got_trail, side),
+                cross_scratch,
+                4,
+                after=(away,),
             )
         else:
-            rows = call(
-                inner_again,
-                (SLOT_ROWS, SLOT_ROWS, FORCE_ROWS, FORCE_ROWS),
-                (table, inner_pairs, hot_a, hot_b),
-                cost=3,
-            )
             leading = call(
-                cross_again, SLOT_ROWS, (table, cross_pairs, hot_c), after=(minus, plus, rows[0])
-            )
-        on_leading, up, down, keep, ghost_reach = call(
-            cross_kernel,
-            (FORCE_ROWS, narrow, narrow, single, reach),
-            (leading, hot_d, ghost_reach, below, above, from_next, from_last),
-            [pltpu.VMEM(SLOT_ROWS.shape, f32), FORCE_SCRATCH],
-            4,
+                cross_again, SLOT_ROWS, (table, cross_pairs, hot_c), after=(lead, trail)
+            )
+            sums = call(inner_rest, (FORCE_ROWS, FORCE_ROWS), rows, cost=2, after=(leading,))
+            on_crossing, lead, trail, side = call(
+                cross_kernel_again,
+                (FORCE_ROWS, narrow, narrow, single),
+                (leading, hot_d, got_lead, got_trail, side, reach),
+                cross_scratch,
+                4,
+                after=(sums[1],),
+            )
+        got_lead, got_trail = snake(lead, "gy", 1), snake(trail, "gy", -1)
+        if first:
+            stay, away = call(relay(4), (PARCELS, PARCELS), (stay, got), after=(side,))
+            got = swap(away, 8)
+            sums = call(inner_rest, (FORCE_ROWS, FORCE_ROWS), rows, cost=2, after=(away,))
+        force = call(
+            scatter_kernel, three, (*sums, on_crossing, hot_a, hot_b, hot_c), cost=2, after=(side,)
         )
-        below, above = shift(up, 0, 1), shift(down, 0, -1)
-        if substep == 0:
-            stay, away = call(relay(2), (PARCELS, PARCELS), (stay, got), after=(keep,))
-            got = swap(away, 4)
-        inner = call(
-            inner_end,
-            three,
-            (hot_a, hot_b, *rows),
-            [FORCE_SCRATCH, FORCE_SCRATCH],
-            3,
-            after=(keep, away),
+        lead, trail, middle = call(
+            pass_forces, (narrow, narrow, single), (got_lead, got_trail, side), after=(force,)
         )
-        cross = call(cross_end, three, (on_leading, hot_c), after=(away,))
-        if substep == 0:
-            stay, away = call(relay(4), (PARCELS, PARCELS), (stay, got), after=(inner, cross))
-            got = swap(away, 8)
-        first, second = pass_forces(above, below, keep)
-        from_last, from_next = shift(first, 1, 0), shift(second, -1, 0)
-        if substep == 0:
+        got_lead, got_trail = snake(lead, "gx", 1), snake(trail, "gx", -1)
+        if first:
             at_grain, parcels = call(
                 fluid_kernel,
                 (full, jax.ShapeDtypeStruct((16, 8, LANES), f32)),
                 (totals, stay, got, cells),
                 (),
                 3,
-                after=(first, second),
+                after=(lead, trail),
             )
         else:
             fluid_out, void_out = call(
                 owned_kernel,
-                (jax.ShapeDtypeStruct(fluid_velocity.shape, f32), table_shape(16, LANES)),
-                (parcels, fluid_velocity, pressure_grad),
-                after=(first, second),
-            )
-        operands = (
-            table, state, moving, at_grain, inner, cross, above, below, from_last, from_next, send
-        )
-        if substep == 0:
-            table, state, moving, first, second = call(
+                (like(fluid_velocity), table_shape(16, LANES)),
+                (parcels, fluid, pressure),
+                after=(lead, trail),
+            )
+        operands = (table, state, moving, at_grain, force, middle, got_lead, got_trail, hot)
+        if first:
+            table, state, moving, lead, trail = call(
                 middle_kernel, (full, full, three, narrow, narrow), operands
             )
         else:
-            shape = jax.ShapeDtypeStruct(positions.shape, f32)
-            positions, velocity = call(last_kernel, (shape, shape), operands, [STAGE])
+            positions, velocity = call(
+                last_kernel, (like(positions), like(positions)), operands, [STAGE]
+            )
     return positions, velocity, fluid_out, void_out.reshape(-1)
 
 

time: 86.4 us -> 69.2 us (0.80)
  the two profiles are of different devices: /device:TPU:7 before, /device:TPU:24 now
where the time goes in v3:
time: 69.2 us; the launch traced here: 69 us
  Pallas kernels  30.1 us (43%)
  starting transfers between devices  19.3 us (28%)
  waiting for transfers between devices  18.8 us (27%)
  between operations  0.83 us (1%)
    pallas_call x23, Pallas kernels, call(): pl.pallas_call(body, out_shape=out_shape, in_specs=[pl.BlockSpec(memory_s...  30.1 us
    ppermute x16, waiting for transfers between devices, snake(): return lax.ppermute(array, ('gx', 'gy'), moves)  17.3 us
    ppermute x16, starting transfers between devices, snake(): return lax.ppermute(array, ('gx', 'gy'), moves)  10.9 us
    ppermute x4, starting transfers between devices, swap(): return lax.ppermute(array, ('gx', 'gy'), moves)  8.47 us
    ppermute x4, waiting for transfers between devices, swap(): return lax.ppermute(array, ('gx', 'gy'), moves)  1.46 us
  transfers between devices with their start and end apart: 20, of which 11 were waited for; matrix products, arithmetic and copies ran while one was open for 0% of the time, Pallas kernels for 32%

profile of v3, /device:TPU:24, one launch (start us, length us, event | category | flops | bytes accessed | tf_op | source)
XLA Modules:
  0.0 69.0 jit_solution(4236752375733086037)
XLA Ops:
  0.6 1.6 %prepare.1 = (f32[128,512]{1,0:T(8,128)S(1)}, f32[128,512]{1,0:T(8,128)S(1)}, bf16[512,512]{1,0:T(8,128)(2,1)S(1)}, f32[128,256]{1,0:T(8,128)S(1)}, f32[128,256]{1,0:T(8,128)S(1)}) custom-call(f32[3,16384]{1,0:T(4,128)} %refs_0_.2, f32[128,128]{1,0:T(8,128)} %bitcast.5, s32[128,128]{1,0:T(8,128)} %bitcast.7, s32[1,512]{1,0:T(1,128)} %bitcast.10), custom_call_target="tpu_custom_call" | custom-call | flops 1000000000 | bytes 1000000 | tf_op jit(solution)/shard_map/prepare/pallas_call | solution.py:556
  2.2 0.8 %collective-permute-start.1 = (f32[128,256]{1,0:T(8,128)S(1)}, f32[128,256]{1,0:T(8,128)S(1)}, u32[]{:S(2)}, u32[]{:S(2)}) collective-permute-start(f32[128,256]{1,0:T(8,128)S(1)} %get-tuple-element.79.refs_0_), channel_id=1, source_target_pairs={{0,16},{1,0},{2,18},{3,2},{4,20},{5,4},{6,22},{7,6},{8,24},{9,8},{... | collective-permute-start | bytes 393224 | tf_op jit(solution)/shard_map/ppermute | solution.py:526
  3.0 3.0 %deposit_kernel.1 = (f32[96,512]{1,0:T(8,128)S(1)}, s32[32,512]{1,0:T(8,128)S(1)}, f32[64,128]{1,0:T(8,128)S(1)}, f32[8,8,128]{2,1,0:T(8,128)S(1)}, f32[8,8,128]...) custom-call(f32[3,16384]{1,0:T(4,128)} %refs_0_.3, ...), custom_call_target="tpu_custom_call" | custom-call | flops 3000000000 | bytes 3000000 | tf_op jit(solution)/shard_map/deposit_kernel/pallas_call | solution.py:556
  6.1 2.1 %collective-permute-start = (f32[8,8,128]{2,1,0:T(8,128)S(1)}, f32[8,8,128]{2,1,0:T(8,128)S(1)}, u32[]{:S(2)}, u32[]{:S(2)}) collective-permute-start(f32[8,8,128]{2,1,0:T(8,128)S(1)} %get-tuple-element.78.refs_4_), channel_id=1, source_target_pairs={{0,1},{1,0},{2,3},{3,2},{4,5},{5,4},{6,7},{7,6},{8,9},{9,8},{10,11... | collective-permute-start | bytes 98312 | tf_op jit(solution)/shard_map/ppermute | solution.py:532
  8.2 1.0 %collective-permute-start.5 = (f32[128,256]{1,0:T(8,128)S(1)}, f32[128,256]{1,0:T(8,128)S(1)}, u32[]{:S(2)}, u32[]{:S(2)}) collective-permute-start(f32[128,256]{1,0:T(8,128)S(1)} %get-tuple-element.81.refs_2_), channel_id=1, source_target_pairs={{0,1},{1,2},{2,3},{3,4},{4,5},{5,6},{6,7},{7,8},{8,9},{9,10},{10,1... | collective-permute-start | bytes 393224 | tf_op jit(solution)/shard_map/ppermute | solution.py:526
  9.2 1.1 %collective-permute-start.6 = (f32[128,256]{1,0:T(8,128)S(1)}, f32[128,256]{1,0:T(8,128)S(1)}, u32[]{:S(2)}, u32[]{:S(2)}) collective-permute-start(f32[128,256]{1,0:T(8,128)S(1)} %get-tuple-element.82.refs_3_), channel_id=1, source_target_pairs={{0,16},{1,0},{2,1},{3,2},{4,3},{5,4},{6,5},{7,6},{8,7},{9,8},{10,9... | collective-permute-start | bytes 393224 | tf_op jit(solution)/shard_map/ppermute | solution.py:526
  10.4 0.9 %collective-permute-start.3 = (f32[8,8,128]{2,1,0:T(8,128)S(1)}, f32[8,8,128]{2,1,0:T(8,128)S(1)}, u32[]{:S(2)}, u32[]{:S(2)}) collective-permute-start(f32[8,8,128]{2,1,0:T(8,128)S(1)} %get-tuple-element.84.refs_2_), channel_id=1, source_target_pairs={{0,2},{1,3},{2,0},{3,1},{4,6},{5,7},{6,4},{7,5},{8,10},{9,11},{10,... | collective-permute-start | bytes 98312 | tf_op jit(solution)/shard_map/ppermute | solution.py:532
  11.3 2.5 %inner_start.1 = (bf16[512,1024]{1,0:T(8,128)(2,1)S(1)}, bf16[512,1024]{1,0:T(8,128)(2,1)S(1)}, f32[1024,128]{1,0:T(8,128)S(1)}, f32[1024,128]{1,0:T(8,128)S(1)}...) custom-call(f32[128,512]{1,0:T(8,128)S(1)} %get-tuple-element.73.refs_8_.refs_0_, ...), custom_call_target="tpu_custom_call" | custom-call | flops 3000000000 | bytes 3000000 | tf_op jit(solution)/shard_map/inner_start/pallas_call | solution.py:556
  13.9 0.8 %cross_start.1 = (bf16[512,1024]{1,0:T(8,128)(2,1)S(1)}, bf16[512,1024]{1,0:T(8,128)(2,1)S(1)}, f32[1024,128]{1,0:T(8,128)S(1)}) custom-call(f32[128,512]{1,0:T(8,128)S(1)} %get-tuple-element.73.refs_8_.refs_0_, s32[5,1024]{1,0:T(8,128)S(1)} %get-tuple-element.85.refs_1_, f32[768,128]{1,0:T(8,128)S(1)} %get-tuple-element.87.refs_2_.refs_3_), custom_call_target="tpu_custom_call" | custom-call | flops 1000000000 | bytes 1000000 | tf_op jit(solution)/shard_map/cross_start/pallas_call | solution.py:556
  14.7 1.4 %collective-permute-done.3.refs_1_ = f32[8,8,128]{2,1,0:T(8,128)S(1)} collective-permute-done((f32[8,8,128]{2,1,0:T(8,128)S(1)}, f32[8,8,128]{2,1,0:T(8,128)S(1)}, u32[]{:S(2)}, u32[]{:S(2)}) %collective-permute-start.3) | collective-permute-done | bytes 32800 | tf_op jit(solution)/shard_map/ppermute | solution.py:532
  16.1 2.0 %collective-permute-start.4 = (f32[8,8,128]{2,1,0:T(8,128)S(1)}, f32[8,8,128]{2,1,0:T(8,128)S(1)}, u32[]{:S(2)}, u32[]{:S(2)}) collective-permute-start(f32[8,8,128]{2,1,0:T(8,128)S(1)} %get-tuple-element.90.refs_5_), channel_id=1, source_target_pairs={{0,4},{1,5},{2,6},{3,7},{4,0},{5,1},{6,2},{7,3},{8,12},{9,13},{10,... | collective-permute-start | bytes 98312 | tf_op jit(solution)/shard_map/ppermute | solution.py:532
  18.1 4.0 %cross_kernel.1 = (f32[768,128]{1,0:T(8,128)S(1)}, f32[96,256]{1,0:T(8,128)S(1)}, f32[96,256]{1,0:T(8,128)S(1)}, f32[96,128]{1,0:T(8,128)S(1)}, f32[32,512]{1,0:T(8,128)S(1)}) custom-call(f32[1024,128]{1,0:T(8,128)S(1)} %get-tuple-element.88.refs_2_.refs_0_, bf16[512,1024]{1,0:T(8,128)(2,1)S(1)} %get-tuple-element.91.refs_1_, ...), custom_call_target="tpu_custom_call" | custom-call | flops 4000000000 | bytes 4000000 | tf_op jit(solution)/shard_map/cross_kernel/pallas_call | solution.py:556
  22.2 3.5 %collective-permute-start.7 = (f32[8,8,128]{2,1,0:T(8,128)S(1)}, f32[8,8,128]{2,1,0:T(8,128)S(1)}, u32[]{:S(2)}, u32[]{:S(2)}) collective-permute-start(f32[8,8,128]{2,1,0:T(8,128)S(1)} %get-tuple-element.95.refs_4_), channel_id=1, source_target_pairs={{0,8},{1,9},{2,10},{3,11},{4,12},{5,13},{6,14},{7,15},{8,0},{9,1},... | collective-permute-start | bytes 98312 | tf_op jit(solution)/shard_map/ppermute | solution.py:532
  25.7 2.0 %collective-permute-start.8 = (f32[96,256]{1,0:T(8,128)S(1)}, f32[96,256]{1,0:T(8,128)S(1)}, u32[]{:S(2)}, u32[]{:S(2)}) collective-permute-start(f32[96,256]{1,0:T(8,128)S(1)} %get-tuple-element.97), channel_id=1, source_target_pairs={{0,1},{1,2},{2,3},{3,4},{4,5},{5,6},{6,7},{7,8},{8,9},{9,10},{10,1... | collective-permute-start | bytes 294920 | tf_op jit(solution)/shard_map/ppermute | solution.py:526
  27.7 1.5 %inner_rest.2 = (f32[768,128]{1,0:T(8,128)S(1)}, f32[768,128]{1,0:T(8,128)S(1)}) custom-call(f32[1024,128]{1,0:T(8,128)S(1)} %get-tuple-element.99.refs_0_, f32[1024,128]{1,0:T(8,128)S(1)} %get-tuple-element.100.refs_1_, f32[768,128]{1,0:T(8,128)S(1)} %get-tuple-element.101.refs_2_, f32[768,128]{1,0:T(8,128)S(1)} %get-tuple-element.87.refs_2_.refs_3_, ...), custom_call_target="tpu_custom_call" | custom-call | flops 2000000000 | bytes 2000000 | tf_op jit(solution)/shard_map/inner_rest/pallas_call | solution.py:556
  29.2 1.2 %scatter_kernel.2.refs_3_.refs_4_ = f32[96,512]{1,0:T(8,128)S(1)} custom-call(f32[768,128]{1,0:T(8,128)S(1)} %get-tuple-element.102.refs_0_, f32[768,128]{1,0:T(8,128)S(1)} %get-tuple-element.103.refs_1_, f32[768,128]{1,0:T(8,128)S(1)} %get-tuple-element.104.refs_2_, bf16[512,1024]{1,0:T(8,128)(2,1)S(1)} %get-tuple-element.105.refs_3_.refs_2_, ...), custom_call_target="tpu_custom_call" | custom-call | flops 2000000000 | bytes 2000000 | tf_op jit(solution)/shard_map/scatter_kernel/pallas_call | solution.py:556
  30.4 4.0 %collective-permute-done.9.refs_1_ = f32[96,256]{1,0:T(8,128)S(1)} collective-permute-done((f32[96,256]{1,0:T(8,128)S(1)}, f32[96,256]{1,0:T(8,128)S(1)}, u32[]{:S(2)}, u32[]{:S(2)}) %collective-permute-start.9) | collective-permute-done | bytes 98336 | tf_op jit(solution)/shard_map/ppermute | solution.py:526
  35.0 2.6 %fluid_kernel.1 = (f32[128,512]{1,0:T(8,128)S(1)}, f32[16,8,128]{2,1,0:T(8,128)S(1)}) custom-call(f32[64,128]{1,0:T(8,128)S(1)} %get-tuple-element.76.refs_0_, f32[8,8,128]{2,1,0:T(8,128)S(1)} %get-tuple-element.94.refs_1_, f32[8,8,128]{2,1,0:T(8,128)S(1)} %collective-permute-done.7.refs_2_, s32[32,512]{1,0:T(8,128)S(1)} %get-tuple-element.96.refs_3_, ...), custom_call_target="tpu_custom_call" | custom-call | flops 3000000000 | bytes 3000000 | tf_op jit(solution)/shard_map/fluid_kernel/pallas_call | solution.py:556
  37.7 1.7 %collective-permute-done.11.refs_7_ = f32[96,256]{1,0:T(8,128)S(1)} collective-permute-done((f32[96,256]{1,0:T(8,128)S(1)}, f32[96,256]{1,0:T(8,128)S(1)}, u32[]{:S(2)}, u32[]{:S(2)}) %collective-permute-start.11) | collective-permute-done | bytes 98336 | tf_op jit(solution)/shard_map/ppermute | solution.py:526
  40.6 2.5 %inner_again.1 = (f32[1024,128]{1,0:T(8,128)S(1)}, f32[1024,128]{1,0:T(8,128)S(1)}, f32[768,128]{1,0:T(8,128)S(1)}, f32[768,128]{1,0:T(8,128)S(1)}) custom-call(f32[128,512]{1,0:T(8,128)S(1)} %get-tuple-element.113.refs_0_, s32[5,1024]{1,0:T(8,128)S(1)} %get-tuple-element.86.refs_1_, bf16[512,1024]{1,0:T(8,128)(2,1)S(1)} %get-tuple-element.105.refs_3_.refs_2_, ...), custom_call_target="tpu_custom_call" | custom-call | flops 3000000000 | bytes 3000000 | tf_op jit(solution)/shard_map/inner_again/pallas_call | solution.py:556
  43.1 1.7 %collective-permute-done.13.refs_3_ = f32[96,256]{1,0:T(8,128)S(1)} collective-permute-done((f32[96,256]{1,0:T(8,128)S(1)}, f32[96,256]{1,0:T(8,128)S(1)}, u32[]{:S(2)}, u32[]{:S(2)}) %collective-permute-start.13) | collective-permute-done | bytes 98336 | tf_op jit(solution)/shard_map/ppermute | solution.py:526
  45.1 1.8 %collective-permute-start.15 = (f32[96,256]{1,0:T(8,128)S(1)}, f32[96,256]{1,0:T(8,128)S(1)}, u32[]{:S(2)}, u32[]{:S(2)}) collective-permute-start(f32[96,256]{1,0:T(8,128)S(1)} %get-tuple-element.123.refs_4_), channel_id=1, source_target_pairs={{0,16},{1,0},{2,1},{3,2},{4,3},{5,4},{6,5},{7,6},{8,7},{9,8},{10,9... | collective-permute-start | bytes 294920 | tf_op jit(solution)/shard_map/ppermute | solution.py:526
  47.6 1.5 %inner_rest.3 = (f32[768,128]{1,0:T(8,128)S(1)}, f32[768,128]{1,0:T(8,128)S(1)}) custom-call(f32[1024,128]{1,0:T(8,128)S(1)} %get-tuple-element.116.refs_0_, f32[1024,128]{1,0:T(8,128)S(1)} %get-tuple-element.117.refs_1_, f32[768,128]{1,0:T(8,128)S(1)} %get-tuple-element.118.refs_2_, f32[768,128]{1,0:T(8,128)S(1)} %get-tuple-element.119.refs_4_.refs_3_, ...), custom_call_target="tpu_custom_call" | custom-call | flops 2000000000 | bytes 2000000 | tf_op jit(solution)/shard_map/inner_rest/pallas_call | solution.py:556
  49.6 2.3 %collective-permute-done.15.refs_3_ = f32[96,256]{1,0:T(8,128)S(1)} collective-permute-done((f32[96,256]{1,0:T(8,128)S(1)}, f32[96,256]{1,0:T(8,128)S(1)}, u32[]{:S(2)}, u32[]{:S(2)}) %collective-permute-start.15) | collective-permute-done | bytes 98336 | tf_op jit(solution)/shard_map/ppermute | solution.py:526
  51.9 4.0 %cross_kernel_again.1 = (f32[768,128]{1,0:T(8,128)S(1)}, f32[96,256]{1,0:T(8,128)S(1)}, f32[96,256]{1,0:T(8,128)S(1)}, f32[96,128]{1,0:T(8,128)S(1)}) custom-call(f32[1024,128]{1,0:T(8,128)S(1)} %cross_again.1.refs_4_.refs_0_, bf16[512,1024]{1,0:T(8,128)(2,1)S(1)} %get-tuple-element.91.refs_1_, f32[96,256]{1,0:T(8,128)S(1)} %collective-permute-done.14.refs_2_, ...), custom_call_target="tpu_custom_call" | custom-call | flops 4000000000 | bytes 4000000 | tf_op jit(solution)/shard_map/cross_kernel_again/pallas_call | solution.py:556
  56.0 2.0 %collective-permute-start.17 = (f32[96,256]{1,0:T(8,128)S(1)}, f32[96,256]{1,0:T(8,128)S(1)}, u32[]{:S(2)}, u32[]{:S(2)}) collective-permute-start(f32[96,256]{1,0:T(8,128)S(1)} %get-tuple-element.131), channel_id=1, source_target_pairs={{0,16},{1,0},{2,1},{3,2},{4,3},{5,4},{6,5},{7,6},{8,7},{9,8},{10,9... | collective-permute-start | bytes 294920 | tf_op jit(solution)/shard_map/ppermute | solution.py:526
  58.0 1.2 %scatter_kernel.3.refs_3_.refs_4_ = f32[96,512]{1,0:T(8,128)S(1)} custom-call(f32[768,128]{1,0:T(8,128)S(1)} %get-tuple-element.124.refs_0_, f32[768,128]{1,0:T(8,128)S(1)} %get-tuple-element.125.refs_6_.refs_1_, f32[768,128]{1,0:T(8,128)S(1)} %get-tuple-element.128.refs_2_, bf16[512,1024]{1,0:T(8,128)(2,1)S(1)} %get-tuple-element.105.refs_3_.refs_2_, ...), custom_call_target="tpu_custom_call" | custom-call | flops 2000000000 | bytes 2000000 | tf_op jit(solution)/shard_map/scatter_kernel/pallas_call | solution.py:556
  59.2 1.4 %collective-permute-done.16.refs_0_ = f32[96,256]{1,0:T(8,128)S(1)} collective-permute-done((f32[96,256]{1,0:T(8,128)S(1)}, f32[96,256]{1,0:T(8,128)S(1)}, u32[]{:S(2)}, u32[]{:S(2)}) %collective-permute-start.16) | collective-permute-done | bytes 98336 | tf_op jit(solution)/shard_map/ppermute | solution.py:526
  60.6 2.2 %collective-permute-done.17.refs_1_ = f32[96,256]{1,0:T(8,128)S(1)} collective-permute-done((f32[96,256]{1,0:T(8,128)S(1)}, f32[96,256]{1,0:T(8,128)S(1)}, u32[]{:S(2)}, u32[]{:S(2)}) %collective-permute-start.17) | collective-permute-done | bytes 98336 | tf_op jit(solution)/shard_map/ppermute | solution.py:526
  64.1 1.0 %collective-permute-done.18.refs_6_ = f32[96,256]{1,0:T(8,128)S(1)} collective-permute-done((f32[96,256]{1,0:T(8,128)S(1)}, f32[96,256]{1,0:T(8,128)S(1)}, u32[]{:S(2)}, u32[]{:S(2)}) %collective-permute-start.18) | collective-permute-done | bytes 98336 | tf_op jit(solution)/shard_map/ppermute | solution.py:526
  65.1 2.5 %collective-permute-done.19.refs_7_ = f32[96,256]{1,0:T(8,128)S(1)} collective-permute-done((f32[96,256]{1,0:T(8,128)S(1)}, f32[96,256]{1,0:T(8,128)S(1)}, u32[]{:S(2)}, u32[]{:S(2)}) %collective-permute-start.19) | collective-permute-done | bytes 98336 | tf_op jit(solution)/shard_map/ppermute | solution.py:526
  67.6 1.4 %last_kernel.1 = (f32[3,16384]{1,0:T(4,128)}, f32[3,16384]{1,0:T(4,128)}) custom-call(f32[128,512]{1,0:T(8,128)S(1)} %get-tuple-element.113.refs_0_, f32[128,512]{1,0:T(8,128)S(1)} %get-tuple-element.114.refs_1_, f32[96,512]{1,0:T(8,128)S(1)} %get-tuple-element.115.refs_2_, f32[128,512]{1,0:T(8,128)S(1)} %get-tuple-element.110.refs_3_, ...), custom_call_target="tpu_custom_call" | custom-call | flops 1000000000 | bytes 1000000 | tf_op jit(solution)/shard_map/last_kernel/pallas_call | solution.py:556
  (31 shorter events, 4.8 us)
Async XLA Ops:
  2.2 6.0 %collective-permute-start.1 = (f32[128,256]{1,0:T(8,128)S(1)}, f32[128,256]{1,0:T(8,128)S(1)}, u32[]{:S(2)}, u32[]{:S(2)}) collective-permute-start(f32[128,256]{1,0:T(8,128)S(1)} %get-tuple-element.79.refs_0_), channel_id=1, source_target_pairs={{0,16},{1,0},{2,18},{3,2},{4,20},{5,4},{6,22},{7,6},{8,24},{9,8},{... | collective-permute-start | bytes 393224 | tf_op jit(solution)/shard_map/ppermute | solution.py:526
  3.0 5.1 %collective-permute-start.2 = (f32[128,256]{1,0:T(8,128)S(1)}, f32[128,256]{1,0:T(8,128)S(1)}, u32[]{:S(2)}, u32[]{:S(2)}) collective-permute-start(f32[128,256]{1,0:T(8,128)S(1)} %get-tuple-element.80.refs_1_), channel_id=1, source_target_pairs={{0,1},{1,17},{2,3},{3,19},{4,5},{5,21},{6,7},{7,23},{8,9},{9,25},{... | collective-permute-start | bytes 393224 | tf_op jit(solution)/shard_map/ppermute | solution.py:526
  6.1 4.3 %collective-permute-start = (f32[8,8,128]{2,1,0:T(8,128)S(1)}, f32[8,8,128]{2,1,0:T(8,128)S(1)}, u32[]{:S(2)}, u32[]{:S(2)}) collective-permute-start(f32[8,8,128]{2,1,0:T(8,128)S(1)} %get-tuple-element.78.refs_4_), channel_id=1, source_target_pairs={{0,1},{1,0},{2,3},{3,2},{4,5},{5,4},{6,7},{7,6},{8,9},{9,8},{10,11... | collective-permute-start | bytes 98312 | tf_op jit(solution)/shard_map/ppermute | solution.py:532
  8.2 9.9 %collective-permute-start.5 = (f32[128,256]{1,0:T(8,128)S(1)}, f32[128,256]{1,0:T(8,128)S(1)}, u32[]{:S(2)}, u32[]{:S(2)}) collective-permute-start(f32[128,256]{1,0:T(8,128)S(1)} %get-tuple-element.81.refs_2_), channel_id=1, source_target_pairs={{0,1},{1,2},{2,3},{3,4},{4,5},{5,6},{6,7},{7,8},{8,9},{9,10},{10,1... | collective-permute-start | bytes 393224 | tf_op jit(solution)/shard_map/ppermute | solution.py:526
  9.2 8.9 %collective-permute-start.6 = (f32[128,256]{1,0:T(8,128)S(1)}, f32[128,256]{1,0:T(8,128)S(1)}, u32[]{:S(2)}, u32[]{:S(2)}) collective-permute-start(f32[128,256]{1,0:T(8,128)S(1)} %get-tuple-element.82.refs_3_), channel_id=1, source_target_pairs={{0,16},{1,0},{2,1},{3,2},{4,3},{5,4},{6,5},{7,6},{8,7},{9,8},{10,9... | collective-permute-start | bytes 393224 | tf_op jit(solution)/shard_map/ppermute | solution.py:526
  10.4 5.7 %collective-permute-start.3 = (f32[8,8,128]{2,1,0:T(8,128)S(1)}, f32[8,8,128]{2,1,0:T(8,128)S(1)}, u32[]{:S(2)}, u32[]{:S(2)}) collective-permute-start(f32[8,8,128]{2,1,0:T(8,128)S(1)} %get-tuple-element.84.refs_2_), channel_id=1, source_target_pairs={{0,2},{1,3},{2,0},{3,1},{4,6},{5,7},{6,4},{7,5},{8,10},{9,11},{10,... | collective-permute-start | bytes 98312 | tf_op jit(solution)/shard_map/ppermute | solution.py:532
  16.1 6.1 %collective-permute-start.4 = (f32[8,8,128]{2,1,0:T(8,128)S(1)}, f32[8,8,128]{2,1,0:T(8,128)S(1)}, u32[]{:S(2)}, u32[]{:S(2)}) collective-permute-start(f32[8,8,128]{2,1,0:T(8,128)S(1)} %get-tuple-element.90.refs_5_), channel_id=1, source_target_pairs={{0,4},{1,5},{2,6},{3,7},{4,0},{5,1},{6,2},{7,3},{8,12},{9,13},{10,... | collective-permute-start | bytes 98312 | tf_op jit(solution)/shard_map/ppermute | solution.py:532
  22.2 12.8 %collective-permute-start.7 = (f32[8,8,128]{2,1,0:T(8,128)S(1)}, f32[8,8,128]{2,1,0:T(8,128)S(1)}, u32[]{:S(2)}, u32[]{:S(2)}) collective-permute-start(f32[8,8,128]{2,1,0:T(8,128)S(1)} %get-tuple-element.95.refs_4_), channel_id=1, source_target_pairs={{0,8},{1,9},{2,10},{3,11},{4,12},{5,13},{6,14},{7,15},{8,0},{9,1},... | collective-permute-start | bytes 98312 | tf_op jit(solution)/shard_map/ppermute | solution.py:532
  25.7 4.7 %collective-permute-start.8 = (f32[96,256]{1,0:T(8,128)S(1)}, f32[96,256]{1,0:T(8,128)S(1)}, u32[]{:S(2)}, u32[]{:S(2)}) collective-permute-start(f32[96,256]{1,0:T(8,128)S(1)} %get-tuple-element.97), channel_id=1, source_target_pairs={{0,1},{1,2},{2,3},{3,4},{4,5},{5,6},{6,7},{7,8},{8,9},{9,10},{10,1... | collective-permute-start | bytes 294920 | tf_op jit(solution)/shard_map/ppermute | solution.py:526
  27.7 6.7 %collective-permute-start.9 = (f32[96,256]{1,0:T(8,128)S(1)}, f32[96,256]{1,0:T(8,128)S(1)}, u32[]{:S(2)}, u32[]{:S(2)}) collective-permute-start(f32[96,256]{1,0:T(8,128)S(1)} %get-tuple-element.98), channel_id=1, source_target_pairs={{0,16},{1,0},{2,1},{3,2},{4,3},{5,4},{6,5},{7,6},{8,7},{9,8},{10,9... | collective-permute-start | bytes 294920 | tf_op jit(solution)/shard_map/ppermute | solution.py:526
  34.4 3.2 %collective-permute-start.10 = (f32[96,256]{1,0:T(8,128)S(1)}, f32[96,256]{1,0:T(8,128)S(1)}, u32[]{:S(2)}, u32[]{:S(2)}) collective-permute-start(f32[96,256]{1,0:T(8,128)S(1)} %get-tuple-element.108.refs_4_), channel_id=1, source_target_pairs={{0,16},{1,0},{2,18},{3,2},{4,20},{5,4},{6,22},{7,6},{8,24},{9,8},{... | collective-permute-start | bytes 294920 | tf_op jit(solution)/shard_map/ppermute | solution.py:526
  34.5 4.9 %collective-permute-start.11 = (f32[96,256]{1,0:T(8,128)S(1)}, f32[96,256]{1,0:T(8,128)S(1)}, u32[]{:S(2)}, u32[]{:S(2)}) collective-permute-start(f32[96,256]{1,0:T(8,128)S(1)} %get-tuple-element.109.refs_5_), channel_id=1, source_target_pairs={{0,1},{1,17},{2,3},{3,19},{4,5},{5,21},{6,7},{7,23},{8,9},{9,25},{... | collective-permute-start | bytes 294920 | tf_op jit(solution)/shard_map/ppermute | solution.py:526
  40.0 3.1 %collective-permute-start.12 = (f32[96,256]{1,0:T(8,128)S(1)}, f32[96,256]{1,0:T(8,128)S(1)}, u32[]{:S(2)}, u32[]{:S(2)}) collective-permute-start(f32[96,256]{1,0:T(8,128)S(1)} %get-tuple-element.120.refs_0_), channel_id=1, source_target_pairs={{0,16},{1,0},{2,18},{3,2},{4,20},{5,4},{6,22},{7,6},{8,24},{9,8},{... | collective-permute-start | bytes 294920 | tf_op jit(solution)/shard_map/ppermute | solution.py:526
  40.2 4.6 %collective-permute-start.13 = (f32[96,256]{1,0:T(8,128)S(1)}, f32[96,256]{1,0:T(8,128)S(1)}, u32[]{:S(2)}, u32[]{:S(2)}) collective-permute-start(f32[96,256]{1,0:T(8,128)S(1)} %get-tuple-element.121.refs_1_), channel_id=1, source_target_pairs={{0,1},{1,17},{2,3},{3,19},{4,5},{5,21},{6,7},{7,23},{8,9},{9,25},{... | collective-permute-start | bytes 294920 | tf_op jit(solution)/shard_map/ppermute | solution.py:526
  44.9 4.7 %collective-permute-start.14 = (f32[96,256]{1,0:T(8,128)S(1)}, f32[96,256]{1,0:T(8,128)S(1)}, u32[]{:S(2)}, u32[]{:S(2)}) collective-permute-start(f32[96,256]{1,0:T(8,128)S(1)} %get-tuple-element.122.refs_3_), channel_id=1, source_target_pairs={{0,1},{1,2},{2,3},{3,4},{4,5},{5,6},{6,7},{7,8},{8,9},{9,10},{10,1... | collective-permute-start | bytes 294920 | tf_op jit(solution)/shard_map/ppermute | solution.py:526
  45.1 6.7 %collective-permute-start.15 = (f32[96,256]{1,0:T(8,128)S(1)}, f32[96,256]{1,0:T(8,128)S(1)}, u32[]{:S(2)}, u32[]{:S(2)}) collective-permute-start(f32[96,256]{1,0:T(8,128)S(1)} %get-tuple-element.123.refs_4_), channel_id=1, source_target_pairs={{0,16},{1,0},{2,1},{3,2},{4,3},{5,4},{6,5},{7,6},{8,7},{9,8},{10,9... | collective-permute-start | bytes 294920 | tf_op jit(solution)/shard_map/ppermute | solution.py:526
  55.9 4.7 %collective-permute-start.16 = (f32[96,256]{1,0:T(8,128)S(1)}, f32[96,256]{1,0:T(8,128)S(1)}, u32[]{:S(2)}, u32[]{:S(2)}) collective-permute-start(f32[96,256]{1,0:T(8,128)S(1)} %get-tuple-element.130), channel_id=1, source_target_pairs={{0,1},{1,2},{2,3},{3,4},{4,5},{5,6},{6,7},{7,8},{8,9},{9,10},{10,1... | collective-permute-start | bytes 294920 | tf_op jit(solution)/shard_map/ppermute | solution.py:526
  56.0 6.8 %collective-permute-start.17 = (f32[96,256]{1,0:T(8,128)S(1)}, f32[96,256]{1,0:T(8,128)S(1)}, u32[]{:S(2)}, u32[]{:S(2)}) collective-permute-start(f32[96,256]{1,0:T(8,128)S(1)} %get-tuple-element.131), channel_id=1, source_target_pairs={{0,16},{1,0},{2,1},{3,2},{4,3},{5,4},{6,5},{7,6},{8,7},{9,8},{10,9... | collective-permute-start | bytes 294920 | tf_op jit(solution)/shard_map/ppermute | solution.py:526
  62.8 2.3 %collective-permute-start.18 = (f32[96,256]{1,0:T(8,128)S(1)}, f32[96,256]{1,0:T(8,128)S(1)}, u32[]{:S(2)}, u32[]{:S(2)}) collective-permute-start(f32[96,256]{1,0:T(8,128)S(1)} %get-tuple-element.133.refs_3_), channel_id=1, source_target_pairs={{0,16},{1,0},{2,18},{3,2},{4,20},{5,4},{6,22},{7,6},{8,24},{9,8},{... | collective-permute-start | bytes 294920 | tf_op jit(solution)/shard_map/ppermute | solution.py:526
  62.9 4.7 %collective-permute-start.19 = (f32[96,256]{1,0:T(8,128)S(1)}, f32[96,256]{1,0:T(8,128)S(1)}, u32[]{:S(2)}, u32[]{:S(2)}) collective-permute-start(f32[96,256]{1,0:T(8,128)S(1)} %get-tuple-element.134.refs_4_), channel_id=1, source_target_pairs={{0,1},{1,17},{2,3},{3,19},{4,5},{5,21},{6,7},{7,23},{8,9},{9,25},{... | collective-permute-start | bytes 294920 | tf_op jit(solution)/shard_map/ppermute | solution.py:526

commit v4 on v3

--- a/solution.py
+++ b/solution.py
@@ -42,8 +42,14 @@
 
 
 def one_hot(index_row, count):
-    rows = lax.broadcasted_iota(jnp.int32, (count, index_row.shape[1]), 0)
-    return jnp.where(rows == index_row, 1.0, 0.0).astype(bf16)
+    width = index_row.shape[1]
+    rows = lax.broadcasted_iota(jnp.int32, (LANES, width), 0).astype(f32).astype(bf16)
+    blocks = []
+    for k in range(count // LANES):
+        within = index_row - k * LANES
+        within = jnp.where((within >= 0) & (within < LANES), within, -1).astype(f32).astype(bf16)
+        blocks.append(jnp.where(rows == within, jnp.ones((), bf16), jnp.zeros((), bf16)))
+    return jnp.concatenate(blocks, axis=0) if len(blocks) > 1 else blocks[0]
 
 
 def dot(left, right):
@@ -70,6 +76,28 @@
     return lax.broadcasted_iota(jnp.int32, shape, 1) < GHOSTS
 
 
+def swap_halves(tile):
+    return jnp.concatenate([tile[:, GHOSTS:], tile[:, :GHOSTS]], axis=1)
+
+
+def fold(whole, half, upper):
+    rows = half.shape[0] // 2
+    low = lower_half((rows, LANES))
+    if upper:
+        packed = jnp.where(low, swap_halves(half[:rows]), half[rows:])
+    else:
+        packed = jnp.where(low, half[:rows], swap_halves(half[rows:]))
+    return jnp.concatenate([whole, packed], axis=0)
+
+
+def unfold(folded, upper):
+    rows = folded.shape[0] // 3
+    packed = folded[2 * rows :]
+    turned = swap_halves(packed)
+    half = [turned, packed] if upper else [packed, turned]
+    return folded[: 2 * rows], jnp.concatenate(half, axis=0)
+
+
 def by_parity(axis, even_first, even_second):
     even = lax.axis_index(axis) % 2 == 0
     return (
@@ -109,19 +137,48 @@
     return total
 
 
-def send_pieces(table, rows, hot, lead, trail):
+def send_pieces(table, rows, hot, lead, trail, middle):
     pieces = gather(jnp.concatenate(split(table[:rows], 3), axis=0), hot[...], rows)
-    half = CLUSTERS // 2
-    lead[...], trail[...] = by_parity("gy", pieces[:, half:], pieces[:, :half])
+    tiles = [pieces[:, k * LANES : (k + 1) * LANES] for k in range(4)]
+    up = fold(tiles[3], tiles[2], True)
+    down = fold(tiles[0], tiles[1], False)
+    lead[...], trail[...] = by_parity("gy", up, down)
+    middle[...] = jnp.where(lower_half(tiles[1].shape), tiles[2], tiles[1])
+
+
+def start_copies(pairs, arrived, first=0):
+    copies = [
+        pltpu.make_async_copy(far, near, arrived.at[first + k])
+        for k, (far, near) in enumerate(pairs)
+    ]
+    for copy in copies:
+        copy.start()
+    return copies
 
 
 def prepare(
-    positions_far, radius_far, mask_far, send_far, table_out, state_out, hot, lead, trail,
+    positions_far, radius_far, mask_far, send_far,
+    velocity_far, cell_far, fluid_far, pressure_far, inner_far, cross_far,
+    table_out, state_out, hot, lead, trail, middle, velocity, cell, fluid, pressure, inner, cross,
     positions, radius, mask, send, stage, arrived,
 ):
-    fetch(
+    needed = start_copies(
         ((positions_far, positions), (radius_far, radius), (mask_far, mask), (send_far, send)), arrived
     )
+    later = start_copies(
+        (
+            (velocity_far, velocity),
+            (cell_far, cell),
+            (fluid_far, fluid),
+            (pressure_far, pressure),
+            (inner_far, inner),
+            (cross_far, cross),
+        ),
+        arrived,
+        4,
+    )
+    for copy in needed:
+        copy.wait()
     parts = load_components(positions, stage)
     reach = to_table(radius[...])
     weights = to_table(mask[...].astype(f32))
@@ -132,7 +189,9 @@
         state_out[c * SLOTS : (c + 1) * SLOTS] = parts[c]
     state_out[3 * SLOTS :] = weights
     hot[...] = one_hot(cluster_column(send[...]), CLUSTERS)
-    send_pieces(table, 4 * SLOTS, hot, lead, trail)
+    send_pieces(table, 4 * SLOTS, hot, lead, trail, middle)
+    for copy in later:
+        copy.wait()
 
 
 def contacts(leading, partner, on_leading, on_partner, begin, end):
@@ -201,7 +260,7 @@
 
 
 def table_parts(table):
-    return jnp.concatenate(split(table[...], 3), axis=0)
+    return jnp.concatenate(split(table[...], 2), axis=0)
 
 
 INNER_SPLIT = 16
@@ -259,36 +318,35 @@
     return jnp.where(lower_half((1, LANES)), flags[0], flags[1]) > 0
 
 
-def pass_ghosts(lead, trail, got_lead, got_trail, lead_out, trail_out, side):
-    low = lower_half((lead.shape[0], LANES))
-    own_second, own_first = by_parity("gy", lead[...], trail[...])
+def pass_ghosts(got_lead, got_trail, middle, lead_out, trail_out, side):
+    low = lower_half(middle.shape)
     from_last, from_next = by_parity("gy", got_lead[...], got_trail[...])
-    minus = [jnp.where(low, from_next[:, :LANES], from_last[:, :LANES]), own_first[:, LANES:]]
-    plus = [jnp.where(low, from_next[:, LANES:], from_last[:, LANES:]), own_second[:, :LANES]]
-    for k in range(2):
-        span = slice(k * LANES, (k + 1) * LANES)
-        lead_out[:, span], trail_out[:, span] = by_parity("gx", plus[k], minus[k])
-    side[...] = jnp.where(low, from_last[:, LANES:], from_next[:, :LANES])
+    last_whole, last_half = unfold(from_last, True)
+    next_whole, next_half = unfold(from_next, False)
+    minus = fold(jnp.where(low, next_whole, last_half), middle[...], True)
+    plus = fold(jnp.where(low, next_half, last_whole), middle[...], False)
+    lead_out[...], trail_out[...] = by_parity("gx", plus, minus)
+    side[...] = jnp.where(low, last_whole, next_whole)
 
 
 def cross_contacts(ghosts, leading, hot_b, on_leading, lead, trail, side_out, partner, on_partner):
-    fill_slots(jnp.concatenate(split(ghosts, 3), axis=0), hot_b, None, partner)
+    fill_slots(table_parts(ghosts), hot_b, None, partner)
     on_partner[...] = jnp.zeros_like(on_partner)
     contacts(leading, partner, on_leading, on_partner, 0, SLOTS)
     back = scatter(on_partner, hot_b)
-    lead[...], trail[...] = by_parity("gx", back[:, : 2 * LANES], back[:, LANES : 3 * LANES])
-    side_out[...] = back[:, 3 * LANES :]
+    tiles = [back[:, k * LANES : (k + 1) * LANES] for k in range(4)]
+    up = fold(tiles[0], tiles[1], True)
+    down = fold(tiles[2], tiles[1], False)
+    lead[...], trail[...] = by_parity("gx", up, down)
+    side_out[...] = tiles[3]
 
 
 def ghost_places(got_lead, got_trail, side):
     from_last, from_next = by_parity("gx", got_lead[...], got_trail[...])
+    last_whole, last_half = unfold(from_last, False)
+    next_whole, next_half = unfold(from_next, True)
     low = lower_half(side.shape)
-    tiles = [
-        from_next[:, :LANES],
-        jnp.where(low, from_last[:, LANES:], from_next[:, LANES:]),
-        from_last[:, :LANES],
-        side[...],
-    ]
+    tiles = [next_whole, jnp.where(low, last_half, next_half), last_whole, side[...]]
     placed = [
         jnp.where(
             present_tile(GHOST_ORDER[2 * k], GHOST_ORDER[2 * k + 1]), tiles[k][: 3 * SLOTS], FAR
@@ -321,22 +379,12 @@
 def pass_forces(got_lead, got_trail, side, lead_out, trail_out, middle):
     low = lower_half((3 * SLOTS, LANES))
     from_last, from_next = by_parity("gx", got_lead[...], got_trail[...])
-    up = [jnp.where(low, from_last[:, :LANES], side[...]), from_next[:, LANES:]]
-    down = [from_last[:, :LANES], jnp.where(low, side[...], from_next[:, LANES:])]
-    for k in range(2):
-        span = slice(k * LANES, (k + 1) * LANES)
-        lead_out[:, span], trail_out[:, span] = by_parity("gy", up[k], down[k])
-    middle[...] = jnp.where(low, from_next[:, :LANES], from_last[:, LANES:])
-
-
-def fetch(pairs, arrived):
-    copies = [
-        pltpu.make_async_copy(far, near, arrived.at[k]) for k, (far, near) in enumerate(pairs)
-    ]
-    for copy in copies:
-        copy.start()
-    for copy in copies:
-        copy.wait()
+    last_whole, last_half = unfold(from_last, True)
+    next_whole, next_half = unfold(from_next, False)
+    up = fold(jnp.where(low, last_whole, side[...]), next_whole, False)
+    down = fold(jnp.where(low, side[...], next_whole), last_whole, True)
+    lead_out[...], trail_out[...] = by_parity("gy", up, down)
+    middle[...] = jnp.where(low, next_half, last_half)
 
 
 def part_parcels(parcels, bit, stay, away):
@@ -363,41 +411,30 @@
 
 
 def deposit_kernel(
-    velocity_far, radius_far, mask_far, cell_far, fluid_far, pressure_far, inner_far, cross_far,
-    velocity_out, cell_out, totals_out, stay, away, fluid, pressure, inner, cross,
-    velocity, radius, mask, cell, stage, arrived,
+    table, state, velocity, cell, fluid, pressure, velocity_out, cell_out, totals_out, stay, away, stage
 ):
-    fetch(
-        (
-            (velocity_far, velocity),
-            (radius_far, radius),
-            (mask_far, mask),
-            (cell_far, cell),
-            (fluid_far, fluid),
-            (pressure_far, pressure),
-            (inner_far, inner),
-            (cross_far, cross),
-        ),
-        arrived,
-    )
     parts = load_components(velocity, stage)
-    reach = to_table(radius[...])
-    weights = to_table(mask[...].astype(f32))
+    reach = table[3 * SLOTS :, :]
+    weights = state[3 * SLOTS :, :]
     cells = to_table(cell[...].astype(f32)).astype(jnp.int32)
     volumes = weights * ((4.0 * math.pi / 3.0) * reach * reach * reach)
     for c in range(3):
         velocity_out[c * SLOTS : (c + 1) * SLOTS] = parts[c]
     cell_out[...] = cells
     amounts = [volumes] + [volumes * part for part in parts]
+    highs = [amount.astype(bf16).astype(f32) for amount in amounts]
+    lows = [amount - high for amount, high in zip(amounts, highs)]
+    rows = lax.broadcasted_iota(jnp.int32, (16, CLUSTERS), 0).astype(f32).astype(bf16)
     total = jnp.zeros((2 * 4 * 16, LANES), f32)
     for slot in range(SLOTS):
         cell_row = cells[slot : slot + 1]
         hot = one_hot(cell_row & (LANES - 1), LANES)
-        group = lax.broadcasted_iota(jnp.int32, (16, CLUSTERS), 0) == (cell_row >> 7)
-        spread = jnp.concatenate(
-            [jnp.where(group, amount[slot : slot + 1], 0.0) for amount in amounts], axis=0
-        )
-        total = total + dot_lanes(jnp.concatenate(split(spread, 2), axis=0), hot)
+        group = rows == (cell_row >> 7).astype(f32).astype(bf16)
+        spread = [
+            jnp.where(group, part[slot : slot + 1].astype(bf16), jnp.zeros((), bf16))
+            for part in highs + lows
+        ]
+        total = total + dot_lanes(jnp.concatenate(spread, axis=0), hot)
     total = total[:64] + total[64:]
     totals_out[...] = total
     parcels = []
@@ -413,7 +450,7 @@
     part_parcels(parcels, 1, stay, away)
 
 
-def fluid_kernel(totals, stay, got, cell, at_grain, parcels_out):
+def fluid_kernel(totals, stay, got, cell, at_grain, parcels_out, stage):
     parcels = join_parcels(stay, got, 8)
     for source in range(16):
         parcels_out[source] = parcels[source]
@@ -427,16 +464,27 @@
         driven = jnp.concatenate([parcels[k][4 + c : 5 + c] for k in range(16)], axis=0)
         fields.append((void_here * driven + time_step * momentum) / below)
     fields.append(drag_rate)
-    parts = jnp.concatenate(split(jnp.concatenate(fields, axis=0), 2), axis=1)
+    mixed = jnp.concatenate(
+        [field[k : k + 1] for k in range(16) for field in fields], axis=0
+    )
+    parts = jnp.concatenate(split(mixed, 2), axis=0)
+    ranges = lax.broadcasted_iota(jnp.int32, (64, CLUSTERS), 0) >> 2
     for slot in range(SLOTS):
         cell_row = cell[slot : slot + 1, :]
-        hot = one_hot(cell_row & (LANES - 1), LANES)
-        seen = dot(parts, jnp.concatenate([hot, hot], axis=0))
-        group = lax.broadcasted_iota(jnp.int32, (16, CLUSTERS), 0) == (cell_row >> 7)
-        for c in range(4):
-            chosen = jnp.where(group, seen[c * 16 : (c + 1) * 16], 0.0)
-            row = c * SLOTS + slot
-            at_grain[row : row + 1, :] = jnp.sum(chosen, axis=0, keepdims=True)
+        seen = dot(parts, one_hot(cell_row & (LANES - 1), LANES))
+        chosen = jnp.where(ranges == (cell_row >> 7), seen[:64] + seen[64:], 0.0)
+        found = chosen[:8]
+        for k in range(1, 8):
+            found = found + chosen[8 * k : 8 * (k + 1)]
+        found = found[:4] + found[4:]
+        for k in range(GROUP):
+            row = k * LANES + slot * 4
+            stage[row : row + 4, :] = found[:, k * LANES : (k + 1) * LANES]
+    for c in range(4):
+        for k in range(GROUP):
+            at_grain[c * SLOTS : (c + 1) * SLOTS, k * LANES : (k + 1) * LANES] = stage[
+                pl.ds(k * LANES + c, SLOTS, stride=4), :
+            ]
 
 
 def owned_kernel(parcels, fluid, pressure, fluid_out, void_out):
@@ -454,11 +502,13 @@
 def advance(state, velocity, reach, at_grain, force, middle, got_lead, got_trail, hot):
     low = lower_half((3 * SLOTS, LANES))
     from_last, from_next = by_parity("gy", got_lead[...], got_trail[...])
+    last_whole, last_half = unfold(from_last, False)
+    next_whole, next_half = unfold(from_next, True)
     tiles = [
-        from_last[:, :LANES],
-        jnp.where(low, from_last[:, LANES:], middle[...]),
-        jnp.where(low, middle[...], from_next[:, :LANES]),
-        from_next[:, LANES:],
+        last_whole,
+        jnp.where(low, last_half, middle[...]),
+        jnp.where(low, middle[...], next_half),
+        next_whole,
     ]
     tiles = [jnp.where(present_tile(2 * k, 2 * k + 1), tiles[k], 0.0) for k in range(4)]
     returned = jnp.concatenate(tiles, axis=1)
@@ -484,7 +534,7 @@
 
 def middle_kernel(
     table, state, velocity, at_grain, force, middle, got_lead, got_trail, hot,
-    table_out, state_out, velocity_out, lead, trail,
+    table_out, state_out, velocity_out, lead, trail, middle_out,
 ):
     reach = table[3 * SLOTS :, :]
     places, speeds, weights = advance(
@@ -497,7 +547,7 @@
         state_out[c * SLOTS : (c + 1) * SLOTS] = places[c]
         velocity_out[c * SLOTS : (c + 1) * SLOTS] = speeds[c]
     state_out[3 * SLOTS :] = weights
-    send_pieces(moved, 3 * SLOTS, hot, lead, trail)
+    send_pieces(moved, 3 * SLOTS, hot, lead, trail, middle_out)
 
 
 def last_kernel(
@@ -584,8 +634,8 @@
     mask = grain_mask.reshape(CHUNKS, LANES)
     cell = grain_cell.reshape(CHUNKS, LANES)
 
-    full, wide = table_shape(4 * SLOTS), table_shape(4 * SLOTS, 2 * LANES)
-    narrow, single = table_shape(3 * SLOTS, 2 * LANES), table_shape(3 * SLOTS, LANES)
+    full, wide = table_shape(4 * SLOTS), table_shape(6 * SLOTS, LANES)
+    narrow, single = table_shape(9 * SLOTS // 2, LANES), table_shape(3 * SLOTS, LANES)
     three, full_tile = table_shape(3 * SLOTS), table_shape(4 * SLOTS, LANES)
 
     def near(array):
@@ -594,16 +644,25 @@
     def like(array):
         return jax.ShapeDtypeStruct(array.shape, array.dtype)
 
-    operands = (positions, radius, mask, send)
-    table, state, hot, lead, trail = call(
+    needed = (positions, radius, mask, send)
+    later = (velocity, cell, fluid_velocity, pressure_grad, inner_pairs, cross_pairs)
+    table, state, hot, lead, trail, middle, *later = call(
         prepare,
-        (full, full, jax.ShapeDtypeStruct((CLUSTERS, CLUSTERS), bf16), wide, wide),
-        operands,
-        [near(array) for array in operands] + [STAGE, pltpu.SemaphoreType.DMA((4,))],
+        (
+            full,
+            full,
+            jax.ShapeDtypeStruct((CLUSTERS, CLUSTERS), bf16),
+            wide,
+            wide,
+            full_tile,
+            *[like(array) for array in later],
+        ),
+        needed + later,
+        [near(array) for array in needed] + [STAGE, pltpu.SemaphoreType.DMA((10,))],
         far=True,
     )
-    operands = (velocity, radius, mask, cell, fluid_velocity, pressure_grad, inner_pairs, cross_pairs)
-    moving, cells, totals, stay, away, fluid, pressure, inner_pairs, cross_pairs = call(
+    velocity, cell, fluid, pressure, inner_pairs, cross_pairs = later
+    moving, cells, totals, stay, away = call(
         deposit_kernel,
         (
             three,
@@ -611,13 +670,10 @@
             table_shape(64, LANES),
             PARCELS,
             PARCELS,
-            *[like(array) for array in operands[4:]],
         ),
-        operands,
-        [near(array) for array in operands[:4]] + [STAGE, pltpu.SemaphoreType.DMA((8,))],
+        (table, state, velocity, cell, fluid, pressure),
+        [STAGE],
         3,
-        far=True,
-        after=(table,),
     )
     got = swap(away, 1)
 
@@ -635,7 +691,7 @@
         lead, trail, side = call(
             pass_ghosts,
             (wide, wide, full_tile) if first else (narrow, narrow, single),
-            (lead, trail, got_lead, got_trail),
+            (got_lead, got_trail, middle),
             after=(away,) if first else (rows[3],),
         )
         got_lead, got_trail = snake(lead, "gy", 1), snake(trail, "gy", -1)
@@ -692,7 +748,7 @@
                 fluid_kernel,
                 (full, jax.ShapeDtypeStruct((16, 8, LANES), f32)),
                 (totals, stay, got, cells),
-                (),
+                [pltpu.VMEM((GROUP * LANES, LANES), f32)],
                 3,
                 after=(lead, trail),
             )
@@ -705,8 +761,8 @@
             )
         operands = (table, state, moving, at_grain, force, middle, got_lead, got_trail, hot)
         if first:
-            table, state, moving, lead, trail = call(
-                middle_kernel, (full, full, three, narrow, narrow), operands
+            table, state, moving, lead, trail, middle = call(
+                middle_kernel, (full, full, three, narrow, narrow, single), operands
             )
         else:
             positions, velocity = call(

time: 69.2 us -> 66.4 us (0.960)
  Pallas kernels: 30.1 us -> 26.7 us
    pallas_call x23, Pallas kernels: 30.1 us -> 26.7 us  [call(): pl.pallas_call(body, out_shape=out_shape, in_specs=[pl.BlockSpec(memory_s...]
  transfers between devices with their start and end apart: 20 -> 20, of which waited for: 11 -> 12; matrix products, arithmetic and copies ran while one was open for 0% -> 0% of each run, Pallas kernels for 32% -> 28%
where the time goes in v4:
time: 66.4 us; the launch traced here: 66.3 us
  Pallas kernels  26.7 us (40%)
  starting transfers between devices  19.7 us (30%)
  waiting for transfers between devices  19 us (29%)
  between operations  0.83 us (1%)
    pallas_call x23, Pallas kernels, call(): pl.pallas_call(body, out_shape=out_shape, in_specs=[pl.BlockSpec(memory_s...  26.7 us
    ppermute x16, waiting for transfers between devices, snake(): return lax.ppermute(array, ('gx', 'gy'), moves)  17.3 us
    ppermute x16, starting transfers between devices, snake(): return lax.ppermute(array, ('gx', 'gy'), moves)  11 us
    ppermute x4, starting transfers between devices, swap(): return lax.ppermute(array, ('gx', 'gy'), moves)  8.7 us
    ppermute x4, waiting for transfers between devices, swap(): return lax.ppermute(array, ('gx', 'gy'), moves)  1.71 us
  transfers between devices with their start and end apart: 20, of which 12 were waited for; matrix products, arithmetic and copies ran while one was open for 0% of the time, Pallas kernels for 28%

profile of v4, /device:TPU:24, one launch (start us, length us, event | category | flops | bytes accessed | tf_op | source)
XLA Modules:
  0.0 66.3 jit_solution(12708198154863707113)
XLA Ops:
  0.6 1.7 %prepare.1 = (f32[128,512]{1,0:T(8,128)S(1)}, f32[128,512]{1,0:T(8,128)S(1)}, bf16[512,512]{1,0:T(8,128)(2,1)S(1)}, f32[192,128]{1,0:T(8,128)S(1)}, f32[192,128]...) custom-call(f32[3,16384]{1,0:T(4,128)} %refs_0_.1, ...), custom_call_target="tpu_custom_call" | custom-call | flops 1000000000 | bytes 1000000 | tf_op jit(solution)/shard_map/prepare/pallas_call | solution.py:606
  2.4 0.8 %collective-permute-start.1 = (f32[192,128]{1,0:T(8,128)S(1)}, f32[192,128]{1,0:T(8,128)S(1)}, u32[]{:S(2)}, u32[]{:S(2)}) collective-permute-start(f32[192,128]{1,0:T(8,128)S(1)} %get-tuple-element.87), channel_id=1, source_target_pairs={{0,16},{1,0},{2,18},{3,2},{4,20},{5,4},{6,22},{7,6},{8,24},{9,8},{... | collective-permute-start | bytes 294920 | tf_op jit(solution)/shard_map/ppermute | solution.py:576
  3.2 1.5 %deposit_kernel.1 = (f32[96,512]{1,0:T(8,128)S(1)}, s32[32,512]{1,0:T(8,128)S(1)}, f32[64,128]{1,0:T(8,128)S(1)}, f32[8,8,128]{2,1,0:T(8,128)S(1)}, f32[8,8,128]{2,1,0:T(8,128)S(1)}) custom-call(f32[128,512]{1,0:T(8,128)S(1)} %get-tuple-element.77.refs_0_, f32[128,512]{1,0:T(8,128)S(1)} %get-tuple-element.78.refs_1_, ...), custom_call_target="tpu_custom_call" | custom-call | flops 3000000000 | bytes 3000000 | tf_op jit(solution)/shard_map/deposit_kernel/pallas_call | solution.py:606
  4.7 2.1 %collective-permute-start = (f32[8,8,128]{2,1,0:T(8,128)S(1)}, f32[8,8,128]{2,1,0:T(8,128)S(1)}, u32[]{:S(2)}, u32[]{:S(2)}) collective-permute-start(f32[8,8,128]{2,1,0:T(8,128)S(1)} %get-tuple-element.86.refs_3_), channel_id=1, source_target_pairs={{0,1},{1,0},{2,3},{3,2},{4,5},{5,4},{6,7},{7,6},{8,9},{9,8},{10,11... | collective-permute-start | bytes 98312 | tf_op jit(solution)/shard_map/ppermute | solution.py:582
  6.8 1.0 %collective-permute-done.2.refs_1_ = f32[192,128]{1,0:T(8,128)S(1)} collective-permute-done((f32[192,128]{1,0:T(8,128)S(1)}, f32[192,128]{1,0:T(8,128)S(1)}, u32[]{:S(2)}, u32[]{:S(2)}) %collective-permute-start.2) | collective-permute-done | bytes 98336 | tf_op jit(solution)/shard_map/ppermute | solution.py:576
  7.9 0.9 %collective-permute-start.5 = (f32[192,128]{1,0:T(8,128)S(1)}, f32[192,128]{1,0:T(8,128)S(1)}, u32[]{:S(2)}, u32[]{:S(2)}) collective-permute-start(f32[192,128]{1,0:T(8,128)S(1)} %get-tuple-element.90.refs_2_), channel_id=1, source_target_pairs={{0,1},{1,2},{2,3},{3,4},{4,5},{5,6},{6,7},{7,8},{8,9},{9,10},{10,1... | collective-permute-start | bytes 294920 | tf_op jit(solution)/shard_map/ppermute | solution.py:576
  8.8 1.2 %collective-permute-start.6 = (f32[192,128]{1,0:T(8,128)S(1)}, f32[192,128]{1,0:T(8,128)S(1)}, u32[]{:S(2)}, u32[]{:S(2)}) collective-permute-start(f32[192,128]{1,0:T(8,128)S(1)} %get-tuple-element.91.refs_3_), channel_id=1, source_target_pairs={{0,16},{1,0},{2,1},{3,2},{4,3},{5,4},{6,5},{7,6},{8,7},{9,8},{10,9... | collective-permute-start | bytes 294920 | tf_op jit(solution)/shard_map/ppermute | solution.py:576
  10.0 0.9 %collective-permute-start.3 = (f32[8,8,128]{2,1,0:T(8,128)S(1)}, f32[8,8,128]{2,1,0:T(8,128)S(1)}, u32[]{:S(2)}, u32[]{:S(2)}) collective-permute-start(f32[8,8,128]{2,1,0:T(8,128)S(1)} %get-tuple-element.93.refs_2_), channel_id=1, source_target_pairs={{0,2},{1,3},{2,0},{3,1},{4,6},{5,7},{6,4},{7,5},{8,10},{9,11},{10,... | collective-permute-start | bytes 98312 | tf_op jit(solution)/shard_map/ppermute | solution.py:582
  11.0 2.2 %inner_start.1 = (bf16[512,1024]{1,0:T(8,128)(2,1)S(1)}, bf16[512,1024]{1,0:T(8,128)(2,1)S(1)}, f32[1024,128]{1,0:T(8,128)S(1)}, f32[1024,128]{1,0:T(8,128)S(1)}...) custom-call(f32[128,512]{1,0:T(8,128)S(1)} %get-tuple-element.77.refs_0_, s32[5,1024]{1,0:T(8,128)S(1)} %get-tuple-element.95.refs_1_, ...), custom_call_target="tpu_custom_call" | custom-call | flops 3000000000 | bytes 3000000 | tf_op jit(solution)/shard_map/inner_start/pallas_call | solution.py:606
  13.8 1.7 %collective-permute-done.3.refs_1_ = f32[8,8,128]{2,1,0:T(8,128)S(1)} collective-permute-done((f32[8,8,128]{2,1,0:T(8,128)S(1)}, f32[8,8,128]{2,1,0:T(8,128)S(1)}, u32[]{:S(2)}, u32[]{:S(2)}) %collective-permute-start.3) | collective-permute-done | bytes 32800 | tf_op jit(solution)/shard_map/ppermute | solution.py:582
  15.5 2.0 %collective-permute-start.4 = (f32[8,8,128]{2,1,0:T(8,128)S(1)}, f32[8,8,128]{2,1,0:T(8,128)S(1)}, u32[]{:S(2)}, u32[]{:S(2)}) collective-permute-start(f32[8,8,128]{2,1,0:T(8,128)S(1)} %get-tuple-element.99.refs_5_), channel_id=1, source_target_pairs={{0,4},{1,5},{2,6},{3,7},{4,0},{5,1},{6,2},{7,3},{8,12},{9,13},{10,... | collective-permute-start | bytes 98312 | tf_op jit(solution)/shard_map/ppermute | solution.py:582
  17.5 4.0 %cross_kernel.1 = (f32[768,128]{1,0:T(8,128)S(1)}, f32[144,128]{1,0:T(8,128)S(1)}, f32[144,128]{1,0:T(8,128)S(1)}, f32[96,128]{1,0:T(8,128)S(1)}, f32[32,512]{1,0:T(8,128)S(1)}) custom-call(f32[1024,128]{1,0:T(8,128)S(1)} %get-tuple-element.97.refs_2_.refs_0_, bf16[512,1024]{1,0:T(8,128)(2,1)S(1)} %get-tuple-element.100.refs_1_, ...), custom_call_target="tpu_custom_call" | custom-call | flops 4000000000 | bytes 4000000 | tf_op jit(solution)/shard_map/cross_kernel/pallas_call | solution.py:606
  21.6 3.7 %collective-permute-start.7 = (f32[8,8,128]{2,1,0:T(8,128)S(1)}, f32[8,8,128]{2,1,0:T(8,128)S(1)}, u32[]{:S(2)}, u32[]{:S(2)}) collective-permute-start(f32[8,8,128]{2,1,0:T(8,128)S(1)} %get-tuple-element.104.refs_4_), channel_id=1, source_target_pairs={{0,8},{1,9},{2,10},{3,11},{4,12},{5,13},{6,14},{7,15},{8,0},{9,1},... | collective-permute-start | bytes 98312 | tf_op jit(solution)/shard_map/ppermute | solution.py:582
  25.3 0.8 %collective-permute-start.8 = (f32[144,128]{1,0:T(8,128)S(1)}, f32[144,128]{1,0:T(8,128)S(1)}, u32[]{:S(2)}, u32[]{:S(2)}) collective-permute-start(f32[144,128]{1,0:T(8,128)S(1)} %get-tuple-element.106), channel_id=1, source_target_pairs={{0,1},{1,2},{2,3},{3,4},{4,5},{5,6},{6,7},{7,8},{8,9},{9,10},{10,1... | collective-permute-start | bytes 221192 | tf_op jit(solution)/shard_map/ppermute | solution.py:576
  26.1 1.2 %collective-permute-start.9 = (f32[144,128]{1,0:T(8,128)S(1)}, f32[144,128]{1,0:T(8,128)S(1)}, u32[]{:S(2)}, u32[]{:S(2)}) collective-permute-start(f32[144,128]{1,0:T(8,128)S(1)} %get-tuple-element.107), channel_id=1, source_target_pairs={{0,16},{1,0},{2,1},{3,2},{4,3},{5,4},{6,5},{7,6},{8,7},{9,8},{10,9... | collective-permute-start | bytes 221192 | tf_op jit(solution)/shard_map/ppermute | solution.py:576
  27.3 1.5 %inner_rest.2 = (f32[768,128]{1,0:T(8,128)S(1)}, f32[768,128]{1,0:T(8,128)S(1)}) custom-call(f32[1024,128]{1,0:T(8,128)S(1)} %get-tuple-element.108.refs_0_, f32[1024,128]{1,0:T(8,128)S(1)} %get-tuple-element.109.refs_1_, f32[768,128]{1,0:T(8,128)S(1)} %get-tuple-element.110.refs_2_, f32[768,128]{1,0:T(8,128)S(1)} %get-tuple-element.96.refs_2_.refs_3_, ...), custom_call_target="tpu_custom_call" | custom-call | flops 2000000000 | bytes 2000000 | tf_op jit(solution)/shard_map/inner_rest/pallas_call | solution.py:606
  28.8 1.2 %scatter_kernel.2.refs_3_.refs_4_ = f32[96,512]{1,0:T(8,128)S(1)} custom-call(f32[768,128]{1,0:T(8,128)S(1)} %get-tuple-element.111.refs_0_, f32[768,128]{1,0:T(8,128)S(1)} %get-tuple-element.112.refs_1_, f32[768,128]{1,0:T(8,128)S(1)} %get-tuple-element.113.refs_2_, bf16[512,1024]{1,0:T(8,128)(2,1)S(1)} %get-tuple-element.114.refs_3_.refs_2_, ...), custom_call_target="tpu_custom_call" | custom-call | flops 2000000000 | bytes 2000000 | tf_op jit(solution)/shard_map/scatter_kernel/pallas_call | solution.py:606
  30.0 2.6 %collective-permute-done.9.refs_1_ = f32[144,128]{1,0:T(8,128)S(1)} collective-permute-done((f32[144,128]{1,0:T(8,128)S(1)}, f32[144,128]{1,0:T(8,128)S(1)}, u32[]{:S(2)}, u32[]{:S(2)}) %collective-permute-start.9) | collective-permute-done | bytes 73760 | tf_op jit(solution)/shard_map/ppermute | solution.py:576
  33.3 1.3 %fluid_kernel.1 = (f32[128,512]{1,0:T(8,128)S(1)}, f32[16,8,128]{2,1,0:T(8,128)S(1)}) custom-call(f32[64,128]{1,0:T(8,128)S(1)} %get-tuple-element.84.refs_0_, f32[8,8,128]{2,1,0:T(8,128)S(1)} %get-tuple-element.103.refs_1_, f32[8,8,128]{2,1,0:T(8,128)S(1)} %collective-permute-done.7.refs_2_, s32[32,512]{1,0:T(8,128)S(1)} %get-tuple-element.105.refs_3_, ...), custom_call_target="tpu_custom_call" | custom-call | flops 3000000000 | bytes 3000000 | tf_op jit(solution)/shard_map/fluid_kernel/pallas_call | solution.py:606
  34.7 2.5 %collective-permute-done.11.refs_7_ = f32[144,128]{1,0:T(8,128)S(1)} collective-permute-done((f32[144,128]{1,0:T(8,128)S(1)}, f32[144,128]{1,0:T(8,128)S(1)}, u32[]{:S(2)}, u32[]{:S(2)}) %collective-permute-start.11) | collective-permute-done | bytes 73760 | tf_op jit(solution)/shard_map/ppermute | solution.py:576
  38.7 2.2 %inner_again.1 = (f32[1024,128]{1,0:T(8,128)S(1)}, f32[1024,128]{1,0:T(8,128)S(1)}, f32[768,128]{1,0:T(8,128)S(1)}, f32[768,128]{1,0:T(8,128)S(1)}) custom-call(f32[128,512]{1,0:T(8,128)S(1)} %get-tuple-element.122.refs_0_, s32[5,1024]{1,0:T(8,128)S(1)} %get-tuple-element.95.refs_1_, bf16[512,1024]{1,0:T(8,128)(2,1)S(1)} %get-tuple-element.114.refs_3_.refs_2_, ...), custom_call_target="tpu_custom_call" | custom-call | flops 3000000000 | bytes 3000000 | tf_op jit(solution)/shard_map/inner_again/pallas_call | solution.py:606
  40.9 1.7 %collective-permute-done.13.refs_1_ = f32[144,128]{1,0:T(8,128)S(1)} collective-permute-done((f32[144,128]{1,0:T(8,128)S(1)}, f32[144,128]{1,0:T(8,128)S(1)}, u32[]{:S(2)}, u32[]{:S(2)}) %collective-permute-start.13) | collective-permute-done | bytes 73760 | tf_op jit(solution)/shard_map/ppermute | solution.py:576
  43.1 1.7 %collective-permute-start.15 = (f32[144,128]{1,0:T(8,128)S(1)}, f32[144,128]{1,0:T(8,128)S(1)}, u32[]{:S(2)}, u32[]{:S(2)}) collective-permute-start(f32[144,128]{1,0:T(8,128)S(1)} %get-tuple-element.133.refs_4_), channel_id=1, source_target_pairs={{0,16},{1,0},{2,1},{3,2},{4,3},{5,4},{6,5},{7,6},{8,7},{9,8},{10,9... | collective-permute-start | bytes 221192 | tf_op jit(solution)/shard_map/ppermute | solution.py:576
  45.3 1.5 %inner_rest.3 = (f32[768,128]{1,0:T(8,128)S(1)}, f32[768,128]{1,0:T(8,128)S(1)}) custom-call(f32[1024,128]{1,0:T(8,128)S(1)} %get-tuple-element.125.refs_0_, f32[1024,128]{1,0:T(8,128)S(1)} %get-tuple-element.126.refs_1_, f32[768,128]{1,0:T(8,128)S(1)} %get-tuple-element.127.refs_2_, f32[768,128]{1,0:T(8,128)S(1)} %get-tuple-element.128.refs_3_, ...), custom_call_target="tpu_custom_call" | custom-call | flops 2000000000 | bytes 2000000 | tf_op jit(solution)/shard_map/inner_rest/pallas_call | solution.py:606
  47.1 2.4 %collective-permute-done.15.refs_3_ = f32[144,128]{1,0:T(8,128)S(1)} collective-permute-done((f32[144,128]{1,0:T(8,128)S(1)}, f32[144,128]{1,0:T(8,128)S(1)}, u32[]{:S(2)}, u32[]{:S(2)}) %collective-permute-start.15) | collective-permute-done | bytes 73760 | tf_op jit(solution)/shard_map/ppermute | solution.py:576
  49.6 4.0 %cross_kernel_again.1 = (f32[768,128]{1,0:T(8,128)S(1)}, f32[144,128]{1,0:T(8,128)S(1)}, f32[144,128]{1,0:T(8,128)S(1)}, f32[96,128]{1,0:T(8,128)S(1)}) custom-call(f32[1024,128]{1,0:T(8,128)S(1)} %cross_again.1.refs_4_.refs_0_, bf16[512,1024]{1,0:T(8,128)(2,1)S(1)} %get-tuple-element.100.refs_1_, f32[144,128]{1,0:T(8,128)S(1)} %collective-permute-done.14.refs_2_, ...), custom_call_target="tpu_custom_call" | custom-call | flops 4000000000 | bytes 4000000 | tf_op jit(solution)/shard_map/cross_kernel_again/pallas_call | solution.py:606
  53.7 2.0 %collective-permute-start.17 = (f32[144,128]{1,0:T(8,128)S(1)}, f32[144,128]{1,0:T(8,128)S(1)}, u32[]{:S(2)}, u32[]{:S(2)}) collective-permute-start(f32[144,128]{1,0:T(8,128)S(1)} %get-tuple-element.141), channel_id=1, source_target_pairs={{0,16},{1,0},{2,1},{3,2},{4,3},{5,4},{6,5},{7,6},{8,7},{9,8},{10,9... | collective-permute-start | bytes 221192 | tf_op jit(solution)/shard_map/ppermute | solution.py:576
  55.7 1.2 %scatter_kernel.3.refs_3_.refs_4_ = f32[96,512]{1,0:T(8,128)S(1)} custom-call(f32[768,128]{1,0:T(8,128)S(1)} %get-tuple-element.134.refs_0_, f32[768,128]{1,0:T(8,128)S(1)} %get-tuple-element.135.refs_6_.refs_1_, f32[768,128]{1,0:T(8,128)S(1)} %get-tuple-element.138.refs_2_, bf16[512,1024]{1,0:T(8,128)(2,1)S(1)} %get-tuple-element.114.refs_3_.refs_2_, ...), custom_call_target="tpu_custom_call" | custom-call | flops 2000000000 | bytes 2000000 | tf_op jit(solution)/shard_map/scatter_kernel/pallas_call | solution.py:606
  56.9 1.1 %collective-permute-done.16.refs_0_ = f32[144,128]{1,0:T(8,128)S(1)} collective-permute-done((f32[144,128]{1,0:T(8,128)S(1)}, f32[144,128]{1,0:T(8,128)S(1)}, u32[]{:S(2)}, u32[]{:S(2)}) %collective-permute-start.16) | collective-permute-done | bytes 73760 | tf_op jit(solution)/shard_map/ppermute | solution.py:576
  58.0 2.2 %collective-permute-done.17.refs_1_ = f32[144,128]{1,0:T(8,128)S(1)} collective-permute-done((f32[144,128]{1,0:T(8,128)S(1)}, f32[144,128]{1,0:T(8,128)S(1)}, u32[]{:S(2)}, u32[]{:S(2)}) %collective-permute-start.17) | collective-permute-done | bytes 73760 | tf_op jit(solution)/shard_map/ppermute | solution.py:576
  62.4 2.5 %collective-permute-done.19.refs_7_ = f32[144,128]{1,0:T(8,128)S(1)} collective-permute-done((f32[144,128]{1,0:T(8,128)S(1)}, f32[144,128]{1,0:T(8,128)S(1)}, u32[]{:S(2)}, u32[]{:S(2)}) %collective-permute-start.19) | collective-permute-done | bytes 73760 | tf_op jit(solution)/shard_map/ppermute | solution.py:576
  64.8 1.4 %last_kernel.1 = (f32[3,16384]{1,0:T(4,128)}, f32[3,16384]{1,0:T(4,128)}) custom-call(f32[128,512]{1,0:T(8,128)S(1)} %get-tuple-element.122.refs_0_, f32[128,512]{1,0:T(8,128)S(1)} %get-tuple-element.123.refs_1_, f32[96,512]{1,0:T(8,128)S(1)} %get-tuple-element.124.refs_2_, f32[128,512]{1,0:T(8,128)S(1)} %get-tuple-element.119.refs_3_, ...), custom_call_target="tpu_custom_call" | custom-call | flops 1000000000 | bytes 1000000 | tf_op jit(solution)/shard_map/last_kernel/pallas_call | solution.py:606
  (31 shorter events, 6.7 us)
Async XLA Ops:
  2.4 4.4 %collective-permute-start.1 = (f32[192,128]{1,0:T(8,128)S(1)}, f32[192,128]{1,0:T(8,128)S(1)}, u32[]{:S(2)}, u32[]{:S(2)}) collective-permute-start(f32[192,128]{1,0:T(8,128)S(1)} %get-tuple-element.87), channel_id=1, source_target_pairs={{0,16},{1,0},{2,18},{3,2},{4,20},{5,4},{6,22},{7,6},{8,24},{9,8},{... | collective-permute-start | bytes 294920 | tf_op jit(solution)/shard_map/ppermute | solution.py:576
  3.2 4.6 %collective-permute-start.2 = (f32[192,128]{1,0:T(8,128)S(1)}, f32[192,128]{1,0:T(8,128)S(1)}, u32[]{:S(2)}, u32[]{:S(2)}) collective-permute-start(f32[192,128]{1,0:T(8,128)S(1)} %get-tuple-element.88), channel_id=1, source_target_pairs={{0,1},{1,17},{2,3},{3,19},{4,5},{5,21},{6,7},{7,23},{8,9},{9,25},{... | collective-permute-start | bytes 294920 | tf_op jit(solution)/shard_map/ppermute | solution.py:576
  4.7 5.3 %collective-permute-start = (f32[8,8,128]{2,1,0:T(8,128)S(1)}, f32[8,8,128]{2,1,0:T(8,128)S(1)}, u32[]{:S(2)}, u32[]{:S(2)}) collective-permute-start(f32[8,8,128]{2,1,0:T(8,128)S(1)} %get-tuple-element.86.refs_3_), channel_id=1, source_target_pairs={{0,1},{1,0},{2,3},{3,2},{4,5},{5,4},{6,7},{7,6},{8,9},{9,8},{10,11... | collective-permute-start | bytes 98312 | tf_op jit(solution)/shard_map/ppermute | solution.py:582
  7.9 9.6 %collective-permute-start.5 = (f32[192,128]{1,0:T(8,128)S(1)}, f32[192,128]{1,0:T(8,128)S(1)}, u32[]{:S(2)}, u32[]{:S(2)}) collective-permute-start(f32[192,128]{1,0:T(8,128)S(1)} %get-tuple-element.90.refs_2_), channel_id=1, source_target_pairs={{0,1},{1,2},{2,3},{3,4},{4,5},{5,6},{6,7},{7,8},{8,9},{9,10},{10,1... | collective-permute-start | bytes 294920 | tf_op jit(solution)/shard_map/ppermute | solution.py:576
  8.8 8.7 %collective-permute-start.6 = (f32[192,128]{1,0:T(8,128)S(1)}, f32[192,128]{1,0:T(8,128)S(1)}, u32[]{:S(2)}, u32[]{:S(2)}) collective-permute-start(f32[192,128]{1,0:T(8,128)S(1)} %get-tuple-element.91.refs_3_), channel_id=1, source_target_pairs={{0,16},{1,0},{2,1},{3,2},{4,3},{5,4},{6,5},{7,6},{8,7},{9,8},{10,9... | collective-permute-start | bytes 294920 | tf_op jit(solution)/shard_map/ppermute | solution.py:576
  10.0 5.5 %collective-permute-start.3 = (f32[8,8,128]{2,1,0:T(8,128)S(1)}, f32[8,8,128]{2,1,0:T(8,128)S(1)}, u32[]{:S(2)}, u32[]{:S(2)}) collective-permute-start(f32[8,8,128]{2,1,0:T(8,128)S(1)} %get-tuple-element.93.refs_2_), channel_id=1, source_target_pairs={{0,2},{1,3},{2,0},{3,1},{4,6},{5,7},{6,4},{7,5},{8,10},{9,11},{10,... | collective-permute-start | bytes 98312 | tf_op jit(solution)/shard_map/ppermute | solution.py:582
  15.5 6.0 %collective-permute-start.4 = (f32[8,8,128]{2,1,0:T(8,128)S(1)}, f32[8,8,128]{2,1,0:T(8,128)S(1)}, u32[]{:S(2)}, u32[]{:S(2)}) collective-permute-start(f32[8,8,128]{2,1,0:T(8,128)S(1)} %get-tuple-element.99.refs_5_), channel_id=1, source_target_pairs={{0,4},{1,5},{2,6},{3,7},{4,0},{5,1},{6,2},{7,3},{8,12},{9,13},{10,... | collective-permute-start | bytes 98312 | tf_op jit(solution)/shard_map/ppermute | solution.py:582
  21.6 11.7 %collective-permute-start.7 = (f32[8,8,128]{2,1,0:T(8,128)S(1)}, f32[8,8,128]{2,1,0:T(8,128)S(1)}, u32[]{:S(2)}, u32[]{:S(2)}) collective-permute-start(f32[8,8,128]{2,1,0:T(8,128)S(1)} %get-tuple-element.104.refs_4_), channel_id=1, source_target_pairs={{0,8},{1,9},{2,10},{3,11},{4,12},{5,13},{6,14},{7,15},{8,0},{9,1},... | collective-permute-start | bytes 98312 | tf_op jit(solution)/shard_map/ppermute | solution.py:582
  25.3 4.7 %collective-permute-start.8 = (f32[144,128]{1,0:T(8,128)S(1)}, f32[144,128]{1,0:T(8,128)S(1)}, u32[]{:S(2)}, u32[]{:S(2)}) collective-permute-start(f32[144,128]{1,0:T(8,128)S(1)} %get-tuple-element.106), channel_id=1, source_target_pairs={{0,1},{1,2},{2,3},{3,4},{4,5},{5,6},{6,7},{7,8},{8,9},{9,10},{10,1... | collective-permute-start | bytes 221192 | tf_op jit(solution)/shard_map/ppermute | solution.py:576
  26.1 6.5 %collective-permute-start.9 = (f32[144,128]{1,0:T(8,128)S(1)}, f32[144,128]{1,0:T(8,128)S(1)}, u32[]{:S(2)}, u32[]{:S(2)}) collective-permute-start(f32[144,128]{1,0:T(8,128)S(1)} %get-tuple-element.107), channel_id=1, source_target_pairs={{0,16},{1,0},{2,1},{3,2},{4,3},{5,4},{6,5},{7,6},{8,7},{9,8},{10,9... | collective-permute-start | bytes 221192 | tf_op jit(solution)/shard_map/ppermute | solution.py:576
  32.7 2.1 %collective-permute-start.10 = (f32[144,128]{1,0:T(8,128)S(1)}, f32[144,128]{1,0:T(8,128)S(1)}, u32[]{:S(2)}, u32[]{:S(2)}) collective-permute-start(f32[144,128]{1,0:T(8,128)S(1)} %get-tuple-element.117.refs_4_), channel_id=1, source_target_pairs={{0,16},{1,0},{2,18},{3,2},{4,20},{5,4},{6,22},{7,6},{8,24},{9,8},{... | collective-permute-start | bytes 221192 | tf_op jit(solution)/shard_map/ppermute | solution.py:576
  32.8 4.4 %collective-permute-start.11 = (f32[144,128]{1,0:T(8,128)S(1)}, f32[144,128]{1,0:T(8,128)S(1)}, u32[]{:S(2)}, u32[]{:S(2)}) collective-permute-start(f32[144,128]{1,0:T(8,128)S(1)} %get-tuple-element.118.refs_5_), channel_id=1, source_target_pairs={{0,1},{1,17},{2,3},{3,19},{4,5},{5,21},{6,7},{7,23},{8,9},{9,25},{... | collective-permute-start | bytes 221192 | tf_op jit(solution)/shard_map/ppermute | solution.py:576
  37.9 3.0 %collective-permute-start.12 = (f32[144,128]{1,0:T(8,128)S(1)}, f32[144,128]{1,0:T(8,128)S(1)}, u32[]{:S(2)}, u32[]{:S(2)}) collective-permute-start(f32[144,128]{1,0:T(8,128)S(1)} %get-tuple-element.129), channel_id=1, source_target_pairs={{0,16},{1,0},{2,18},{3,2},{4,20},{5,4},{6,22},{7,6},{8,24},{9,8},{... | collective-permute-start | bytes 221192 | tf_op jit(solution)/shard_map/ppermute | solution.py:576
  38.2 4.4 %collective-permute-start.13 = (f32[144,128]{1,0:T(8,128)S(1)}, f32[144,128]{1,0:T(8,128)S(1)}, u32[]{:S(2)}, u32[]{:S(2)}) collective-permute-start(f32[144,128]{1,0:T(8,128)S(1)} %get-tuple-element.130), channel_id=1, source_target_pairs={{0,1},{1,17},{2,3},{3,19},{4,5},{5,21},{6,7},{7,23},{8,9},{9,25},{... | collective-permute-start | bytes 221192 | tf_op jit(solution)/shard_map/ppermute | solution.py:576
  42.7 4.4 %collective-permute-start.14 = (f32[144,128]{1,0:T(8,128)S(1)}, f32[144,128]{1,0:T(8,128)S(1)}, u32[]{:S(2)}, u32[]{:S(2)}) collective-permute-start(f32[144,128]{1,0:T(8,128)S(1)} %get-tuple-element.132.refs_3_), channel_id=1, source_target_pairs={{0,1},{1,2},{2,3},{3,4},{4,5},{5,6},{6,7},{7,8},{8,9},{9,10},{10,1... | collective-permute-start | bytes 221192 | tf_op jit(solution)/shard_map/ppermute | solution.py:576
  43.1 6.5 %collective-permute-start.15 = (f32[144,128]{1,0:T(8,128)S(1)}, f32[144,128]{1,0:T(8,128)S(1)}, u32[]{:S(2)}, u32[]{:S(2)}) collective-permute-start(f32[144,128]{1,0:T(8,128)S(1)} %get-tuple-element.133.refs_4_), channel_id=1, source_target_pairs={{0,16},{1,0},{2,1},{3,2},{4,3},{5,4},{6,5},{7,6},{8,7},{9,8},{10,9... | collective-permute-start | bytes 221192 | tf_op jit(solution)/shard_map/ppermute | solution.py:576
  53.6 4.4 %collective-permute-start.16 = (f32[144,128]{1,0:T(8,128)S(1)}, f32[144,128]{1,0:T(8,128)S(1)}, u32[]{:S(2)}, u32[]{:S(2)}) collective-permute-start(f32[144,128]{1,0:T(8,128)S(1)} %get-tuple-element.140), channel_id=1, source_target_pairs={{0,1},{1,2},{2,3},{3,4},{4,5},{5,6},{6,7},{7,8},{8,9},{9,10},{10,1... | collective-permute-start | bytes 221192 | tf_op jit(solution)/shard_map/ppermute | solution.py:576
  53.7 6.5 %collective-permute-start.17 = (f32[144,128]{1,0:T(8,128)S(1)}, f32[144,128]{1,0:T(8,128)S(1)}, u32[]{:S(2)}, u32[]{:S(2)}) collective-permute-start(f32[144,128]{1,0:T(8,128)S(1)} %get-tuple-element.141), channel_id=1, source_target_pairs={{0,16},{1,0},{2,1},{3,2},{4,3},{5,4},{6,5},{7,6},{8,7},{9,8},{10,9... | collective-permute-start | bytes 221192 | tf_op jit(solution)/shard_map/ppermute | solution.py:576
  60.3 2.1 %collective-permute-start.18 = (f32[144,128]{1,0:T(8,128)S(1)}, f32[144,128]{1,0:T(8,128)S(1)}, u32[]{:S(2)}, u32[]{:S(2)}) collective-permute-start(f32[144,128]{1,0:T(8,128)S(1)} %get-tuple-element.143.refs_3_), channel_id=1, source_target_pairs={{0,16},{1,0},{2,18},{3,2},{4,20},{5,4},{6,22},{7,6},{8,24},{9,8},{... | collective-permute-start | bytes 221192 | tf_op jit(solution)/shard_map/ppermute | solution.py:576
  60.4 4.4 %collective-permute-start.19 = (f32[144,128]{1,0:T(8,128)S(1)}, f32[144,128]{1,0:T(8,128)S(1)}, u32[]{:S(2)}, u32[]{:S(2)}) collective-permute-start(f32[144,128]{1,0:T(8,128)S(1)} %get-tuple-element.144.refs_4_), channel_id=1, source_target_pairs={{0,1},{1,17},{2,3},{3,19},{4,5},{5,21},{6,7},{7,23},{8,9},{9,25},{... | collective-permute-start | bytes 221192 | tf_op jit(solution)/shard_map/ppermute | solution.py:576

commit v5 on v4

--- a/solution.py
+++ b/solution.py
@@ -16,6 +16,9 @@
 GROUP = 4
 NEIGHBOURS = ((-1, -1), (-1, 0), (-1, 1), (0, -1), (0, 1), (1, -1), (1, 0), (1, 1))
 GHOST_ORDER = (7, 2, 3, 4, 5, 0, 1, 6)
+PAIRED = ("gx", "gy")
+OTHER = {"gx": "gy", "gy": "gx"}
+BITS = (1, 4, 2, 8)
 FAR = 2.0**30
 
 spring = 4.0
@@ -106,6 +109,16 @@
     )
 
 
+def outgoing(axis, up, down):
+    if axis in PAIRED:
+        return by_parity(axis, down, up)
+    return by_parity(OTHER[axis], up, down)
+
+
+def incoming(axis, lead, trail):
+    return by_parity(axis if axis in PAIRED else OTHER[axis], lead, trail)
+
+
 def to_table(square):
     turned = square.T
     return jnp.concatenate([turned[k * SLOTS : (k + 1) * SLOTS] for k in range(GROUP)], axis=1)
@@ -142,7 +155,7 @@
     tiles = [pieces[:, k * LANES : (k + 1) * LANES] for k in range(4)]
     up = fold(tiles[3], tiles[2], True)
     down = fold(tiles[0], tiles[1], False)
-    lead[...], trail[...] = by_parity("gy", up, down)
+    lead[...], trail[...] = outgoing("gx", up, down)
     middle[...] = jnp.where(lower_half(tiles[1].shape), tiles[2], tiles[1])
 
 
@@ -320,12 +333,12 @@
 
 def pass_ghosts(got_lead, got_trail, middle, lead_out, trail_out, side):
     low = lower_half(middle.shape)
-    from_last, from_next = by_parity("gy", got_lead[...], got_trail[...])
+    from_last, from_next = incoming("gx", got_lead[...], got_trail[...])
     last_whole, last_half = unfold(from_last, True)
     next_whole, next_half = unfold(from_next, False)
     minus = fold(jnp.where(low, next_whole, last_half), middle[...], True)
     plus = fold(jnp.where(low, next_half, last_whole), middle[...], False)
-    lead_out[...], trail_out[...] = by_parity("gx", plus, minus)
+    lead_out[...], trail_out[...] = outgoing("gy", plus, minus)
     side[...] = jnp.where(low, last_whole, next_whole)
 
 
@@ -337,12 +350,12 @@
     tiles = [back[:, k * LANES : (k + 1) * LANES] for k in range(4)]
     up = fold(tiles[0], tiles[1], True)
     down = fold(tiles[2], tiles[1], False)
-    lead[...], trail[...] = by_parity("gx", up, down)
+    lead[...], trail[...] = outgoing("gy", up, down)
     side_out[...] = tiles[3]
 
 
 def ghost_places(got_lead, got_trail, side):
-    from_last, from_next = by_parity("gx", got_lead[...], got_trail[...])
+    from_last, from_next = incoming("gy", got_lead[...], got_trail[...])
     last_whole, last_half = unfold(from_last, False)
     next_whole, next_half = unfold(from_next, True)
     low = lower_half(side.shape)
@@ -378,12 +391,12 @@
 
 def pass_forces(got_lead, got_trail, side, lead_out, trail_out, middle):
     low = lower_half((3 * SLOTS, LANES))
-    from_last, from_next = by_parity("gx", got_lead[...], got_trail[...])
+    from_last, from_next = incoming("gy", got_lead[...], got_trail[...])
     last_whole, last_half = unfold(from_last, True)
     next_whole, next_half = unfold(from_next, False)
     up = fold(jnp.where(low, last_whole, side[...]), next_whole, False)
     down = fold(jnp.where(low, side[...], next_whole), last_whole, True)
-    lead_out[...], trail_out[...] = by_parity("gy", up, down)
+    lead_out[...], trail_out[...] = outgoing("gx", up, down)
     middle[...] = jnp.where(low, next_half, last_half)
 
 
@@ -403,9 +416,9 @@
     return parcels
 
 
-def relay(bit):
+def relay(step):
     def relay_parcels(stay, got, stay_out, away_out):
-        part_parcels(join_parcels(stay, got, bit), 2 * bit, stay_out, away_out)
+        part_parcels(join_parcels(stay, got, BITS[step]), BITS[step + 1], stay_out, away_out)
 
     return relay_parcels
 
@@ -447,11 +460,11 @@
                 axis=0,
             )
         )
-    part_parcels(parcels, 1, stay, away)
+    part_parcels(parcels, BITS[0], stay, away)
 
 
 def fluid_kernel(totals, stay, got, cell, at_grain, parcels_out, stage):
-    parcels = join_parcels(stay, got, 8)
+    parcels = join_parcels(stay, got, BITS[3])
     for source in range(16):
         parcels_out[source] = parcels[source]
     volume = totals[:16]
@@ -501,7 +514,7 @@
 
 def advance(state, velocity, reach, at_grain, force, middle, got_lead, got_trail, hot):
     low = lower_half((3 * SLOTS, LANES))
-    from_last, from_next = by_parity("gy", got_lead[...], got_trail[...])
+    from_last, from_next = incoming("gx", got_lead[...], got_trail[...])
     last_whole, last_half = unfold(from_last, False)
     next_whole, next_half = unfold(from_next, True)
     tiles = [
@@ -561,19 +574,22 @@
     store_components(velocity_out, stage, jnp.concatenate(speeds, axis=0))
 
 
-def snake(array, axis, sign):
+def exchange(lead, trail, axis):
     size_x, size_y = lax.axis_size("gx"), lax.axis_size("gy")
-    moves = []
+    routes = ([], [])
     for x in range(size_x):
         for y in range(size_y):
-            if axis == "gx":
-                target = (x + (sign if y % 2 == 0 else -sign), y)
-                target = target if 0 <= target[0] < size_x else (x, y ^ 1)
-            else:
-                target = (x, y + (sign if x % 2 == 0 else -sign))
-                target = target if 0 <= target[1] < size_y else (x ^ 1, y)
-            moves.append((x * size_y + y, target[0] * size_y + target[1]))
-    return lax.ppermute(array, ("gx", "gy"), moves)
+            along, across = (x, y) if axis == "gx" else (y, x)
+            last = (size_x if axis == "gx" else size_y) - 1
+            up_first = along % 2 == 1 if axis in PAIRED else across % 2 == 0
+            for route, step in zip(routes, (1, -1) if up_first else (-1, 1)):
+                target = along + step
+                ends = (target, across) if 0 <= target <= last else (along, across ^ 1)
+                to_x, to_y = ends if axis == "gx" else ends[::-1]
+                route.append((x * size_y + y, to_x * size_y + to_y))
+    return tuple(
+        lax.ppermute(block, ("gx", "gy"), route) for block, route in zip((lead, trail), routes)
+    )
 
 
 def swap(array, bit):
@@ -675,12 +691,12 @@
         [STAGE],
         3,
     )
-    got = swap(away, 1)
+    got = swap(away, BITS[0])
 
     cross_scratch = [pltpu.VMEM(SLOT_ROWS.shape, f32), FORCE_SCRATCH]
     for substep in range(2):
         first = substep == 0
-        got_lead, got_trail = snake(lead, "gx", 1), snake(trail, "gx", -1)
+        got_lead, got_trail = exchange(lead, trail, "gx")
         if not first:
             rows = call(
                 inner_again,
@@ -694,10 +710,10 @@
             (got_lead, got_trail, middle),
             after=(away,) if first else (rows[3],),
         )
-        got_lead, got_trail = snake(lead, "gy", 1), snake(trail, "gy", -1)
+        got_lead, got_trail = exchange(lead, trail, "gy")
         if first:
-            stay, away = call(relay(1), (PARCELS, PARCELS), (stay, got), after=(lead, trail))
-            got = swap(away, 2)
+            stay, away = call(relay(0), (PARCELS, PARCELS), (stay, got), after=(lead, trail))
+            got = swap(away, BITS[1])
             hot_a, hot_b, *rows = call(
                 inner_start,
                 (HOT, HOT, SLOT_ROWS, SLOT_ROWS, FORCE_ROWS, FORCE_ROWS),
@@ -708,15 +724,12 @@
             hot_c, hot_d, leading = call(
                 cross_start, (HOT, HOT, SLOT_ROWS), (table, cross_pairs), after=(rows[3],)
             )
-            stay, away = call(relay(2), (PARCELS, PARCELS), (stay, got), after=(leading,))
-            got = swap(away, 4)
             on_crossing, lead, trail, side, reach = call(
                 cross_kernel,
                 (FORCE_ROWS, narrow, narrow, single, table_shape(SLOTS)),
                 (leading, hot_d, got_lead, got_trail, side),
                 cross_scratch,
                 4,
-                after=(away,),
             )
         else:
             leading = call(
@@ -731,18 +744,24 @@
                 4,
                 after=(sums[1],),
             )
-        got_lead, got_trail = snake(lead, "gy", 1), snake(trail, "gy", -1)
+        got_lead, got_trail = exchange(lead, trail, "gy")
         if first:
-            stay, away = call(relay(4), (PARCELS, PARCELS), (stay, got), after=(side,))
-            got = swap(away, 8)
+            stay, away = call(relay(1), (PARCELS, PARCELS), (stay, got), after=(side,))
+            got = swap(away, BITS[2])
             sums = call(inner_rest, (FORCE_ROWS, FORCE_ROWS), rows, cost=2, after=(away,))
         force = call(
             scatter_kernel, three, (*sums, on_crossing, hot_a, hot_b, hot_c), cost=2, after=(side,)
         )
+        if first:
+            stay, away = call(relay(2), (PARCELS, PARCELS), (stay, got), after=(force,))
+            got = swap(away, BITS[3])
         lead, trail, middle = call(
-            pass_forces, (narrow, narrow, single), (got_lead, got_trail, side), after=(force,)
+            pass_forces,
+            (narrow, narrow, single),
+            (got_lead, got_trail, side),
+            after=(force, away) if first else (force,),
         )
-        got_lead, got_trail = snake(lead, "gx", 1), snake(trail, "gx", -1)
+        got_lead, got_trail = exchange(lead, trail, "gx")
         if first:
             at_grain, parcels = call(
                 fluid_kernel,

time: 66.4 us -> 62.4 us (0.940)
  waiting for transfers between devices: 19 us -> 11.6 us
  starting transfers between devices: 19.7 us -> 22.7 us
    ppermute x16, waiting for transfers between devices: 17.3 us -> 11 us  [exchange(): lax.ppermute(block, ('gx', 'gy'), route)]
    ppermute x16, starting transfers between devices: 11 us -> 14.2 us  [exchange(): lax.ppermute(block, ('gx', 'gy'), route)]
    ppermute x4, waiting for transfers between devices: 1.71 us -> 0.56 us  [swap(): return lax.ppermute(array, ('gx', 'gy'), moves)]
  transfers between devices with their start and end apart: 20 -> 20, of which waited for: 12 -> 7; matrix products, arithmetic and copies ran while one was open for 0% -> 0% of each run, Pallas kernels for 28% -> 30%
where the time goes in v5:
time: 62.4 us; the launch traced here: 61.8 us
  Pallas kernels  26.7 us (43%)
  starting transfers between devices  22.7 us (36%)
  waiting for transfers between devices  11.6 us (19%)
  between operations  0.82 us (1%)
    pallas_call x23, Pallas kernels, call(): pl.pallas_call(body, out_shape=out_shape, in_specs=[pl.BlockSpec(memory_s...  26.7 us
    ppermute x16, starting transfers between devices, exchange(): lax.ppermute(block, ('gx', 'gy'), route)  14.2 us
    ppermute x16, waiting for transfers between devices, exchange(): lax.ppermute(block, ('gx', 'gy'), route)  11 us
    ppermute x4, starting transfers between devices, swap(): return lax.ppermute(array, ('gx', 'gy'), moves)  8.49 us
  transfers between devices with their start and end apart: 20, of which 7 were waited for; matrix products, arithmetic and copies ran while one was open for 0% of the time, Pallas kernels for 30%

profile of v5, /device:TPU:24, one launch (start us, length us, event | category | flops | bytes accessed | tf_op | source)
XLA Modules:
  0.0 61.8 jit_solution(5575435289301824672)
XLA Ops:
  0.6 1.7 %prepare.1 = (f32[128,512]{1,0:T(8,128)S(1)}, f32[128,512]{1,0:T(8,128)S(1)}, bf16[512,512]{1,0:T(8,128)(2,1)S(1)}, f32[192,128]{1,0:T(8,128)S(1)}, f32[192,128]...) custom-call(f32[3,16384]{1,0:T(4,128)} %refs_0_.1, ...), custom_call_target="tpu_custom_call" | custom-call | flops 1000000000 | bytes 1000000 | tf_op jit(solution)/shard_map/prepare/pallas_call | solution.py:622
  2.4 0.8 %collective-permute-start.1 = (f32[192,128]{1,0:T(8,128)S(1)}, f32[192,128]{1,0:T(8,128)S(1)}, u32[]{:S(2)}, u32[]{:S(2)}) collective-permute-start(f32[192,128]{1,0:T(8,128)S(1)} %get-tuple-element.87), channel_id=1, source_target_pairs={{0,1},{1,0},{2,3},{3,2},{4,5},{5,4},{6,7},{7,6},{8,9},{9,8},{10,11... | collective-permute-start | bytes 294920 | tf_op jit(solution)/shard_map/ppermute | solution.py:591
  3.2 0.9 %collective-permute-start.2 = (f32[192,128]{1,0:T(8,128)S(1)}, f32[192,128]{1,0:T(8,128)S(1)}, u32[]{:S(2)}, u32[]{:S(2)}) collective-permute-start(f32[192,128]{1,0:T(8,128)S(1)} %get-tuple-element.88), channel_id=1, source_target_pairs={{0,16},{1,17},{2,18},{3,19},{4,20},{5,21},{6,22},{7,23},{8,24},{9,... | collective-permute-start | bytes 294920 | tf_op jit(solution)/shard_map/ppermute | solution.py:591
  4.0 1.5 %deposit_kernel.1 = (f32[96,512]{1,0:T(8,128)S(1)}, s32[32,512]{1,0:T(8,128)S(1)}, f32[64,128]{1,0:T(8,128)S(1)}, f32[8,8,128]{2,1,0:T(8,128)S(1)}, f32[8,8,128]{2,1,0:T(8,128)S(1)}) custom-call(f32[128,512]{1,0:T(8,128)S(1)} %get-tuple-element.77.refs_0_, f32[128,512]{1,0:T(8,128)S(1)} %get-tuple-element.78.refs_1_, ...), custom_call_target="tpu_custom_call" | custom-call | flops 3000000000 | bytes 3000000 | tf_op jit(solution)/shard_map/deposit_kernel/pallas_call | solution.py:622
  5.5 0.8 %collective-permute-start = (f32[8,8,128]{2,1,0:T(8,128)S(1)}, f32[8,8,128]{2,1,0:T(8,128)S(1)}, u32[]{:S(2)}, u32[]{:S(2)}) collective-permute-start(f32[8,8,128]{2,1,0:T(8,128)S(1)} %get-tuple-element.86.refs_3_), channel_id=1, source_target_pairs={{0,1},{1,0},{2,3},{3,2},{4,5},{5,4},{6,7},{7,6},{8,9},{9,8},{10,11... | collective-permute-start | bytes 98312 | tf_op jit(solution)/shard_map/ppermute | solution.py:598
  6.4 0.7 %collective-permute-done.1.refs_0_ = f32[192,128]{1,0:T(8,128)S(1)} collective-permute-done((f32[192,128]{1,0:T(8,128)S(1)}, f32[192,128]{1,0:T(8,128)S(1)}, u32[]{:S(2)}, u32[]{:S(2)}) %collective-permute-start.1) | collective-permute-done | bytes 98336 | tf_op jit(solution)/shard_map/ppermute | solution.py:591
  7.2 1.8 %collective-permute-start.4 = (f32[192,128]{1,0:T(8,128)S(1)}, f32[192,128]{1,0:T(8,128)S(1)}, u32[]{:S(2)}, u32[]{:S(2)}) collective-permute-start(f32[192,128]{1,0:T(8,128)S(1)} %get-tuple-element.90.refs_2_), channel_id=1, source_target_pairs={{0,16},{1,2},{2,1},{3,4},{4,3},{5,6},{6,5},{7,8},{8,7},{9,10},{10,... | collective-permute-start | bytes 294920 | tf_op jit(solution)/shard_map/ppermute | solution.py:591
  9.6 2.0 %collective-permute-start.3 = (f32[8,8,128]{2,1,0:T(8,128)S(1)}, f32[8,8,128]{2,1,0:T(8,128)S(1)}, u32[]{:S(2)}, u32[]{:S(2)}) collective-permute-start(f32[8,8,128]{2,1,0:T(8,128)S(1)} %get-tuple-element.93.refs_2_), channel_id=1, source_target_pairs={{0,4},{1,5},{2,6},{3,7},{4,0},{5,1},{6,2},{7,3},{8,12},{9,13},{10,... | collective-permute-start | bytes 98312 | tf_op jit(solution)/shard_map/ppermute | solution.py:598
  11.6 2.2 %inner_start.1 = (bf16[512,1024]{1,0:T(8,128)(2,1)S(1)}, bf16[512,1024]{1,0:T(8,128)(2,1)S(1)}, f32[1024,128]{1,0:T(8,128)S(1)}, f32[1024,128]{1,0:T(8,128)S(1)}...) custom-call(f32[128,512]{1,0:T(8,128)S(1)} %get-tuple-element.77.refs_0_, s32[5,1024]{1,0:T(8,128)S(1)} %get-tuple-element.95.refs_1_, ...), custom_call_target="tpu_custom_call" | custom-call | flops 3000000000 | bytes 3000000 | tf_op jit(solution)/shard_map/inner_start/pallas_call | solution.py:622
  13.8 0.6 %cross_start.1 = (bf16[512,1024]{1,0:T(8,128)(2,1)S(1)}, bf16[512,1024]{1,0:T(8,128)(2,1)S(1)}, f32[1024,128]{1,0:T(8,128)S(1)}) custom-call(f32[128,512]{1,0:T(8,128)S(1)} %get-tuple-element.77.refs_0_, s32[5,1024]{1,0:T(8,128)S(1)} %get-tuple-element.94.refs_1_, f32[768,128]{1,0:T(8,128)S(1)} %get-tuple-element.96.refs_2_.refs_3_), custom_call_target="tpu_custom_call" | custom-call | flops 1000000000 | bytes 1000000 | tf_op jit(solution)/shard_map/cross_start/pallas_call | solution.py:622
  14.4 4.0 %cross_kernel.1 = (f32[768,128]{1,0:T(8,128)S(1)}, f32[144,128]{1,0:T(8,128)S(1)}, f32[144,128]{1,0:T(8,128)S(1)}, f32[96,128]{1,0:T(8,128)S(1)}, f32[32,512]{1,0:T(8,128)S(1)}) custom-call(f32[1024,128]{1,0:T(8,128)S(1)} %get-tuple-element.97.refs_0_, bf16[512,1024]{1,0:T(8,128)(2,1)S(1)} %get-tuple-element.98.refs_1_, ...), custom_call_target="tpu_custom_call" | custom-call | flops 4000000000 | bytes 4000000 | tf_op jit(solution)/shard_map/cross_kernel/pallas_call | solution.py:622
  18.5 2.0 %collective-permute-start.6 = (f32[8,8,128]{2,1,0:T(8,128)S(1)}, f32[8,8,128]{2,1,0:T(8,128)S(1)}, u32[]{:S(2)}, u32[]{:S(2)}) collective-permute-start(f32[8,8,128]{2,1,0:T(8,128)S(1)} %get-tuple-element.102.refs_4_), channel_id=1, source_target_pairs={{0,2},{1,3},{2,0},{3,1},{4,6},{5,7},{6,4},{7,5},{8,10},{9,11},{10,... | collective-permute-start | bytes 98312 | tf_op jit(solution)/shard_map/ppermute | solution.py:598
  20.5 1.8 %collective-permute-start.8 = (f32[144,128]{1,0:T(8,128)S(1)}, f32[144,128]{1,0:T(8,128)S(1)}, u32[]{:S(2)}, u32[]{:S(2)}) collective-permute-start(f32[144,128]{1,0:T(8,128)S(1)} %get-tuple-element.115), channel_id=1, source_target_pairs={{0,16},{1,2},{2,1},{3,4},{4,3},{5,6},{6,5},{7,8},{8,7},{9,10},{10,... | collective-permute-start | bytes 221192 | tf_op jit(solution)/shard_map/ppermute | solution.py:591
  22.3 1.5 %inner_rest.2 = (f32[768,128]{1,0:T(8,128)S(1)}, f32[768,128]{1,0:T(8,128)S(1)}) custom-call(f32[1024,128]{1,0:T(8,128)S(1)} %get-tuple-element.103.refs_0_, f32[1024,128]{1,0:T(8,128)S(1)} %get-tuple-element.104.refs_1_, f32[768,128]{1,0:T(8,128)S(1)} %get-tuple-element.105.refs_2_, f32[768,128]{1,0:T(8,128)S(1)} %get-tuple-element.96.refs_2_.refs_3_, ...), custom_call_target="tpu_custom_call" | custom-call | flops 2000000000 | bytes 2000000 | tf_op jit(solution)/shard_map/inner_rest/pallas_call | solution.py:622
  23.8 1.2 %scatter_kernel.2.refs_2_.refs_3_.refs_4_ = f32[96,512]{1,0:T(8,128)S(1)} custom-call(f32[768,128]{1,0:T(8,128)S(1)} %get-tuple-element.106.refs_0_, f32[768,128]{1,0:T(8,128)S(1)} %get-tuple-element.107.refs_1_, f32[768,128]{1,0:T(8,128)S(1)} %get-tuple-element.108.refs_2_, bf16[512,1024]{1,0:T(8,128)(2,1)S(1)} %get-tuple-element.109.refs_3_.refs_2_, ...), custom_call_target="tpu_custom_call" | custom-call | flops 2000000000 | bytes 2000000 | tf_op jit(solution)/shard_map/scatter_kernel/pallas_call | solution.py:622
  25.0 3.7 %collective-permute-start.7 = (f32[8,8,128]{2,1,0:T(8,128)S(1)}, f32[8,8,128]{2,1,0:T(8,128)S(1)}, u32[]{:S(2)}, u32[]{:S(2)}) collective-permute-start(f32[8,8,128]{2,1,0:T(8,128)S(1)} %get-tuple-element.113.refs_4_), channel_id=1, source_target_pairs={{0,8},{1,9},{2,10},{3,11},{4,12},{5,13},{6,14},{7,15},{8,0},{9,1},... | collective-permute-start | bytes 98312 | tf_op jit(solution)/shard_map/ppermute | solution.py:598
  28.8 2.1 %collective-permute-start.10 = (f32[144,128]{1,0:T(8,128)S(1)}, f32[144,128]{1,0:T(8,128)S(1)}, u32[]{:S(2)}, u32[]{:S(2)}) collective-permute-start(f32[144,128]{1,0:T(8,128)S(1)} %get-tuple-element.117.refs_4_), channel_id=1, source_target_pairs={{0,1},{1,0},{2,3},{3,2},{4,5},{5,4},{6,7},{7,6},{8,9},{9,8},{10,11... | collective-permute-start | bytes 221192 | tf_op jit(solution)/shard_map/ppermute | solution.py:591
  30.9 1.3 %fluid_kernel.1 = (f32[128,512]{1,0:T(8,128)S(1)}, f32[16,8,128]{2,1,0:T(8,128)S(1)}) custom-call(f32[64,128]{1,0:T(8,128)S(1)} %get-tuple-element.84.refs_0_, f32[8,8,128]{2,1,0:T(8,128)S(1)} %get-tuple-element.112.refs_1_, f32[8,8,128]{2,1,0:T(8,128)S(1)} %collective-permute-done.7.refs_2_, s32[32,512]{1,0:T(8,128)S(1)} %get-tuple-element.114.refs_3_, ...), custom_call_target="tpu_custom_call" | custom-call | flops 3000000000 | bytes 3000000 | tf_op jit(solution)/shard_map/fluid_kernel/pallas_call | solution.py:622
  32.2 1.0 %collective-permute-done.10.refs_6_ = f32[144,128]{1,0:T(8,128)S(1)} collective-permute-done((f32[144,128]{1,0:T(8,128)S(1)}, f32[144,128]{1,0:T(8,128)S(1)}, u32[]{:S(2)}, u32[]{:S(2)}) %collective-permute-start.10) | collective-permute-done | bytes 73760 | tf_op jit(solution)/shard_map/ppermute | solution.py:591
  33.2 0.7 %middle_kernel.1 = (f32[128,512]{1,0:T(8,128)S(1)}, f32[128,512]{1,0:T(8,128)S(1)}, f32[96,512]{1,0:T(8,128)S(1)}, f32[144,128]{1,0:T(8,128)S(1)}, f32[144,128]{1,0:T(8,128)S(1)}, /*index=5*/f32[96,128]{1,0:T(8,128)S(1)}) custom-call(f32[128,512]{1,0:T(8,128)S(1)} %get-tuple-element.77.refs_0_, f32[128,512]{1,0:T(8,128)S(1)} %get-tuple-element.78.refs_1_, ...), custom_call_target="tpu_custom_call" | custom-call | flops 1000000000 | bytes 1000000 | tf_op jit(solution)/shard_map/middle_kernel/pallas_call | solution.py:622
  33.9 2.1 %collective-permute-start.12 = (f32[144,128]{1,0:T(8,128)S(1)}, f32[144,128]{1,0:T(8,128)S(1)}, u32[]{:S(2)}, u32[]{:S(2)}) collective-permute-start(f32[144,128]{1,0:T(8,128)S(1)} %get-tuple-element.129), channel_id=1, source_target_pairs={{0,1},{1,0},{2,3},{3,2},{4,5},{5,4},{6,7},{7,6},{8,9},{9,8},{10,11... | collective-permute-start | bytes 221192 | tf_op jit(solution)/shard_map/ppermute | solution.py:591
  36.0 2.2 %inner_again.1 = (f32[1024,128]{1,0:T(8,128)S(1)}, f32[1024,128]{1,0:T(8,128)S(1)}, f32[768,128]{1,0:T(8,128)S(1)}, f32[768,128]{1,0:T(8,128)S(1)}) custom-call(f32[128,512]{1,0:T(8,128)S(1)} %get-tuple-element.122.refs_0_, s32[5,1024]{1,0:T(8,128)S(1)} %get-tuple-element.95.refs_1_, bf16[512,1024]{1,0:T(8,128)(2,1)S(1)} %get-tuple-element.109.refs_3_.refs_2_, ...), custom_call_target="tpu_custom_call" | custom-call | flops 3000000000 | bytes 3000000 | tf_op jit(solution)/shard_map/inner_again/pallas_call | solution.py:622
  38.5 2.2 %collective-permute-start.14 = (f32[144,128]{1,0:T(8,128)S(1)}, f32[144,128]{1,0:T(8,128)S(1)}, u32[]{:S(2)}, u32[]{:S(2)}) collective-permute-start(f32[144,128]{1,0:T(8,128)S(1)} %get-tuple-element.132.refs_3_), channel_id=1, source_target_pairs={{0,16},{1,2},{2,1},{3,4},{4,3},{5,6},{6,5},{7,8},{8,7},{9,10},{10,... | collective-permute-start | bytes 221192 | tf_op jit(solution)/shard_map/ppermute | solution.py:591
  41.1 1.5 %inner_rest.3 = (f32[768,128]{1,0:T(8,128)S(1)}, f32[768,128]{1,0:T(8,128)S(1)}) custom-call(f32[1024,128]{1,0:T(8,128)S(1)} %get-tuple-element.125.refs_0_, f32[1024,128]{1,0:T(8,128)S(1)} %get-tuple-element.126.refs_1_, f32[768,128]{1,0:T(8,128)S(1)} %get-tuple-element.127.refs_2_, f32[768,128]{1,0:T(8,128)S(1)} %get-tuple-element.128.refs_3_, ...), custom_call_target="tpu_custom_call" | custom-call | flops 2000000000 | bytes 2000000 | tf_op jit(solution)/shard_map/inner_rest/pallas_call | solution.py:622
  42.6 2.6 %collective-permute-done.14.refs_2_ = f32[144,128]{1,0:T(8,128)S(1)} collective-permute-done((f32[144,128]{1,0:T(8,128)S(1)}, f32[144,128]{1,0:T(8,128)S(1)}, u32[]{:S(2)}, u32[]{:S(2)}) %collective-permute-start.14) | collective-permute-done | bytes 73760 | tf_op jit(solution)/shard_map/ppermute | solution.py:591
  45.2 4.0 %cross_kernel_again.1 = (f32[768,128]{1,0:T(8,128)S(1)}, f32[144,128]{1,0:T(8,128)S(1)}, f32[144,128]{1,0:T(8,128)S(1)}, f32[96,128]{1,0:T(8,128)S(1)}) custom-call(f32[1024,128]{1,0:T(8,128)S(1)} %cross_again.1.refs_4_.refs_0_, bf16[512,1024]{1,0:T(8,128)(2,1)S(1)} %get-tuple-element.98.refs_1_, f32[144,128]{1,0:T(8,128)S(1)} %collective-permute-done.14.refs_2_, ...), custom_call_target="tpu_custom_call" | custom-call | flops 4000000000 | bytes 4000000 | tf_op jit(solution)/shard_map/cross_kernel_again/pallas_call | solution.py:622
  49.3 2.2 %collective-permute-start.16 = (f32[144,128]{1,0:T(8,128)S(1)}, f32[144,128]{1,0:T(8,128)S(1)}, u32[]{:S(2)}, u32[]{:S(2)}) collective-permute-start(f32[144,128]{1,0:T(8,128)S(1)} %get-tuple-element.140), channel_id=1, source_target_pairs={{0,16},{1,2},{2,1},{3,4},{4,3},{5,6},{6,5},{7,8},{8,7},{9,10},{10,... | collective-permute-start | bytes 221192 | tf_op jit(solution)/shard_map/ppermute | solution.py:591
  51.4 1.2 %scatter_kernel.3.refs_3_.refs_4_ = f32[96,512]{1,0:T(8,128)S(1)} custom-call(f32[768,128]{1,0:T(8,128)S(1)} %get-tuple-element.134.refs_0_, f32[768,128]{1,0:T(8,128)S(1)} %get-tuple-element.135.refs_6_.refs_1_, f32[768,128]{1,0:T(8,128)S(1)} %get-tuple-element.138.refs_2_, bf16[512,1024]{1,0:T(8,128)(2,1)S(1)} %get-tuple-element.109.refs_3_.refs_2_, ...), custom_call_target="tpu_custom_call" | custom-call | flops 2000000000 | bytes 2000000 | tf_op jit(solution)/shard_map/scatter_kernel/pallas_call | solution.py:622
  52.6 3.2 %collective-permute-done.16.refs_0_ = f32[144,128]{1,0:T(8,128)S(1)} collective-permute-done((f32[144,128]{1,0:T(8,128)S(1)}, f32[144,128]{1,0:T(8,128)S(1)}, u32[]{:S(2)}, u32[]{:S(2)}) %collective-permute-start.16) | collective-permute-done | bytes 73760 | tf_op jit(solution)/shard_map/ppermute | solution.py:591
  56.2 0.7 %owned_kernel.1 = (f32[3,2048]{1,0:T(4,128)}, f32[16,128]{1,0:T(8,128)}) custom-call(f32[16,8,128]{2,1,0:T(8,128)S(1)} %get-tuple-element.147.refs_0_, f32[3,2048]{1,0:T(4,128)S(1)} %get-tuple-element.81.refs_4_.refs_1_, f32[3,2048]{1,0:T(4,128)S(1)} %get-tuple-element.82.refs_5_.refs_2_, f32[144,128]{1,0:T(8,128)S(1)} %get-tuple-element.143.refs_3_, ...), custom_call_target="tpu_custom_call" | custom-call | flops 1000000000 | bytes 1000000 | tf_op jit(solution)/shard_map/owned_kernel/pallas_call | solution.py:622
  56.9 3.4 %collective-permute-done.18.refs_6_ = f32[144,128]{1,0:T(8,128)S(1)} collective-permute-done((f32[144,128]{1,0:T(8,128)S(1)}, f32[144,128]{1,0:T(8,128)S(1)}, u32[]{:S(2)}, u32[]{:S(2)}) %collective-permute-start.18) | collective-permute-done | bytes 73760 | tf_op jit(solution)/shard_map/ppermute | solution.py:591
  60.3 1.4 %last_kernel.1 = (f32[3,16384]{1,0:T(4,128)}, f32[3,16384]{1,0:T(4,128)}) custom-call(f32[128,512]{1,0:T(8,128)S(1)} %get-tuple-element.122.refs_0_, f32[128,512]{1,0:T(8,128)S(1)} %get-tuple-element.123.refs_1_, f32[96,512]{1,0:T(8,128)S(1)} %get-tuple-element.124.refs_2_, f32[128,512]{1,0:T(8,128)S(1)} %get-tuple-element.119.refs_3_, ...), custom_call_target="tpu_custom_call" | custom-call | flops 1000000000 | bytes 1000000 | tf_op jit(solution)/shard_map/last_kernel/pallas_call | solution.py:622
  (31 shorter events, 2.0 us)
Async XLA Ops:
  2.4 4.7 %collective-permute-start.1 = (f32[192,128]{1,0:T(8,128)S(1)}, f32[192,128]{1,0:T(8,128)S(1)}, u32[]{:S(2)}, u32[]{:S(2)}) collective-permute-start(f32[192,128]{1,0:T(8,128)S(1)} %get-tuple-element.87), channel_id=1, source_target_pairs={{0,1},{1,0},{2,3},{3,2},{4,5},{5,4},{6,7},{7,6},{8,9},{9,8},{10,11... | collective-permute-start | bytes 294920 | tf_op jit(solution)/shard_map/ppermute | solution.py:591
  3.2 3.9 %collective-permute-start.2 = (f32[192,128]{1,0:T(8,128)S(1)}, f32[192,128]{1,0:T(8,128)S(1)}, u32[]{:S(2)}, u32[]{:S(2)}) collective-permute-start(f32[192,128]{1,0:T(8,128)S(1)} %get-tuple-element.88), channel_id=1, source_target_pairs={{0,16},{1,17},{2,18},{3,19},{4,20},{5,21},{6,22},{7,23},{8,24},{9,... | collective-permute-start | bytes 294920 | tf_op jit(solution)/shard_map/ppermute | solution.py:591
  5.5 4.0 %collective-permute-start = (f32[8,8,128]{2,1,0:T(8,128)S(1)}, f32[8,8,128]{2,1,0:T(8,128)S(1)}, u32[]{:S(2)}, u32[]{:S(2)}) collective-permute-start(f32[8,8,128]{2,1,0:T(8,128)S(1)} %get-tuple-element.86.refs_3_), channel_id=1, source_target_pairs={{0,1},{1,0},{2,3},{3,2},{4,5},{5,4},{6,7},{7,6},{8,9},{9,8},{10,11... | collective-permute-start | bytes 98312 | tf_op jit(solution)/shard_map/ppermute | solution.py:598
  7.2 7.2 %collective-permute-start.4 = (f32[192,128]{1,0:T(8,128)S(1)}, f32[192,128]{1,0:T(8,128)S(1)}, u32[]{:S(2)}, u32[]{:S(2)}) collective-permute-start(f32[192,128]{1,0:T(8,128)S(1)} %get-tuple-element.90.refs_2_), channel_id=1, source_target_pairs={{0,16},{1,2},{2,1},{3,4},{4,3},{5,6},{6,5},{7,8},{8,7},{9,10},{10,... | collective-permute-start | bytes 294920 | tf_op jit(solution)/shard_map/ppermute | solution.py:591
  9.0 5.4 %collective-permute-start.5 = (f32[192,128]{1,0:T(8,128)S(1)}, f32[192,128]{1,0:T(8,128)S(1)}, u32[]{:S(2)}, u32[]{:S(2)}) collective-permute-start(f32[192,128]{1,0:T(8,128)S(1)} %get-tuple-element.91.refs_3_), channel_id=1, source_target_pairs={{0,1},{1,0},{2,3},{3,2},{4,5},{5,4},{6,7},{7,6},{8,9},{9,8},{10,11... | collective-permute-start | bytes 294920 | tf_op jit(solution)/shard_map/ppermute | solution.py:591
  9.6 8.9 %collective-permute-start.3 = (f32[8,8,128]{2,1,0:T(8,128)S(1)}, f32[8,8,128]{2,1,0:T(8,128)S(1)}, u32[]{:S(2)}, u32[]{:S(2)}) collective-permute-start(f32[8,8,128]{2,1,0:T(8,128)S(1)} %get-tuple-element.93.refs_2_), channel_id=1, source_target_pairs={{0,4},{1,5},{2,6},{3,7},{4,0},{5,1},{6,2},{7,3},{8,12},{9,13},{10,... | collective-permute-start | bytes 98312 | tf_op jit(solution)/shard_map/ppermute | solution.py:598
  18.5 6.5 %collective-permute-start.6 = (f32[8,8,128]{2,1,0:T(8,128)S(1)}, f32[8,8,128]{2,1,0:T(8,128)S(1)}, u32[]{:S(2)}, u32[]{:S(2)}) collective-permute-start(f32[8,8,128]{2,1,0:T(8,128)S(1)} %get-tuple-element.102.refs_4_), channel_id=1, source_target_pairs={{0,2},{1,3},{2,0},{3,1},{4,6},{5,7},{6,4},{7,5},{8,10},{9,11},{10,... | collective-permute-start | bytes 98312 | tf_op jit(solution)/shard_map/ppermute | solution.py:598
  20.5 8.1 %collective-permute-start.8 = (f32[144,128]{1,0:T(8,128)S(1)}, f32[144,128]{1,0:T(8,128)S(1)}, u32[]{:S(2)}, u32[]{:S(2)}) collective-permute-start(f32[144,128]{1,0:T(8,128)S(1)} %get-tuple-element.115), channel_id=1, source_target_pairs={{0,16},{1,2},{2,1},{3,4},{4,3},{5,6},{6,5},{7,8},{8,7},{9,10},{10,... | collective-permute-start | bytes 221192 | tf_op jit(solution)/shard_map/ppermute | solution.py:591
  22.3 6.4 %collective-permute-start.9 = (f32[144,128]{1,0:T(8,128)S(1)}, f32[144,128]{1,0:T(8,128)S(1)}, u32[]{:S(2)}, u32[]{:S(2)}) collective-permute-start(f32[144,128]{1,0:T(8,128)S(1)} %get-tuple-element.116), channel_id=1, source_target_pairs={{0,1},{1,0},{2,3},{3,2},{4,5},{5,4},{6,7},{7,6},{8,9},{9,8},{10,11... | collective-permute-start | bytes 221192 | tf_op jit(solution)/shard_map/ppermute | solution.py:591
  25.0 5.9 %collective-permute-start.7 = (f32[8,8,128]{2,1,0:T(8,128)S(1)}, f32[8,8,128]{2,1,0:T(8,128)S(1)}, u32[]{:S(2)}, u32[]{:S(2)}) collective-permute-start(f32[8,8,128]{2,1,0:T(8,128)S(1)} %get-tuple-element.113.refs_4_), channel_id=1, source_target_pairs={{0,8},{1,9},{2,10},{3,11},{4,12},{5,13},{6,14},{7,15},{8,0},{9,1},... | collective-permute-start | bytes 98312 | tf_op jit(solution)/shard_map/ppermute | solution.py:598
  28.8 4.4 %collective-permute-start.10 = (f32[144,128]{1,0:T(8,128)S(1)}, f32[144,128]{1,0:T(8,128)S(1)}, u32[]{:S(2)}, u32[]{:S(2)}) collective-permute-start(f32[144,128]{1,0:T(8,128)S(1)} %get-tuple-element.117.refs_4_), channel_id=1, source_target_pairs={{0,1},{1,0},{2,3},{3,2},{4,5},{5,4},{6,7},{7,6},{8,9},{9,8},{10,11... | collective-permute-start | bytes 221192 | tf_op jit(solution)/shard_map/ppermute | solution.py:591
  30.9 2.3 %collective-permute-start.11 = (f32[144,128]{1,0:T(8,128)S(1)}, f32[144,128]{1,0:T(8,128)S(1)}, u32[]{:S(2)}, u32[]{:S(2)}) collective-permute-start(f32[144,128]{1,0:T(8,128)S(1)} %get-tuple-element.118.refs_5_), channel_id=1, source_target_pairs={{0,16},{1,17},{2,18},{3,19},{4,20},{5,21},{6,22},{7,23},{8,24},{9,... | collective-permute-start | bytes 221192 | tf_op jit(solution)/shard_map/ppermute | solution.py:591
  33.9 4.4 %collective-permute-start.12 = (f32[144,128]{1,0:T(8,128)S(1)}, f32[144,128]{1,0:T(8,128)S(1)}, u32[]{:S(2)}, u32[]{:S(2)}) collective-permute-start(f32[144,128]{1,0:T(8,128)S(1)} %get-tuple-element.129), channel_id=1, source_target_pairs={{0,1},{1,0},{2,3},{3,2},{4,5},{5,4},{6,7},{7,6},{8,9},{9,8},{10,11... | collective-permute-start | bytes 221192 | tf_op jit(solution)/shard_map/ppermute | solution.py:591
  36.0 2.3 %collective-permute-start.13 = (f32[144,128]{1,0:T(8,128)S(1)}, f32[144,128]{1,0:T(8,128)S(1)}, u32[]{:S(2)}, u32[]{:S(2)}) collective-permute-start(f32[144,128]{1,0:T(8,128)S(1)} %get-tuple-element.130), channel_id=1, source_target_pairs={{0,16},{1,17},{2,18},{3,19},{4,20},{5,21},{6,22},{7,23},{8,24},{9,... | collective-permute-start | bytes 221192 | tf_op jit(solution)/shard_map/ppermute | solution.py:591
  38.5 6.7 %collective-permute-start.14 = (f32[144,128]{1,0:T(8,128)S(1)}, f32[144,128]{1,0:T(8,128)S(1)}, u32[]{:S(2)}, u32[]{:S(2)}) collective-permute-start(f32[144,128]{1,0:T(8,128)S(1)} %get-tuple-element.132.refs_3_), channel_id=1, source_target_pairs={{0,16},{1,2},{2,1},{3,4},{4,3},{5,6},{6,5},{7,8},{8,7},{9,10},{10,... | collective-permute-start | bytes 221192 | tf_op jit(solution)/shard_map/ppermute | solution.py:591
  40.7 4.6 %collective-permute-start.15 = (f32[144,128]{1,0:T(8,128)S(1)}, f32[144,128]{1,0:T(8,128)S(1)}, u32[]{:S(2)}, u32[]{:S(2)}) collective-permute-start(f32[144,128]{1,0:T(8,128)S(1)} %get-tuple-element.133.refs_4_), channel_id=1, source_target_pairs={{0,1},{1,0},{2,3},{3,2},{4,5},{5,4},{6,7},{7,6},{8,9},{9,8},{10,11... | collective-permute-start | bytes 221192 | tf_op jit(solution)/shard_map/ppermute | solution.py:591
  49.3 6.5 %collective-permute-start.16 = (f32[144,128]{1,0:T(8,128)S(1)}, f32[144,128]{1,0:T(8,128)S(1)}, u32[]{:S(2)}, u32[]{:S(2)}) collective-permute-start(f32[144,128]{1,0:T(8,128)S(1)} %get-tuple-element.140), channel_id=1, source_target_pairs={{0,16},{1,2},{2,1},{3,4},{4,3},{5,6},{6,5},{7,8},{8,7},{9,10},{10,... | collective-permute-start | bytes 221192 | tf_op jit(solution)/shard_map/ppermute | solution.py:591
  51.4 4.4 %collective-permute-start.17 = (f32[144,128]{1,0:T(8,128)S(1)}, f32[144,128]{1,0:T(8,128)S(1)}, u32[]{:S(2)}, u32[]{:S(2)}) collective-permute-start(f32[144,128]{1,0:T(8,128)S(1)} %get-tuple-element.141), channel_id=1, source_target_pairs={{0,1},{1,0},{2,3},{3,2},{4,5},{5,4},{6,7},{7,6},{8,9},{9,8},{10,11... | collective-permute-start | bytes 221192 | tf_op jit(solution)/shard_map/ppermute | solution.py:591
  55.9 4.4 %collective-permute-start.18 = (f32[144,128]{1,0:T(8,128)S(1)}, f32[144,128]{1,0:T(8,128)S(1)}, u32[]{:S(2)}, u32[]{:S(2)}) collective-permute-start(f32[144,128]{1,0:T(8,128)S(1)} %get-tuple-element.143.refs_3_), channel_id=1, source_target_pairs={{0,1},{1,0},{2,3},{3,2},{4,5},{5,4},{6,7},{7,6},{8,9},{9,8},{10,11... | collective-permute-start | bytes 221192 | tf_op jit(solution)/shard_map/ppermute | solution.py:591
  56.0 4.3 %collective-permute-start.19 = (f32[144,128]{1,0:T(8,128)S(1)}, f32[144,128]{1,0:T(8,128)S(1)}, u32[]{:S(2)}, u32[]{:S(2)}) collective-permute-start(f32[144,128]{1,0:T(8,128)S(1)} %get-tuple-element.144.refs_4_), channel_id=1, source_target_pairs={{0,16},{1,17},{2,18},{3,19},{4,20},{5,21},{6,22},{7,23},{8,24},{9,... | collective-permute-start | bytes 221192 | tf_op jit(solution)/shard_map/ppermute | solution.py:591

commit v6 on v5

--- a/solution.py
+++ b/solution.py
@@ -18,7 +18,7 @@
 GHOST_ORDER = (7, 2, 3, 4, 5, 0, 1, 6)
 PAIRED = ("gx", "gy")
 OTHER = {"gx": "gy", "gy": "gx"}
-BITS = (1, 4, 2, 8)
+BITS = (1, 2, 4, 8)
 FAR = 2.0**30
 
 spring = 4.0
@@ -151,7 +151,7 @@
 
 
 def send_pieces(table, rows, hot, lead, trail, middle):
-    pieces = gather(jnp.concatenate(split(table[:rows], 3), axis=0), hot[...], rows)
+    pieces = gather(table_parts(table[:rows]), hot[...], rows)
     tiles = [pieces[:, k * LANES : (k + 1) * LANES] for k in range(4)]
     up = fold(tiles[3], tiles[2], True)
     down = fold(tiles[0], tiles[1], False)
@@ -264,11 +264,15 @@
             ]
 
 
-def scatter(sums, hot):
-    pieces = jnp.concatenate(
-        [sums[pl.ds(k, 3 * SLOTS, stride=8), :] for k in range(PAIRS // LANES)], axis=1
-    )
-    added = dot_lanes(jnp.concatenate(split(pieces, 2), axis=0), hot[...])
+def scatter(*terms):
+    parts, hots = [], []
+    for sums, hot, sign in terms:
+        pieces = jnp.concatenate(
+            [sums[pl.ds(k, 3 * SLOTS, stride=8), :] for k in range(PAIRS // LANES)], axis=1
+        )
+        parts.append(jnp.concatenate(split(pieces if sign > 0 else -pieces, 2), axis=0))
+        hots.append(hot[...])
+    added = dot_lanes(jnp.concatenate(parts, axis=1), jnp.concatenate(hots, axis=1))
     return added[: 3 * SLOTS] + added[3 * SLOTS :]
 
 
@@ -315,9 +319,7 @@
 
 
 def scatter_kernel(on_leading, on_partner, on_crossing, hot_a, hot_b, hot_c, force):
-    force[...] = (
-        scatter(on_leading, hot_a) - scatter(on_partner, hot_b) + scatter(on_crossing, hot_c)
-    )
+    force[...] = scatter((on_leading, hot_a, 1), (on_partner, hot_b, -1), (on_crossing, hot_c, 1))
 
 
 def present_tile(low, high):
@@ -346,7 +348,7 @@
     fill_slots(table_parts(ghosts), hot_b, None, partner)
     on_partner[...] = jnp.zeros_like(on_partner)
     contacts(leading, partner, on_leading, on_partner, 0, SLOTS)
-    back = scatter(on_partner, hot_b)
+    back = scatter((on_partner, hot_b, 1))
     tiles = [back[:, k * LANES : (k + 1) * LANES] for k in range(4)]
     up = fold(tiles[0], tiles[1], True)
     down = fold(tiles[2], tiles[1], False)
@@ -704,11 +706,15 @@
                 (table, inner_pairs, hot_a, hot_b),
                 cost=3,
             )
+        if first:
+            hot_c, hot_d, leading = call(
+                cross_start, (HOT, HOT, SLOT_ROWS), (table, cross_pairs), after=(away,)
+            )
         lead, trail, side = call(
             pass_ghosts,
             (wide, wide, full_tile) if first else (narrow, narrow, single),
             (got_lead, got_trail, middle),
-            after=(away,) if first else (rows[3],),
+            after=(leading,) if first else (rows[3],),
         )
         got_lead, got_trail = exchange(lead, trail, "gy")
         if first:
@@ -721,9 +727,6 @@
                 cost=3,
                 after=(away,),
             )
-            hot_c, hot_d, leading = call(
-                cross_start, (HOT, HOT, SLOT_ROWS), (table, cross_pairs), after=(rows[3],)
-            )
             on_crossing, lead, trail, side, reach = call(
                 cross_kernel,
                 (FORCE_ROWS, narrow, narrow, single, table_shape(SLOTS)),
@@ -749,17 +752,20 @@
             stay, away = call(relay(1), (PARCELS, PARCELS), (stay, got), after=(side,))
             got = swap(away, BITS[2])
             sums = call(inner_rest, (FORCE_ROWS, FORCE_ROWS), rows, cost=2, after=(away,))
+            stay, away = call(relay(2), (PARCELS, PARCELS), (stay, got), after=(sums[1],))
+            got = swap(away, BITS[3])
         force = call(
-            scatter_kernel, three, (*sums, on_crossing, hot_a, hot_b, hot_c), cost=2, after=(side,)
+            scatter_kernel,
+            three,
+            (*sums, on_crossing, hot_a, hot_b, hot_c),
+            cost=2,
+            after=(side, away) if first else (side,),
         )
-        if first:
-            stay, away = call(relay(2), (PARCELS, PARCELS), (stay, got), after=(force,))
-            got = swap(away, BITS[3])
         lead, trail, middle = call(
             pass_forces,
             (narrow, narrow, single),
             (got_lead, got_trail, side),
-            after=(force, away) if first else (force,),
+            after=(force,),
         )
         got_lead, got_trail = exchange(lead, trail, "gx")
         if first:

time: 62.4 us -> 62.2 us (level)
    ppermute x4, starting transfers between devices: 8.49 us -> 7.7 us  [swap(): return lax.ppermute(array, ('gx', 'gy'), moves)]
    ppermute x16, waiting for transfers between devices: 11 us -> 11.8 us  [exchange(): lax.ppermute(block, ('gx', 'gy'), route)]
  transfers between devices with their start and end apart: 20 -> 20, of which waited for: 7 -> 8; matrix products, arithmetic and copies ran while one was open for 0% -> 0% of each run, Pallas kernels for 30% -> 30%
where the time goes in v6:
time: 62.2 us; the launch traced here: 61.7 us
  Pallas kernels  26.6 us (43%)
  starting transfers between devices  22.5 us (36%)
  waiting for transfers between devices  11.8 us (19%)
  between operations  0.83 us (1%)
    pallas_call x23, Pallas kernels, call(): pl.pallas_call(body, out_shape=out_shape, in_specs=[pl.BlockSpec(memory_s...  26.6 us
    ppermute x16, starting transfers between devices, exchange(): lax.ppermute(block, ('gx', 'gy'), route)  14.8 us
    ppermute x16, waiting for transfers between devices, exchange(): lax.ppermute(block, ('gx', 'gy'), route)  11.8 us
    ppermute x4, starting transfers between devices, swap(): return lax.ppermute(array, ('gx', 'gy'), moves)  7.7 us
  transfers between devices with their start and end apart: 20, of which 8 were waited for; matrix products, arithmetic and copies ran while one was open for 0% of the time, Pallas kernels for 30%

profile of v6, /device:TPU:24, one launch (start us, length us, event | category | flops | bytes accessed | tf_op | source)
XLA Modules:
  0.0 61.7 jit_solution(888236925720397338)
XLA Ops:
  0.6 1.6 %prepare.1 = (f32[128,512]{1,0:T(8,128)S(1)}, f32[128,512]{1,0:T(8,128)S(1)}, bf16[512,512]{1,0:T(8,128)(2,1)S(1)}, f32[192,128]{1,0:T(8,128)S(1)}, f32[192,128]...) custom-call(f32[3,16384]{1,0:T(4,128)} %refs_0_.1, ...), custom_call_target="tpu_custom_call" | custom-call | flops 1000000000 | bytes 1000000 | tf_op jit(solution)/shard_map/prepare/pallas_call | solution.py:624
  2.3 0.8 %collective-permute-start.1 = (f32[192,128]{1,0:T(8,128)S(1)}, f32[192,128]{1,0:T(8,128)S(1)}, u32[]{:S(2)}, u32[]{:S(2)}) collective-permute-start(f32[192,128]{1,0:T(8,128)S(1)} %get-tuple-element.87), channel_id=1, source_target_pairs={{0,1},{1,0},{2,3},{3,2},{4,5},{5,4},{6,7},{7,6},{8,9},{9,8},{10,11... | collective-permute-start | bytes 294920 | tf_op jit(solution)/shard_map/ppermute | solution.py:593
  3.1 0.9 %collective-permute-start.2 = (f32[192,128]{1,0:T(8,128)S(1)}, f32[192,128]{1,0:T(8,128)S(1)}, u32[]{:S(2)}, u32[]{:S(2)}) collective-permute-start(f32[192,128]{1,0:T(8,128)S(1)} %get-tuple-element.88), channel_id=1, source_target_pairs={{0,16},{1,17},{2,18},{3,19},{4,20},{5,21},{6,22},{7,23},{8,24},{9,... | collective-permute-start | bytes 294920 | tf_op jit(solution)/shard_map/ppermute | solution.py:593
  4.0 1.5 %deposit_kernel.1 = (f32[96,512]{1,0:T(8,128)S(1)}, s32[32,512]{1,0:T(8,128)S(1)}, f32[64,128]{1,0:T(8,128)S(1)}, f32[8,8,128]{2,1,0:T(8,128)S(1)}, f32[8,8,128]{2,1,0:T(8,128)S(1)}) custom-call(f32[128,512]{1,0:T(8,128)S(1)} %get-tuple-element.77.refs_0_, f32[128,512]{1,0:T(8,128)S(1)} %get-tuple-element.78.refs_1_, ...), custom_call_target="tpu_custom_call" | custom-call | flops 3000000000 | bytes 3000000 | tf_op jit(solution)/shard_map/deposit_kernel/pallas_call | solution.py:624
  5.5 0.8 %collective-permute-start = (f32[8,8,128]{2,1,0:T(8,128)S(1)}, f32[8,8,128]{2,1,0:T(8,128)S(1)}, u32[]{:S(2)}, u32[]{:S(2)}) collective-permute-start(f32[8,8,128]{2,1,0:T(8,128)S(1)} %get-tuple-element.86.refs_2_), channel_id=1, source_target_pairs={{0,1},{1,0},{2,3},{3,2},{4,5},{5,4},{6,7},{7,6},{8,9},{9,8},{10,11... | collective-permute-start | bytes 98312 | tf_op jit(solution)/shard_map/ppermute | solution.py:600
  7.1 2.5 %collective-permute-start.4 = (f32[192,128]{1,0:T(8,128)S(1)}, f32[192,128]{1,0:T(8,128)S(1)}, u32[]{:S(2)}, u32[]{:S(2)}) collective-permute-start(f32[192,128]{1,0:T(8,128)S(1)} %get-tuple-element.92.refs_2_), channel_id=1, source_target_pairs={{0,16},{1,2},{2,1},{3,4},{4,3},{5,6},{6,5},{7,8},{8,7},{9,10},{10,... | collective-permute-start | bytes 294920 | tf_op jit(solution)/shard_map/ppermute | solution.py:593
  9.6 1.2 %collective-permute-start.3 = (f32[8,8,128]{2,1,0:T(8,128)S(1)}, f32[8,8,128]{2,1,0:T(8,128)S(1)}, u32[]{:S(2)}, u32[]{:S(2)}) collective-permute-start(f32[8,8,128]{2,1,0:T(8,128)S(1)} %get-tuple-element.95.refs_2_), channel_id=1, source_target_pairs={{0,2},{1,3},{2,0},{3,1},{4,6},{5,7},{6,4},{7,5},{8,10},{9,11},{10,... | collective-permute-start | bytes 98312 | tf_op jit(solution)/shard_map/ppermute | solution.py:600
  10.8 2.2 %inner_start.1 = (bf16[512,1024]{1,0:T(8,128)(2,1)S(1)}, bf16[512,1024]{1,0:T(8,128)(2,1)S(1)}, f32[1024,128]{1,0:T(8,128)S(1)}, f32[1024,128]{1,0:T(8,128)S(1)}...) custom-call(f32[128,512]{1,0:T(8,128)S(1)} %get-tuple-element.77.refs_0_, s32[5,1024]{1,0:T(8,128)S(1)} %get-tuple-element.101.refs_1_, ...), custom_call_target="tpu_custom_call" | custom-call | flops 3000000000 | bytes 3000000 | tf_op jit(solution)/shard_map/inner_start/pallas_call | solution.py:624
  13.0 0.9 %collective-permute-done.4.refs_2_ = f32[192,128]{1,0:T(8,128)S(1)} collective-permute-done((f32[192,128]{1,0:T(8,128)S(1)}, f32[192,128]{1,0:T(8,128)S(1)}, u32[]{:S(2)}, u32[]{:S(2)}) %collective-permute-start.4) | collective-permute-done | bytes 98336 | tf_op jit(solution)/shard_map/ppermute | solution.py:593
  14.2 4.0 %cross_kernel.1 = (f32[768,128]{1,0:T(8,128)S(1)}, f32[144,128]{1,0:T(8,128)S(1)}, f32[144,128]{1,0:T(8,128)S(1)}, f32[96,128]{1,0:T(8,128)S(1)}, f32[32,512]{1,0:T(8,128)S(1)}) custom-call(f32[1024,128]{1,0:T(8,128)S(1)} %get-tuple-element.91.refs_3_.refs_0_, bf16[512,1024]{1,0:T(8,128)(2,1)S(1)} %get-tuple-element.96.refs_1_, ...), custom_call_target="tpu_custom_call" | custom-call | flops 4000000000 | bytes 4000000 | tf_op jit(solution)/shard_map/cross_kernel/pallas_call | solution.py:624
  18.2 2.0 %collective-permute-start.6 = (f32[8,8,128]{2,1,0:T(8,128)S(1)}, f32[8,8,128]{2,1,0:T(8,128)S(1)}, u32[]{:S(2)}, u32[]{:S(2)}) collective-permute-start(f32[8,8,128]{2,1,0:T(8,128)S(1)} %get-tuple-element.100.refs_4_), channel_id=1, source_target_pairs={{0,4},{1,5},{2,6},{3,7},{4,0},{5,1},{6,2},{7,3},{8,12},{9,13},{10,... | collective-permute-start | bytes 98312 | tf_op jit(solution)/shard_map/ppermute | solution.py:600
  20.2 2.0 %collective-permute-start.8 = (f32[144,128]{1,0:T(8,128)S(1)}, f32[144,128]{1,0:T(8,128)S(1)}, u32[]{:S(2)}, u32[]{:S(2)}) collective-permute-start(f32[144,128]{1,0:T(8,128)S(1)} %get-tuple-element.110), channel_id=1, source_target_pairs={{0,16},{1,2},{2,1},{3,4},{4,3},{5,6},{6,5},{7,8},{8,7},{9,10},{10,... | collective-permute-start | bytes 221192 | tf_op jit(solution)/shard_map/ppermute | solution.py:593
  22.2 1.5 %inner_rest.2 = (f32[768,128]{1,0:T(8,128)S(1)}, f32[768,128]{1,0:T(8,128)S(1)}) custom-call(f32[1024,128]{1,0:T(8,128)S(1)} %get-tuple-element.102.refs_0_, f32[1024,128]{1,0:T(8,128)S(1)} %get-tuple-element.103.refs_1_, f32[768,128]{1,0:T(8,128)S(1)} %get-tuple-element.104.refs_2_, f32[768,128]{1,0:T(8,128)S(1)} %get-tuple-element.105.refs_3_, ...), custom_call_target="tpu_custom_call" | custom-call | flops 2000000000 | bytes 2000000 | tf_op jit(solution)/shard_map/inner_rest/pallas_call | solution.py:624
  23.7 3.7 %collective-permute-start.7 = (f32[8,8,128]{2,1,0:T(8,128)S(1)}, f32[8,8,128]{2,1,0:T(8,128)S(1)}, u32[]{:S(2)}, u32[]{:S(2)}) collective-permute-start(f32[8,8,128]{2,1,0:T(8,128)S(1)} %get-tuple-element.108.refs_7_), channel_id=1, source_target_pairs={{0,8},{1,9},{2,10},{3,11},{4,12},{5,13},{6,14},{7,15},{8,0},{9,1},... | collective-permute-start | bytes 98312 | tf_op jit(solution)/shard_map/ppermute | solution.py:600
  27.4 1.2 %scatter_kernel.2.refs_3_.refs_4_ = f32[96,512]{1,0:T(8,128)S(1)} custom-call(f32[768,128]{1,0:T(8,128)S(1)} %get-tuple-element.112.refs_0_, f32[768,128]{1,0:T(8,128)S(1)} %get-tuple-element.106.refs_2_.refs_1_, f32[768,128]{1,0:T(8,128)S(1)} %get-tuple-element.113.refs_2_, bf16[512,1024]{1,0:T(8,128)(2,1)S(1)} %get-tuple-element.114.refs_3_.refs_2_, ...), custom_call_target="tpu_custom_call" | custom-call | flops 2000000000 | bytes 2000000 | tf_op jit(solution)/shard_map/scatter_kernel/pallas_call | solution.py:624
  28.7 2.1 %collective-permute-start.10 = (f32[144,128]{1,0:T(8,128)S(1)}, f32[144,128]{1,0:T(8,128)S(1)}, u32[]{:S(2)}, u32[]{:S(2)}) collective-permute-start(f32[144,128]{1,0:T(8,128)S(1)} %get-tuple-element.117.refs_4_), channel_id=1, source_target_pairs={{0,1},{1,0},{2,3},{3,2},{4,5},{5,4},{6,7},{7,6},{8,9},{9,8},{10,11... | collective-permute-start | bytes 221192 | tf_op jit(solution)/shard_map/ppermute | solution.py:593
  30.8 1.3 %fluid_kernel.1 = (f32[128,512]{1,0:T(8,128)S(1)}, f32[16,8,128]{2,1,0:T(8,128)S(1)}) custom-call(f32[64,128]{1,0:T(8,128)S(1)} %get-tuple-element.84.refs_0_, f32[8,8,128]{2,1,0:T(8,128)S(1)} %get-tuple-element.107.refs_1_, f32[8,8,128]{2,1,0:T(8,128)S(1)} %collective-permute-done.7.refs_2_, s32[32,512]{1,0:T(8,128)S(1)} %get-tuple-element.109.refs_3_, ...), custom_call_target="tpu_custom_call" | custom-call | flops 3000000000 | bytes 3000000 | tf_op jit(solution)/shard_map/fluid_kernel/pallas_call | solution.py:624
  32.2 1.0 %collective-permute-done.10.refs_6_ = f32[144,128]{1,0:T(8,128)S(1)} collective-permute-done((f32[144,128]{1,0:T(8,128)S(1)}, f32[144,128]{1,0:T(8,128)S(1)}, u32[]{:S(2)}, u32[]{:S(2)}) %collective-permute-start.10) | collective-permute-done | bytes 73760 | tf_op jit(solution)/shard_map/ppermute | solution.py:593
  33.2 0.7 %middle_kernel.1 = (f32[128,512]{1,0:T(8,128)S(1)}, f32[128,512]{1,0:T(8,128)S(1)}, f32[96,512]{1,0:T(8,128)S(1)}, f32[144,128]{1,0:T(8,128)S(1)}, f32[144,128]{1,0:T(8,128)S(1)}, /*index=5*/f32[96,128]{1,0:T(8,128)S(1)}) custom-call(f32[128,512]{1,0:T(8,128)S(1)} %get-tuple-element.77.refs_0_, f32[128,512]{1,0:T(8,128)S(1)} %get-tuple-element.78.refs_1_, ...), custom_call_target="tpu_custom_call" | custom-call | flops 1000000000 | bytes 1000000 | tf_op jit(solution)/shard_map/middle_kernel/pallas_call | solution.py:624
  33.8 2.1 %collective-permute-start.12 = (f32[144,128]{1,0:T(8,128)S(1)}, f32[144,128]{1,0:T(8,128)S(1)}, u32[]{:S(2)}, u32[]{:S(2)}) collective-permute-start(f32[144,128]{1,0:T(8,128)S(1)} %get-tuple-element.129), channel_id=1, source_target_pairs={{0,1},{1,0},{2,3},{3,2},{4,5},{5,4},{6,7},{7,6},{8,9},{9,8},{10,11... | collective-permute-start | bytes 221192 | tf_op jit(solution)/shard_map/ppermute | solution.py:593
  35.9 2.2 %inner_again.1 = (f32[1024,128]{1,0:T(8,128)S(1)}, f32[1024,128]{1,0:T(8,128)S(1)}, f32[768,128]{1,0:T(8,128)S(1)}, f32[768,128]{1,0:T(8,128)S(1)}) custom-call(f32[128,512]{1,0:T(8,128)S(1)} %get-tuple-element.122.refs_0_, s32[5,1024]{1,0:T(8,128)S(1)} %get-tuple-element.101.refs_1_, bf16[512,1024]{1,0:T(8,128)(2,1)S(1)} %get-tuple-element.114.refs_3_.refs_2_, ...), custom_call_target="tpu_custom_call" | custom-call | flops 3000000000 | bytes 3000000 | tf_op jit(solution)/shard_map/inner_again/pallas_call | solution.py:624
  38.4 1.6 %collective-permute-start.14 = (f32[144,128]{1,0:T(8,128)S(1)}, f32[144,128]{1,0:T(8,128)S(1)}, u32[]{:S(2)}, u32[]{:S(2)}) collective-permute-start(f32[144,128]{1,0:T(8,128)S(1)} %get-tuple-element.132.refs_3_), channel_id=1, source_target_pairs={{0,16},{1,2},{2,1},{3,4},{4,3},{5,6},{6,5},{7,8},{8,7},{9,10},{10,... | collective-permute-start | bytes 221192 | tf_op jit(solution)/shard_map/ppermute | solution.py:593
  39.9 0.6 %collective-permute-start.15 = (f32[144,128]{1,0:T(8,128)S(1)}, f32[144,128]{1,0:T(8,128)S(1)}, u32[]{:S(2)}, u32[]{:S(2)}) collective-permute-start(f32[144,128]{1,0:T(8,128)S(1)} %get-tuple-element.133.refs_4_), channel_id=1, source_target_pairs={{0,1},{1,0},{2,3},{3,2},{4,5},{5,4},{6,7},{7,6},{8,9},{9,8},{10,11... | collective-permute-start | bytes 221192 | tf_op jit(solution)/shard_map/ppermute | solution.py:593
  41.0 1.5 %inner_rest.3 = (f32[768,128]{1,0:T(8,128)S(1)}, f32[768,128]{1,0:T(8,128)S(1)}) custom-call(f32[1024,128]{1,0:T(8,128)S(1)} %get-tuple-element.125.refs_0_, f32[1024,128]{1,0:T(8,128)S(1)} %get-tuple-element.126.refs_1_, f32[768,128]{1,0:T(8,128)S(1)} %get-tuple-element.127.refs_2_, f32[768,128]{1,0:T(8,128)S(1)} %get-tuple-element.128.refs_3_, ...), custom_call_target="tpu_custom_call" | custom-call | flops 2000000000 | bytes 2000000 | tf_op jit(solution)/shard_map/inner_rest/pallas_call | solution.py:624
  42.5 2.6 %collective-permute-done.14.refs_2_ = f32[144,128]{1,0:T(8,128)S(1)} collective-permute-done((f32[144,128]{1,0:T(8,128)S(1)}, f32[144,128]{1,0:T(8,128)S(1)}, u32[]{:S(2)}, u32[]{:S(2)}) %collective-permute-start.14) | collective-permute-done | bytes 73760 | tf_op jit(solution)/shard_map/ppermute | solution.py:593
  45.1 4.0 %cross_kernel_again.1 = (f32[768,128]{1,0:T(8,128)S(1)}, f32[144,128]{1,0:T(8,128)S(1)}, f32[144,128]{1,0:T(8,128)S(1)}, f32[96,128]{1,0:T(8,128)S(1)}) custom-call(f32[1024,128]{1,0:T(8,128)S(1)} %cross_again.1.refs_4_.refs_0_, bf16[512,1024]{1,0:T(8,128)(2,1)S(1)} %get-tuple-element.96.refs_1_, f32[144,128]{1,0:T(8,128)S(1)} %collective-permute-done.14.refs_2_, ...), custom_call_target="tpu_custom_call" | custom-call | flops 4000000000 | bytes 4000000 | tf_op jit(solution)/shard_map/cross_kernel_again/pallas_call | solution.py:624
  49.2 1.9 %collective-permute-start.16 = (f32[144,128]{1,0:T(8,128)S(1)}, f32[144,128]{1,0:T(8,128)S(1)}, u32[]{:S(2)}, u32[]{:S(2)}) collective-permute-start(f32[144,128]{1,0:T(8,128)S(1)} %get-tuple-element.140), channel_id=1, source_target_pairs={{0,16},{1,2},{2,1},{3,4},{4,3},{5,6},{6,5},{7,8},{8,7},{9,10},{10,... | collective-permute-start | bytes 221192 | tf_op jit(solution)/shard_map/ppermute | solution.py:593
  51.1 1.2 %scatter_kernel.3.refs_3_.refs_4_ = f32[96,512]{1,0:T(8,128)S(1)} custom-call(f32[768,128]{1,0:T(8,128)S(1)} %get-tuple-element.134.refs_0_, f32[768,128]{1,0:T(8,128)S(1)} %get-tuple-element.135.refs_6_.refs_1_, f32[768,128]{1,0:T(8,128)S(1)} %get-tuple-element.138.refs_2_, bf16[512,1024]{1,0:T(8,128)(2,1)S(1)} %get-tuple-element.114.refs_3_.refs_2_, ...), custom_call_target="tpu_custom_call" | custom-call | flops 2000000000 | bytes 2000000 | tf_op jit(solution)/shard_map/scatter_kernel/pallas_call | solution.py:624
  52.3 3.4 %collective-permute-done.16.refs_0_ = f32[144,128]{1,0:T(8,128)S(1)} collective-permute-done((f32[144,128]{1,0:T(8,128)S(1)}, f32[144,128]{1,0:T(8,128)S(1)}, u32[]{:S(2)}, u32[]{:S(2)}) %collective-permute-start.16) | collective-permute-done | bytes 73760 | tf_op jit(solution)/shard_map/ppermute | solution.py:593
  56.1 0.7 %owned_kernel.1 = (f32[3,2048]{1,0:T(4,128)}, f32[16,128]{1,0:T(8,128)}) custom-call(f32[16,8,128]{2,1,0:T(8,128)S(1)} %get-tuple-element.147.refs_0_, f32[3,2048]{1,0:T(4,128)S(1)} %get-tuple-element.81.refs_4_.refs_1_, f32[3,2048]{1,0:T(4,128)S(1)} %get-tuple-element.82.refs_5_.refs_2_, f32[144,128]{1,0:T(8,128)S(1)} %get-tuple-element.143.refs_3_, ...), custom_call_target="tpu_custom_call" | custom-call | flops 1000000000 | bytes 1000000 | tf_op jit(solution)/shard_map/owned_kernel/pallas_call | solution.py:624
  56.8 3.4 %collective-permute-done.18.refs_6_ = f32[144,128]{1,0:T(8,128)S(1)} collective-permute-done((f32[144,128]{1,0:T(8,128)S(1)}, f32[144,128]{1,0:T(8,128)S(1)}, u32[]{:S(2)}, u32[]{:S(2)}) %collective-permute-start.18) | collective-permute-done | bytes 73760 | tf_op jit(solution)/shard_map/ppermute | solution.py:593
  60.2 1.4 %last_kernel.1 = (f32[3,16384]{1,0:T(4,128)}, f32[3,16384]{1,0:T(4,128)}) custom-call(f32[128,512]{1,0:T(8,128)S(1)} %get-tuple-element.122.refs_0_, f32[128,512]{1,0:T(8,128)S(1)} %get-tuple-element.123.refs_1_, f32[96,512]{1,0:T(8,128)S(1)} %get-tuple-element.124.refs_2_, f32[128,512]{1,0:T(8,128)S(1)} %get-tuple-element.119.refs_3_, ...), custom_call_target="tpu_custom_call" | custom-call | flops 1000000000 | bytes 1000000 | tf_op jit(solution)/shard_map/last_kernel/pallas_call | solution.py:624
  (31 shorter events, 2.4 us)
Async XLA Ops:
  2.3 4.7 %collective-permute-start.1 = (f32[192,128]{1,0:T(8,128)S(1)}, f32[192,128]{1,0:T(8,128)S(1)}, u32[]{:S(2)}, u32[]{:S(2)}) collective-permute-start(f32[192,128]{1,0:T(8,128)S(1)} %get-tuple-element.87), channel_id=1, source_target_pairs={{0,1},{1,0},{2,3},{3,2},{4,5},{5,4},{6,7},{7,6},{8,9},{9,8},{10,11... | collective-permute-start | bytes 294920 | tf_op jit(solution)/shard_map/ppermute | solution.py:593
  3.1 3.9 %collective-permute-start.2 = (f32[192,128]{1,0:T(8,128)S(1)}, f32[192,128]{1,0:T(8,128)S(1)}, u32[]{:S(2)}, u32[]{:S(2)}) collective-permute-start(f32[192,128]{1,0:T(8,128)S(1)} %get-tuple-element.88), channel_id=1, source_target_pairs={{0,16},{1,17},{2,18},{3,19},{4,20},{5,21},{6,22},{7,23},{8,24},{9,... | collective-permute-start | bytes 294920 | tf_op jit(solution)/shard_map/ppermute | solution.py:593
  5.5 4.1 %collective-permute-start = (f32[8,8,128]{2,1,0:T(8,128)S(1)}, f32[8,8,128]{2,1,0:T(8,128)S(1)}, u32[]{:S(2)}, u32[]{:S(2)}) collective-permute-start(f32[8,8,128]{2,1,0:T(8,128)S(1)} %get-tuple-element.86.refs_2_), channel_id=1, source_target_pairs={{0,1},{1,0},{2,3},{3,2},{4,5},{5,4},{6,7},{7,6},{8,9},{9,8},{10,11... | collective-permute-start | bytes 98312 | tf_op jit(solution)/shard_map/ppermute | solution.py:600
  7.1 6.8 %collective-permute-start.4 = (f32[192,128]{1,0:T(8,128)S(1)}, f32[192,128]{1,0:T(8,128)S(1)}, u32[]{:S(2)}, u32[]{:S(2)}) collective-permute-start(f32[192,128]{1,0:T(8,128)S(1)} %get-tuple-element.92.refs_2_), channel_id=1, source_target_pairs={{0,16},{1,2},{2,1},{3,4},{4,3},{5,6},{6,5},{7,8},{8,7},{9,10},{10,... | collective-permute-start | bytes 294920 | tf_op jit(solution)/shard_map/ppermute | solution.py:593
  9.6 4.6 %collective-permute-start.5 = (f32[192,128]{1,0:T(8,128)S(1)}, f32[192,128]{1,0:T(8,128)S(1)}, u32[]{:S(2)}, u32[]{:S(2)}) collective-permute-start(f32[192,128]{1,0:T(8,128)S(1)} %get-tuple-element.93.refs_3_), channel_id=1, source_target_pairs={{0,1},{1,0},{2,3},{3,2},{4,5},{5,4},{6,7},{7,6},{8,9},{9,8},{10,11... | collective-permute-start | bytes 294920 | tf_op jit(solution)/shard_map/ppermute | solution.py:593
  9.6 8.6 %collective-permute-start.3 = (f32[8,8,128]{2,1,0:T(8,128)S(1)}, f32[8,8,128]{2,1,0:T(8,128)S(1)}, u32[]{:S(2)}, u32[]{:S(2)}) collective-permute-start(f32[8,8,128]{2,1,0:T(8,128)S(1)} %get-tuple-element.95.refs_2_), channel_id=1, source_target_pairs={{0,2},{1,3},{2,0},{3,1},{4,6},{5,7},{6,4},{7,5},{8,10},{9,11},{10,... | collective-permute-start | bytes 98312 | tf_op jit(solution)/shard_map/ppermute | solution.py:600
  18.2 5.5 %collective-permute-start.6 = (f32[8,8,128]{2,1,0:T(8,128)S(1)}, f32[8,8,128]{2,1,0:T(8,128)S(1)}, u32[]{:S(2)}, u32[]{:S(2)}) collective-permute-start(f32[8,8,128]{2,1,0:T(8,128)S(1)} %get-tuple-element.100.refs_4_), channel_id=1, source_target_pairs={{0,4},{1,5},{2,6},{3,7},{4,0},{5,1},{6,2},{7,3},{8,12},{9,13},{10,... | collective-permute-start | bytes 98312 | tf_op jit(solution)/shard_map/ppermute | solution.py:600
  20.2 8.4 %collective-permute-start.8 = (f32[144,128]{1,0:T(8,128)S(1)}, f32[144,128]{1,0:T(8,128)S(1)}, u32[]{:S(2)}, u32[]{:S(2)}) collective-permute-start(f32[144,128]{1,0:T(8,128)S(1)} %get-tuple-element.110), channel_id=1, source_target_pairs={{0,16},{1,2},{2,1},{3,4},{4,3},{5,6},{6,5},{7,8},{8,7},{9,10},{10,... | collective-permute-start | bytes 221192 | tf_op jit(solution)/shard_map/ppermute | solution.py:593
  22.2 6.4 %collective-permute-start.9 = (f32[144,128]{1,0:T(8,128)S(1)}, f32[144,128]{1,0:T(8,128)S(1)}, u32[]{:S(2)}, u32[]{:S(2)}) collective-permute-start(f32[144,128]{1,0:T(8,128)S(1)} %get-tuple-element.111), channel_id=1, source_target_pairs={{0,1},{1,0},{2,3},{3,2},{4,5},{5,4},{6,7},{7,6},{8,9},{9,8},{10,11... | collective-permute-start | bytes 221192 | tf_op jit(solution)/shard_map/ppermute | solution.py:593
  23.7 7.1 %collective-permute-start.7 = (f32[8,8,128]{2,1,0:T(8,128)S(1)}, f32[8,8,128]{2,1,0:T(8,128)S(1)}, u32[]{:S(2)}, u32[]{:S(2)}) collective-permute-start(f32[8,8,128]{2,1,0:T(8,128)S(1)} %get-tuple-element.108.refs_7_), channel_id=1, source_target_pairs={{0,8},{1,9},{2,10},{3,11},{4,12},{5,13},{6,14},{7,15},{8,0},{9,1},... | collective-permute-start | bytes 98312 | tf_op jit(solution)/shard_map/ppermute | solution.py:600
  28.7 4.4 %collective-permute-start.10 = (f32[144,128]{1,0:T(8,128)S(1)}, f32[144,128]{1,0:T(8,128)S(1)}, u32[]{:S(2)}, u32[]{:S(2)}) collective-permute-start(f32[144,128]{1,0:T(8,128)S(1)} %get-tuple-element.117.refs_4_), channel_id=1, source_target_pairs={{0,1},{1,0},{2,3},{3,2},{4,5},{5,4},{6,7},{7,6},{8,9},{9,8},{10,11... | collective-permute-start | bytes 221192 | tf_op jit(solution)/shard_map/ppermute | solution.py:593
  30.8 2.3 %collective-permute-start.11 = (f32[144,128]{1,0:T(8,128)S(1)}, f32[144,128]{1,0:T(8,128)S(1)}, u32[]{:S(2)}, u32[]{:S(2)}) collective-permute-start(f32[144,128]{1,0:T(8,128)S(1)} %get-tuple-element.118.refs_5_), channel_id=1, source_target_pairs={{0,16},{1,17},{2,18},{3,19},{4,20},{5,21},{6,22},{7,23},{8,24},{9,... | collective-permute-start | bytes 221192 | tf_op jit(solution)/shard_map/ppermute | solution.py:593
  33.8 4.4 %collective-permute-start.12 = (f32[144,128]{1,0:T(8,128)S(1)}, f32[144,128]{1,0:T(8,128)S(1)}, u32[]{:S(2)}, u32[]{:S(2)}) collective-permute-start(f32[144,128]{1,0:T(8,128)S(1)} %get-tuple-element.129), channel_id=1, source_target_pairs={{0,1},{1,0},{2,3},{3,2},{4,5},{5,4},{6,7},{7,6},{8,9},{9,8},{10,11... | collective-permute-start | bytes 221192 | tf_op jit(solution)/shard_map/ppermute | solution.py:593
  35.9 2.3 %collective-permute-start.13 = (f32[144,128]{1,0:T(8,128)S(1)}, f32[144,128]{1,0:T(8,128)S(1)}, u32[]{:S(2)}, u32[]{:S(2)}) collective-permute-start(f32[144,128]{1,0:T(8,128)S(1)} %get-tuple-element.130), channel_id=1, source_target_pairs={{0,16},{1,17},{2,18},{3,19},{4,20},{5,21},{6,22},{7,23},{8,24},{9,... | collective-permute-start | bytes 221192 | tf_op jit(solution)/shard_map/ppermute | solution.py:593
  38.4 6.7 %collective-permute-start.14 = (f32[144,128]{1,0:T(8,128)S(1)}, f32[144,128]{1,0:T(8,128)S(1)}, u32[]{:S(2)}, u32[]{:S(2)}) collective-permute-start(f32[144,128]{1,0:T(8,128)S(1)} %get-tuple-element.132.refs_3_), channel_id=1, source_target_pairs={{0,16},{1,2},{2,1},{3,4},{4,3},{5,6},{6,5},{7,8},{8,7},{9,10},{10,... | collective-permute-start | bytes 221192 | tf_op jit(solution)/shard_map/ppermute | solution.py:593
  39.9 5.2 %collective-permute-start.15 = (f32[144,128]{1,0:T(8,128)S(1)}, f32[144,128]{1,0:T(8,128)S(1)}, u32[]{:S(2)}, u32[]{:S(2)}) collective-permute-start(f32[144,128]{1,0:T(8,128)S(1)} %get-tuple-element.133.refs_4_), channel_id=1, source_target_pairs={{0,1},{1,0},{2,3},{3,2},{4,5},{5,4},{6,7},{7,6},{8,9},{9,8},{10,11... | collective-permute-start | bytes 221192 | tf_op jit(solution)/shard_map/ppermute | solution.py:593
  49.2 6.5 %collective-permute-start.16 = (f32[144,128]{1,0:T(8,128)S(1)}, f32[144,128]{1,0:T(8,128)S(1)}, u32[]{:S(2)}, u32[]{:S(2)}) collective-permute-start(f32[144,128]{1,0:T(8,128)S(1)} %get-tuple-element.140), channel_id=1, source_target_pairs={{0,16},{1,2},{2,1},{3,4},{4,3},{5,6},{6,5},{7,8},{8,7},{9,10},{10,... | collective-permute-start | bytes 221192 | tf_op jit(solution)/shard_map/ppermute | solution.py:593
  51.1 4.6 %collective-permute-start.17 = (f32[144,128]{1,0:T(8,128)S(1)}, f32[144,128]{1,0:T(8,128)S(1)}, u32[]{:S(2)}, u32[]{:S(2)}) collective-permute-start(f32[144,128]{1,0:T(8,128)S(1)} %get-tuple-element.141), channel_id=1, source_target_pairs={{0,1},{1,0},{2,3},{3,2},{4,5},{5,4},{6,7},{7,6},{8,9},{9,8},{10,11... | collective-permute-start | bytes 221192 | tf_op jit(solution)/shard_map/ppermute | solution.py:593
  55.8 4.4 %collective-permute-start.18 = (f32[144,128]{1,0:T(8,128)S(1)}, f32[144,128]{1,0:T(8,128)S(1)}, u32[]{:S(2)}, u32[]{:S(2)}) collective-permute-start(f32[144,128]{1,0:T(8,128)S(1)} %get-tuple-element.143.refs_3_), channel_id=1, source_target_pairs={{0,1},{1,0},{2,3},{3,2},{4,5},{5,4},{6,7},{7,6},{8,9},{9,8},{10,11... | collective-permute-start | bytes 221192 | tf_op jit(solution)/shard_map/ppermute | solution.py:593
  55.9 4.3 %collective-permute-start.19 = (f32[144,128]{1,0:T(8,128)S(1)}, f32[144,128]{1,0:T(8,128)S(1)}, u32[]{:S(2)}, u32[]{:S(2)}) collective-permute-start(f32[144,128]{1,0:T(8,128)S(1)} %get-tuple-element.144.refs_4_), channel_id=1, source_target_pairs={{0,16},{1,17},{2,18},{3,19},{4,20},{5,21},{6,22},{7,23},{8,24},{9,... | collective-permute-start | bytes 221192 | tf_op jit(solution)/shard_map/ppermute | solution.py:593
